TPU v7x, 32 devices: a whole 2x2x4 slice. The times are simulated.
32 devices in a mesh: slab: 2 (over x), row: 16 (over z, y, core).
Axes of the slice: x: 2, y: 2, z: 4, core: 2. Of those that a mesh axis runs over, the one named last changes fastest.
Arguments:
- slab: bfloat16 [32, 128, 128, 128], P(('slab', 'row')), parts along dimension 0, may hold values from -12 to 12
- row_factor: bfloat16 [32, 8], P('slab'), parts along dimension 0, may hold values from -1.5 to 1.5
- col_factor: bfloat16 [256, 8], P('slab'), parts along dimension 0, may hold values from -0.5 to 0.5
- det_row_factor: bfloat16 [256, 64], P('slab'), parts along dimension 0, may hold values from -0.5 to 0.5
- det_col_factor: bfloat16 [256, 64], P('slab'), parts along dimension 0, may hold values from -0.5 to 0.5
Outputs:
- scan_row_gram: float32 [32, 16], P('slab'), parts along dimension 0
- scan_col_gram: float32 [256, 128], P('slab'), parts along dimension 0
- det_row_gram: float32 [256, 128], P('slab'), parts along dimension 0
- det_col_gram: float32 [256, 128], P('slab'), parts along dimension 0
There are 2 independent parts, one for each index of `slab`. A program takes and returns all parts, laid end to end along the dimension named above; each array names one. Nothing has to cross between parts.
All inputs are finite; a program needn't handle non-finite values.
Results may differ from a plain program's by a relative error of at most 0.0016.
Values may be sent and summed in bfloat16 or wider, within the bound.
No kernel may reach another device: no remote copies, remote signals or barrier semaphores. Data moves between devices by JAX's collectives and lax.ppermute only.
A program may use at most 64 MiB of HBM per device.

v0:
```python
import jax
import jax.numpy as jnp
from jax import lax
from jax.sharding import PartitionSpec as P

DET_RANK = 64
SCAN_RANK = 8


def local(slab, row_factor, col_factor, det_row_factor, det_col_factor):
    rows_here = slab.shape[0]
    scan_scale = 1.0 / (SCAN_RANK * DET_RANK * DET_RANK)
    det_scale = 1.0 / (SCAN_RANK * SCAN_RANK * DET_RANK)
    half_right = jnp.einsum(
        "rckl,lb->rcbk", slab, det_col_factor, preferred_element_type=jnp.float32
    ).astype(jnp.bfloat16)
    half_left = jnp.einsum(
        "rckl,ka->rcal", slab, det_row_factor, preferred_element_type=jnp.float32
    ).astype(jnp.bfloat16)
    row_weights = row_factor.astype(jnp.float32)
    cubes = jnp.einsum(
        "rcbk,ka->rcab", half_right, det_row_factor, preferred_element_type=jnp.float32
    ).astype(jnp.bfloat16)
    cubes = lax.all_to_all(cubes, "row", split_axis=2, concat_axis=0, tiled=True)
    first_row = lax.axis_index("row") * rows_here
    own_weights = lax.dynamic_slice_in_dim(row_weights, first_row, rows_here, 0)
    right_cols = jnp.einsum(
        "rcbk,cj->rjbk", half_right, col_factor, preferred_element_type=jnp.float32
    )
    left_cols = jnp.einsum(
        "rcal,cj->rjal", half_left, col_factor, preferred_element_type=jnp.float32
    )
    right_part = jnp.einsum(
        "rjbk,ri->bijk", right_cols, own_weights, precision=lax.Precision.HIGHEST
    )
    left_part = jnp.einsum("rjal,ri->aijl", left_cols, own_weights, precision=lax.Precision.HIGHEST)
    right_total, left_total = (
        lax.psum_scatter(right_part, "row", scatter_dimension=0, tiled=True),
        lax.psum_scatter(left_part, "row", scatter_dimension=0, tiled=True),
    )
    det_right = right_total.astype(jnp.bfloat16)
    det_left = left_total.astype(jnp.bfloat16)
    flattened = cubes.reshape(cubes.shape[0], cubes.shape[1], -1)
    row_unfold = jnp.einsum(
        "rcf,cj->rjf", flattened, col_factor, preferred_element_type=jnp.float32
    ).astype(jnp.bfloat16)
    col_unfold = jnp.einsum(
        "rcf,ri->icf", flattened, row_factor, preferred_element_type=jnp.float32
    ).astype(jnp.bfloat16)
    row_gram = (
        jnp.einsum("rjf,sjf->rs", row_unfold, row_unfold, preferred_element_type=jnp.float32)
        * scan_scale
    )
    col_gram = (
        jnp.einsum("icf,idf->cd", col_unfold, col_unfold, preferred_element_type=jnp.float32)
        * scan_scale
    )
    right_gram = (
        jnp.einsum("bijk,bijm->km", det_right, det_right, preferred_element_type=jnp.float32)
        * det_scale
    )
    left_gram = (
        jnp.einsum("aijl,aijm->lm", det_left, det_left, preferred_element_type=jnp.float32)
        * det_scale
    )
    return lax.psum((row_gram, col_gram, right_gram, left_gram), "row")


def solution(mesh):
    in_specs = (
        P(("slab", "row"), None, None, None),
        P("slab", None),
        P("slab", None),
        P("slab", None),
        P("slab", None),
    )
    out_specs = (P("slab", None), P("slab", None), P("slab", None), P("slab", None))
    return jax.shard_map(local, mesh=mesh, in_specs=in_specs, out_specs=out_specs, check_vma=False)
```

profile of v0, /device:TPU:0, one launch (start us, length us, event | category | flops | bytes accessed | tf_op | source)
XLA Modules:
  0.0 251.9 jit_solution(8951093092647103212)
XLA Ops:
  7.2 3.9 %convert_bitcast_fusion.1 = bf16[128,64,128]{2,1,0:T(8,128)(2,1)S(1)} fusion(bf16[1,128,128,128]{3,2,1,0:T(8,128)(2,1)} %param.5, bf16[128,64]{0,1:T(8,128)(2,1)} %param.9), kind=kOutput, calls=%fused_computation.9 | convolution fusion | flops 269484032 | bytes 6307840 | tf_op jit(solution)/shard_map/rckl,lb->rcbk/dot_general | solution.py:14
  11.2 0.7 convert_bitcast_fusion
  11.9 1.2 fusion.21
  13.1 1.2 fusion.24
  14.4 0.2 convert_reduce_fusion
  14.5 2.7 %multiply_bitcast_fusion = (f32[64,8,8,128]{3,2,1,0:T(8,128)}, f32[64,8,8,128]{3,2,1,0:T(8,128)}) fusion(f32[8,64,128]{2,0,1:T(8,128)S(1)} %fusion.24, f32[8]{0:T(128)S(1)} %convert_reduce_fusion, f32[8,64,128]{2,0,1:T(8,128)S(1)} %fusion.21), kind=kLoop, calls=%fused_computation.6 | loop fusion | flops 1048576 | bytes 4718624 | tf_op jit(solution)/shard_map/rjal,ri->aijl/transpose | solution.py:36
  17.3 0.7 reduce-scatter.3.cloned.1.call-update
  18.0 1.5 fusion.17
  19.5 0.7 copy.13
  20.2 32.9 %all_to_all.15 = bf16[1,128,64,64]{1,3,0,2:T(8,128)(2,1)S(1)} all-to-all(bf16[1,128,64,64]{1,3,0,2:T(8,128)(2,1)S(1)} %copy.13), channel_id=1, replica_groups=mesh['slab'=2,'row'=16] {'row'}, dimensions={2} | all-to-all | bytes 2097152 | tf_op jit(solution)/shard_map/all_to_all | solution.py:24
  53.2 0.9 copy.17
  54.1 0.3 fusion.20
  54.3 1.0 fusion.30
  55.3 0.4 fusion.27
  55.7 26.7 %reduce-scatter.5.cloned.1.call-done = f32[4,8,8,128]{3,2,1,0:T(8,128)} async-done(((f32[64,8,8,128]{3,2,1,0:T(8,128)}), f32[4,8,8,128]{3,2,1,0:T(8,128)}) %reduce-scatter.5.cloned.1.call-update) | async-done | bytes 131088 | tf_op jit(solution)/shard_map/reduce_scatter | solution.py:39
  82.3 1.8 fusion.28
  84.2 63.0 %reduce-scatter.3.cloned.1.call-done = f32[4,8,8,128]{3,2,1,0:T(8,128)} async-done(((f32[64,8,8,128]{3,2,1,0:T(8,128)}), f32[4,8,8,128]{3,2,1,0:T(8,128)}) %reduce-scatter.3.cloned.1.call-update) | async-done | bytes 131088 | tf_op jit(solution)/shard_map/reduce_scatter | solution.py:38
  147.2 1.8 fusion.29
  149.0 0.1 fusion.31
  149.2 30.6 %psum.28 = f32[16,16]{1,0:T(8,128)} all-reduce(f32[16,16]{1,0:T(8,128)S(1)} %fusion.31), channel_id=1, replica_groups=mesh['slab'=2,'row'=16] {'row'}, use_global_device_ids=true, to_apply=%region_0.0 | all-reduce | flops 256 | bytes 2048 | tf_op jit(solution)/shard_map/psum | solution.py:66
  179.8 61.1 %all-reduce.3.cloned.1.call-done = (f32[128,128]{1,0:T(8,128)}, f32[128,128]{1,0:T(8,128)}, f32[128,128]{1,0:T(8,128)}) async-done(((f32[128,128]{1,0:T(8,128)}, f32[128,128]{1,0:T(8,128)}, f32[128,128]{1,0:T(8,128)}), (f32[128,128]{1,0:T(8,128)}, f32[128,128]{1,0:T(8,128)}, f32[128,128]{1,0:T(8,128)})) %all-reduce.3.cloned.1.call-update) | async-done | bytes 196624 | tf_op jit(solution)/shard_map/psum | solution.py:66
  240.9 1.5 copy.46
  242.4 1.5 copy.47
  243.9 1.5 copy.48
  (13 shorter events, 0.2 us)
Async XLA Ops:
  7.2 4.0 %copy-start = (bf16[128,64]{0,1:T(8,128)(2,1)S(1)}, bf16[128,64]{0,1:T(8,128)(2,1)}, u32[]{:S(2)}) copy-start(bf16[128,64]{0,1:T(8,128)(2,1)} %param.8) | copy-start | bytes 49156
  7.2 75.2 %reduce-scatter.5.cloned.1.call-start = ((), (), s32[]{:S(2)}) async-start(), calls=%async_computation.4 | async-start | bytes 2228224 | tf_op jit(solution)/shard_map/reduce_scatter | solution.py:39
  7.2 3.9 %copy-start.1 = (bf16[1,128,128,128]{3,2,1,0:T(8,128)(2,1)S(1)}, bf16[1,128,128,128]{3,2,1,0:T(8,128)(2,1)}, u32[]{:S(2)}) copy-start(bf16[1,128,128,128]{3,2,1,0:T(8,128)(2,1)} %param.5) | copy-start | bytes 12582916
  11.2 0.7 copy-start.3
  11.9 2.4 copy-start.2
  17.2 130.0 %reduce-scatter.3.cloned.1.call-start = ((), (), s32[]{:S(2)}) async-start(), calls=%async_computation.3 | async-start | bytes 2228224 | tf_op jit(solution)/shard_map/reduce_scatter | solution.py:38
  18.0 222.9 %all-reduce.3.cloned.1.call-start = ((), (), s32[]{:S(2)}) async-start(), calls=%async_computation.5 | async-start | bytes 393216 | tf_op jit(solution)/shard_map/psum | solution.py:66
Sparse Core Ops, SparseCore 0:
  17.3 64.9 reduce-scatter.4
  86.5 60.6 reduce-scatter.2
  151.5 89.3 all-reduce.2
where the time goes:
time: 252 us
  waiting for transfers between devices  152 us (60%)
  blocking collectives  63.6 us (25%)
  matrix products  13.9 us (6%)
  between operations  13.8 us (5%)
  local copies, waits for them, and re-layouts  6.02 us (2%)
  other arithmetic  2.85 us (1%)
    reduce_scatter x1, waiting for transfers between devices, local(): lax.psum_scatter(right_part, 'row', scatter_dimension=0, tiled=True)  63 us
    psum x1, waiting for transfers between devices, local(): return lax.psum((row_gram, col_gram, right_gram, left_gram), 'row')  61.1 us
    all_to_all x1, blocking collectives, local(): lax.all_to_all(cubes, 'row', split_axis=2, concat_axis=0, tiled=True)  32.9 us
    psum x1, blocking collectives, local(): return lax.psum((row_gram, col_gram, right_gram, left_gram), 'row')  30.6 us
    reduce_scatter x1, waiting for transfers between devices, local(): lax.psum_scatter(left_part, 'row', scatter_dimension=0, tiled=True)  26.7 us
  transfers between devices with their start and end apart: 3, of which 3 were waited for; matrix products, arithmetic and copies ran while one was open for 3% of the time, Pallas kernels for 0%

commit v1 on v0

v1 whole, which is shorter than its diff:
```python
import functools

import jax
import jax.numpy as jnp
from jax import lax
from jax.experimental import pallas as pl
from jax.experimental.pallas import tpu as pltpu
from jax.sharding import PartitionSpec as P

DET_RANK = 64
SCAN_RANK = 8
SCAN_SCALE = 1.0 / (SCAN_RANK * DET_RANK * DET_RANK)
DET_SCALE = 1.0 / (SCAN_RANK * SCAN_RANK * DET_RANK)
LANES = 128
BF16 = jnp.bfloat16
F32 = jnp.float32
LAST = (((1,), (1,)), ((), ()))
FIRST = (((0,), (0,)), ((), ()))


def dot(x, y, dims=None):
    if dims is None:
        return jnp.dot(x, y, preferred_element_type=F32)
    return lax.dot_general(x, y, dims, preferred_element_type=F32)


def project(n, cuts, slab, cft_in, dt_in, vt_in, out, cft, dt, vt, images, right, left, arrived, ready):
    cols, pixels = slab.shape[0], slab.shape[1]
    pitch = cols + 1
    rank = dt.shape[0]
    own = rank // n
    cuts = [0, *cuts, cols]
    copies = [
        pltpu.make_async_copy(slab.at[pl.ds(a, b - a)], images.at[pl.ds(a, b - a)], arrived.at[i])
        for i, (a, b) in enumerate(zip(cuts, cuts[1:]))
    ]
    factors = [
        pltpu.make_async_copy(x, y, ready.at[i]) for i, (x, y) in enumerate([(dt_in, dt), (vt_in, vt), (cft_in, cft)])
    ]
    for copy in factors + copies:
        copy.start()
    for copy in factors:
        copy.wait()
    none = jnp.zeros((rank, pixels), BF16)
    dt2 = jnp.concatenate([jnp.concatenate([dt[...], none], 1), jnp.concatenate([none, dt[...]], 1)], 0)
    vt2 = jnp.concatenate([jnp.concatenate([vt[...], none], 1), jnp.concatenate([none, vt[...]], 1)], 0)
    tall = dt[...].T
    none = jnp.zeros_like(tall)
    dd = jnp.concatenate([jnp.concatenate([tall, none], 1), jnp.concatenate([none, tall], 1)], 0)
    for at, copy in enumerate(copies):
        copy.wait()
        for c in range(cuts[at], cuts[at + 1], 4):
            four = jnp.concatenate(
                [
                    jnp.concatenate([images[c], images[c + 1]], axis=1),
                    jnp.concatenate([images[c + 2], images[c + 3]], axis=1),
                ],
                axis=0,
            )
            rights = dot(vt2, four, LAST)
            lefts = dot(dt2, four)
            for i in range(2):
                for j in range(2):
                    at_c = pl.ds(c + 2 * i + j, rank, stride=pitch)
                    right[at_c, :] = rights[j * rank : (j + 1) * rank, i * pixels : (i + 1) * pixels]
                    left[at_c, :] = lefts[i * rank : (i + 1) * rank, j * pixels : (j + 1) * pixels]
    n_cube = own // 2 * cols
    n_part = own * SCAN_RANK
    pair = 2 * SCAN_RANK
    for p in range(n):
        for h in range(own // 2):
            b = p * own + 2 * h
            two_right = [right[pl.ds((b + k) * pitch, cols), :].astype(BF16) for k in range(2)]
            two_left = [left[pl.ds((b + k) * pitch, cols), :].astype(BF16) for k in range(2)]
            x = jnp.concatenate(two_right, axis=1)
            y = jnp.concatenate(two_left, axis=1)
            out[p, pl.ds(h * cols, cols), :] = dot(x, dd).astype(BF16)
            sums = dot(cft[...], x)
            out[p, pl.ds(n_cube + h * pair, pair), :] = jnp.concatenate(
                [sums[:, :pixels], sums[:, pixels:]], axis=0
            ).astype(BF16)
            sums = dot(cft[...], y)
            out[p, pl.ds(n_cube + n_part + h * pair, pair), :] = jnp.concatenate(
                [sums[:, :pixels], sums[:, pixels:]], axis=0
            ).astype(BF16)


def projections(n, cuts, slab, cft, dt, vt):
    cols, pixels = slab.shape[0], slab.shape[1]
    rank = dt.shape[0]
    own = rank // n
    rows = own // 2 * cols + 2 * own * SCAN_RANK
    in_vmem = pl.BlockSpec(memory_space=pltpu.VMEM)
    return pl.pallas_call(
        functools.partial(project, n, cuts),
        out_shape=jax.ShapeDtypeStruct((n, rows, pixels), BF16),
        in_specs=[pl.BlockSpec(memory_space=pl.ANY)] * 4,
        out_specs=in_vmem,
        scratch_shapes=[
            pltpu.VMEM(cft.shape, BF16),
            pltpu.VMEM(dt.shape, BF16),
            pltpu.VMEM(vt.shape, BF16),
            pltpu.VMEM(slab.shape, BF16),
            pltpu.VMEM((rank * (cols + 1), pixels), F32),
            pltpu.VMEM((rank * (cols + 1), pixels), F32),
            pltpu.SemaphoreType.DMA((len(cuts) + 1,)),
            pltpu.SemaphoreType.DMA((3,)),
        ],
        compiler_params=pltpu.CompilerParams(vmem_limit_bytes=56 << 20),
    )(slab, cft, dt, vt)


def one_hot(shape, rows_per, cols_per):
    r = lax.broadcasted_iota(jnp.int32, shape, 0)
    c = lax.broadcasted_iota(jnp.int32, shape, 1)
    return r // rows_per == c // cols_per


def grams_of(own, got, rft, cft, keep, send, spread, unfold, rowbuf, total):
    rows, cols = got.shape[0], cft.shape[1]
    pixels = got.shape[2]
    pairs = own // 2
    n_cube = pairs * cols
    n_part = own * SCAN_RANK
    group = 16
    tall = one_hot((SCAN_RANK * group, SCAN_RANK), group, 1).astype(BF16)
    wide = one_hot((rows, rows * group), 1, group).astype(BF16)
    weights = dot(tall, rft[...]).astype(BF16)
    weights = dot(weights, wide)
    r = lax.broadcasted_iota(jnp.int32, weights.shape, 0)
    c = lax.broadcasted_iota(jnp.int32, weights.shape, 1)
    spread[...] = jnp.where(r % group == c % group, weights, 0.0).astype(BF16)

    def gather(start):
        return jnp.concatenate([got[s, pl.ds(start, group), :] for s in range(rows)], axis=0)

    for g in range(cols // group):
        x = jnp.concatenate([gather(h * cols + g * group) for h in range(pairs)], axis=1)
        u = dot(spread[...], x).astype(BF16)
        for i in range(SCAN_RANK):
            unfold[i, pl.ds(g * group, group), :] = u[i * group : (i + 1) * group]
    gram = jnp.zeros((cols, cols), F32)
    for i in range(SCAN_RANK):
        gram += dot(unfold[i], unfold[i], LAST)
    total[pl.ds(0, cols), :] = gram * SCAN_SCALE
    for s in range(rows):
        x = jnp.concatenate([got[s, pl.ds(h * cols, cols), :] for h in range(pairs)], axis=1)
        y = dot(cft[...], x)
        for h in range(pairs):
            rowbuf[h, pl.ds(s, SCAN_RANK, stride=rows), :] = y[:, h * LANES : (h + 1) * LANES]
    gram = jnp.zeros((rows, rows), F32)
    for i in range(SCAN_RANK):
        for h in range(pairs):
            x = rowbuf[h, pl.ds(i * rows, rows), :].astype(BF16)
            gram += dot(x, x, LAST)
    total[pl.ds(cols, rows), :] = jnp.zeros((rows, total.shape[1]), F32)
    total[pl.ds(cols, rows), pl.ds(0, rows)] = gram * SCAN_SCALE
    for side in range(2):
        gram = jnp.zeros((pixels, pixels), F32)
        for g in range(n_part // group):
            x = gather(n_cube + side * n_part + g * group)
            u = dot(spread[...], x).astype(BF16)
            gram += dot(u, u, FIRST)
        total[pl.ds(cols + rows + side * pixels, pixels), :] = gram * DET_SCALE
    half = keep.shape[0]
    core = lax.axis_index("row") % 2
    keep[...] = total[pl.ds(pl.multiple_of(core * half, 8), half), :]
    send[...] = total[pl.ds(pl.multiple_of((1 - core) * half, 8), half), :]


def partial_grams(own, got, rft, cft):
    rows, cols, pixels = rft.shape[1], cft.shape[1], got.shape[2]
    height = cols + rows + 2 * pixels
    half = jax.ShapeDtypeStruct((height // 2, pixels), F32)
    return pl.pallas_call(
        functools.partial(grams_of, own),
        out_shape=(half, half),
        scratch_shapes=[
            pltpu.VMEM((SCAN_RANK * 16, rows * 16), BF16),
            pltpu.VMEM((SCAN_RANK, cols, own * DET_RANK), BF16),
            pltpu.VMEM((own // 2, SCAN_RANK * rows, LANES), F32),
            pltpu.VMEM((height, pixels), F32),
        ],
        compiler_params=pltpu.CompilerParams(vmem_limit_bytes=40 << 20),
    )(got, rft, cft)


def swap(x, n, step):
    return lax.ppermute(x, "row", [(i, i ^ step) for i in range(n)])


def local(n, slab, row_factor, col_factor, det_row_factor, det_col_factor):
    slab = slab.reshape(slab.shape[-3:])
    cols, pixels = slab.shape[0], slab.shape[1]
    rows = row_factor.shape[0]
    own = DET_RANK // n
    packed = projections(n, (cols // 2, cols * 13 // 16), slab, col_factor.T, det_row_factor.T, det_col_factor.T)
    got = lax.all_to_all(packed, "row", split_axis=0, concat_axis=0, tiled=True)
    mine, other = partial_grams(own, got, row_factor.T, col_factor.T)
    mine = mine + swap(other, n, 1)
    step = 2
    while step < n:
        mine = mine + swap(mine, n, step)
        step *= 2
    other = swap(mine, n, 1)
    first = lax.axis_index("row") % 2 == 0
    grams = jnp.concatenate([jnp.where(first, mine, other), jnp.where(first, other, mine)])
    cut = cols + rows
    return (
        grams[cols:cut, :rows],
        grams[:cols],
        grams[cut : cut + pixels],
        grams[cut + pixels :],
    )


def all_sum(x, n):
    step = 1
    while step < n:
        x = x + swap(x, n, step)
        step *= 2
    return x


def plain(n, slab, row_factor, col_factor, det_row_factor, det_col_factor):
    slab = slab.reshape(slab.shape[-3:])
    rows, own = row_factor.shape[0], DET_RANK // n
    half_right = jnp.einsum("ckl,lb->cbk", slab, det_col_factor, preferred_element_type=F32).astype(BF16)
    half_left = jnp.einsum("ckl,ka->cal", slab, det_row_factor, preferred_element_type=F32).astype(BF16)
    cubes = jnp.einsum("cbk,ka->bca", half_right, det_row_factor, preferred_element_type=F32).astype(BF16)
    right_cols = jnp.einsum("cbk,cj->bjk", half_right, col_factor, preferred_element_type=F32).astype(BF16)
    left_cols = jnp.einsum("cal,cj->ajl", half_left, col_factor, preferred_element_type=F32).astype(BF16)
    cubes, right_cols, left_cols = (
        lax.all_to_all(x.reshape((n, own) + x.shape[1:]), "row", split_axis=0, concat_axis=0, tiled=True)
        for x in (cubes, right_cols, left_cols)
    )
    row_unfold = jnp.einsum("rbca,cj->rjba", cubes, col_factor, preferred_element_type=F32).astype(BF16)
    col_unfold = jnp.einsum("rbca,ri->ibca", cubes, row_factor, preferred_element_type=F32).astype(BF16)
    det_right = jnp.einsum("rbjk,ri->ibjk", right_cols, row_factor, preferred_element_type=F32).astype(BF16)
    det_left = jnp.einsum("rajl,ri->iajl", left_cols, row_factor, preferred_element_type=F32).astype(BF16)
    row_gram = jnp.einsum("rjba,sjba->rs", row_unfold, row_unfold, preferred_element_type=F32)
    col_gram = jnp.einsum("ibca,ibda->cd", col_unfold, col_unfold, preferred_element_type=F32)
    right_gram = jnp.einsum("ibjk,ibjm->km", det_right, det_right, preferred_element_type=F32)
    left_gram = jnp.einsum("iajl,iajm->lm", det_left, det_left, preferred_element_type=F32)
    scaled = (row_gram * SCAN_SCALE, col_gram * SCAN_SCALE, right_gram * DET_SCALE, left_gram * DET_SCALE)
    return lax.psum(scaled, "row")


def solution(mesh):
    in_specs = (
        P(("slab", "row"), None, None, None),
        P("slab", None),
        P("slab", None),
        P("slab", None),
        P("slab", None),
    )
    out_specs = (P("slab", None), P("slab", None), P("slab", None), P("slab", None))
    n = mesh.shape["row"]
    paired = DET_RANK % (2 * n) == 0 and n & (n - 1) == 0
    run = functools.partial(local if paired else plain, n)
    return jax.shard_map(run, mesh=mesh, in_specs=in_specs, out_specs=out_specs, check_vma=False)
```

time: 252 us -> 68.8 us (0.27)
  waiting for transfers between devices: 152 us -> 15.5 us
  blocking collectives: 63.6 us -> 38.9 us
  matrix products: 13.9 us -> 0 us
  between operations: 13.8 us -> 0.69 us
  Pallas kernels: 0 us -> 7.77 us
  local copies, waits for them, and re-layouts: 6.02 us -> 0.61 us
  starting transfers between devices: 0.12 us -> 4.33 us
    reduce_scatter x2 -> x0, waiting for transfers between devices: 89.7 us -> none  [the longest x1 63 us: local(): lax.psum_scatter(right_part, 'row', scatter_dimension=0, tiled=True)]
    psum x1 -> x0, waiting for transfers between devices: 61.1 us -> none  [local(): return lax.psum((row_gram, col_gram, right_gram, left_gram), 'row')]
    psum x1 -> x0, blocking collectives: 30.6 us -> none  [local(): return lax.psum((row_gram, col_gram, right_gram, left_gram), 'row')]
    ppermute x0 -> x5, waiting for transfers between devices: none -> 15.5 us  [swap(): return lax.ppermute(x, 'row', [(i, i ^ step) for i in range(n)])]
    dot_general x11 -> x0, matrix products: 13.9 us -> none  [the longest x1 3.92 us: local(): jnp.einsum('rckl,lb->rcbk', slab, det_col_factor, preferred_element_type=...]
    pallas_call x0 -> x2, Pallas kernels: none -> 7.77 us  [the longest x1 6.37 us: projections(): pl.pallas_call(functools.partial(project, n, cuts), out_shape=jax.ShapeDt...]
    all_to_all x1, blocking collectives: 32.9 us -> 38.9 us  [local(): got = lax.all_to_all(packed, 'row', split_axis=0, concat_axis=0, tiled=True)]
    unnamed x11 -> x4, local copies, waits for them, and re-layouts: 4.44 us -> 0.01 us
  transfers between devices with their start and end apart: 3 -> 5, of which waited for: 3 -> 5; matrix products, arithmetic and copies ran while one was open for 3% -> 0% of each run, Pallas kernels for 0% -> 0%
where the time goes in v1:
time: 68.8 us; the launch traced here: 68.5 us
  blocking collectives  38.9 us (57%)
  waiting for transfers between devices  15.5 us (23%)
  Pallas kernels  7.77 us (11%)
  starting transfers between devices  4.33 us (6%)
  other arithmetic  0.75 us (1%)
  between operations  0.69 us (1%)
    all_to_all x1, blocking collectives, local(): got = lax.all_to_all(packed, 'row', split_axis=0, concat_axis=0, tiled=True)  38.9 us
    ppermute x5, waiting for transfers between devices, swap(): return lax.ppermute(x, 'row', [(i, i ^ step) for i in range(n)])  15.5 us
    pallas_call x1, Pallas kernels, projections(): pl.pallas_call(functools.partial(project, n, cuts), out_shape=jax.ShapeDt...  6.37 us
    ppermute x5, starting transfers between devices, swap(): return lax.ppermute(x, 'row', [(i, i ^ step) for i in range(n)])  4.33 us
    pallas_call x1, Pallas kernels, partial_grams(): pl.pallas_call(functools.partial(grams_of, own), out_shape=(half, half),...  1.4 us
  transfers between devices with their start and end apart: 5, of which 5 were waited for; matrix products, arithmetic and copies ran while one was open for 0% of the time, Pallas kernels for 0%

profile of v1, /device:TPU:0, one launch (start us, length us, event | category | flops | bytes accessed | tf_op | source)
XLA Modules:
  0.0 68.5 jit_solution(16056799776469459743)
XLA Ops:
  0.6 6.4 %shard_map.84 = bf16[16,320,128]{2,1,0:T(8,128)(2,1)} custom-call(bf16[128,128,128]{2,1,0:T(8,128)(2,1)} %bitcast.8, bf16[8,128]{1,0:T(8,128)(2,1)} %bitcast.5, bf16[64,128]{1,0:T(8,128)(2,1)} %bitcast.9, bf16[64,128]{1,0:T(8,128)(2,1)} %bitcast.10), custom_call_target="tpu_custom_call" | custom-call | tf_op jit(solution)/shard_map/pallas_call | solution.py:94
  7.0 0.0 copy-start
  7.0 0.0 copy-start.1
  7.0 38.9 %all_to_all.5.got = bf16[16,320,128]{2,1,0:T(8,128)(2,1)S(1)} all-to-all(bf16[16,320,128]{2,1,0:T(8,128)(2,1)} %shard_map.84), channel_id=1, replica_groups=mesh['slab'=2,'row'=16] {'row'}, dimensions={0} | all-to-all | bytes 2621440 | tf_op jit(solution)/shard_map/all_to_all | solution.py:198
  46.0 0.0 copy-done
  46.0 0.0 copy-done.1
  46.0 1.4 %shard_map.85 = (f32[200,128]{1,0:T(8,128)S(1)}, f32[200,128]{1,0:T(8,128)S(1)}) custom-call(bf16[16,320,128]{2,1,0:T(8,128)(2,1)S(1)} %all_to_all.5.got, bf16[8,16]{1,0:T(8,128)(2,1)S(1)} %bitcast.7, bf16[8,128]{1,0:T(8,128)(2,1)S(1)} %bitcast.6), custom_call_target="tpu_custom_call" | custom-call | tf_op jit(solution)/shard_map/pallas_call | solution.py:175
  47.4 0.8 %collective-permute-start = (f32[200,128]{1,0:T(8,128)S(1)}, f32[200,128]{1,0:T(8,128)S(1)}, u32[]{:S(2)}, u32[]{:S(2)}) collective-permute-start(f32[200,128]{1,0:T(8,128)S(1)} %get-tuple-element.7), channel_id=1, source_target_pairs={{0,1},{1,0},{2,3},{3,2},{4,5},{5,4},{6,7},{7,6},{8,9},{9,8},{10,11... | collective-permute-start | bytes 307208 | tf_op jit(solution)/shard_map/ppermute | solution.py:189
  48.2 0.9 %collective-permute-done = f32[200,128]{1,0:T(8,128)S(1)} collective-permute-done((f32[200,128]{1,0:T(8,128)S(1)}, f32[200,128]{1,0:T(8,128)S(1)}, u32[]{:S(2)}, u32[]{:S(2)}) %collective-permute-start) | collective-permute-done | bytes 102432 | tf_op jit(solution)/shard_map/ppermute | solution.py:189
  49.2 0.9 %collective-permute-start.1 = (f32[200,128]{1,0:T(8,128)S(1)}, f32[200,128]{1,0:T(8,128)S(1)}, u32[]{:S(2)}, u32[]{:S(2)}) collective-permute-start(f32[200,128]{1,0:T(8,128)S(1)} %add.17), channel_id=1, source_target_pairs={{0,2},{1,3},{2,0},{3,1},{4,6},{5,7},{6,4},{7,5},{8,10},{9,11},{10,... | collective-permute-start | bytes 307208 | tf_op jit(solution)/shard_map/ppermute | solution.py:189
  50.0 4.3 %collective-permute-done.1 = f32[200,128]{1,0:T(8,128)S(1)} collective-permute-done((f32[200,128]{1,0:T(8,128)S(1)}, f32[200,128]{1,0:T(8,128)S(1)}, u32[]{:S(2)}, u32[]{:S(2)}) %collective-permute-start.1) | collective-permute-done | bytes 102432 | tf_op jit(solution)/shard_map/ppermute | solution.py:189
  54.4 1.0 %collective-permute-start.2 = (f32[200,128]{1,0:T(8,128)S(1)}, f32[200,128]{1,0:T(8,128)S(1)}, u32[]{:S(2)}, u32[]{:S(2)}) collective-permute-start(f32[200,128]{1,0:T(8,128)S(1)} %add.18), channel_id=1, source_target_pairs={{0,4},{1,5},{2,6},{3,7},{4,0},{5,1},{6,2},{7,3},{8,12},{9,13},{10,... | collective-permute-start | bytes 307208 | tf_op jit(solution)/shard_map/ppermute | solution.py:189
  55.4 3.7 %collective-permute-done.2 = f32[200,128]{1,0:T(8,128)S(1)} collective-permute-done((f32[200,128]{1,0:T(8,128)S(1)}, f32[200,128]{1,0:T(8,128)S(1)}, u32[]{:S(2)}, u32[]{:S(2)}) %collective-permute-start.2) | collective-permute-done | bytes 102432 | tf_op jit(solution)/shard_map/ppermute | solution.py:189
  59.1 1.5 %collective-permute-start.3 = (f32[200,128]{1,0:T(8,128)S(1)}, f32[200,128]{1,0:T(8,128)S(1)}, u32[]{:S(2)}, u32[]{:S(2)}) collective-permute-start(f32[200,128]{1,0:T(8,128)S(1)} %add.19), channel_id=1, source_target_pairs={{0,8},{1,9},{2,10},{3,11},{4,12},{5,13},{6,14},{7,15},{8,0},{9,1},... | collective-permute-start | bytes 307208 | tf_op jit(solution)/shard_map/ppermute | solution.py:189
  60.6 5.2 %collective-permute-done.3 = f32[200,128]{1,0:T(8,128)S(1)} collective-permute-done((f32[200,128]{1,0:T(8,128)S(1)}, f32[200,128]{1,0:T(8,128)S(1)}, u32[]{:S(2)}, u32[]{:S(2)}) %collective-permute-start.3) | collective-permute-done | bytes 102432 | tf_op jit(solution)/shard_map/ppermute | solution.py:189
  65.9 0.1 collective-permute-start.4
  66.0 1.3 %collective-permute-done.4 = f32[200,128]{1,0:T(8,128)S(1)} collective-permute-done((f32[200,128]{1,0:T(8,128)S(1)}, f32[200,128]{1,0:T(8,128)S(1)}, u32[]{:S(2)}, u32[]{:S(2)}) %collective-permute-start.4) | collective-permute-done | bytes 102432 | tf_op jit(solution)/shard_map/ppermute | solution.py:189
  67.3 0.6 slice.16
  67.9 0.7 fusion
  (5 shorter events, 0.1 us)
Async XLA Ops:
  7.0 38.9 %copy-start = (bf16[128,8]{0,1:T(8,128)(2,1)S(1)}, bf16[128,8]{0,1:T(8,128)(2,1)}, u32[]{:S(2)}) copy-start(bf16[128,8]{0,1:T(8,128)(2,1)} %param.7) | copy-start | bytes 6148
  7.0 38.9 %copy-start.1 = (bf16[16,8]{0,1:T(8,128)(2,1)S(1)}, bf16[16,8]{0,1:T(8,128)(2,1)}, u32[]{:S(2)}) copy-start(bf16[16,8]{0,1:T(8,128)(2,1)} %param.6) | copy-start | bytes 772
  47.4 1.8 %collective-permute-start = (f32[200,128]{1,0:T(8,128)S(1)}, f32[200,128]{1,0:T(8,128)S(1)}, u32[]{:S(2)}, u32[]{:S(2)}) collective-permute-start(f32[200,128]{1,0:T(8,128)S(1)} %get-tuple-element.7), channel_id=1, source_target_pairs={{0,1},{1,0},{2,3},{3,2},{4,5},{5,4},{6,7},{7,6},{8,9},{9,8},{10,11... | collective-permute-start | bytes 307208 | tf_op jit(solution)/shard_map/ppermute | solution.py:189
  49.2 5.2 %collective-permute-start.1 = (f32[200,128]{1,0:T(8,128)S(1)}, f32[200,128]{1,0:T(8,128)S(1)}, u32[]{:S(2)}, u32[]{:S(2)}) collective-permute-start(f32[200,128]{1,0:T(8,128)S(1)} %add.17), channel_id=1, source_target_pairs={{0,2},{1,3},{2,0},{3,1},{4,6},{5,7},{6,4},{7,5},{8,10},{9,11},{10,... | collective-permute-start | bytes 307208 | tf_op jit(solution)/shard_map/ppermute | solution.py:189
  54.4 4.7 %collective-permute-start.2 = (f32[200,128]{1,0:T(8,128)S(1)}, f32[200,128]{1,0:T(8,128)S(1)}, u32[]{:S(2)}, u32[]{:S(2)}) collective-permute-start(f32[200,128]{1,0:T(8,128)S(1)} %add.18), channel_id=1, source_target_pairs={{0,4},{1,5},{2,6},{3,7},{4,0},{5,1},{6,2},{7,3},{8,12},{9,13},{10,... | collective-permute-start | bytes 307208 | tf_op jit(solution)/shard_map/ppermute | solution.py:189
  59.1 6.7 %collective-permute-start.3 = (f32[200,128]{1,0:T(8,128)S(1)}, f32[200,128]{1,0:T(8,128)S(1)}, u32[]{:S(2)}, u32[]{:S(2)}) collective-permute-start(f32[200,128]{1,0:T(8,128)S(1)} %add.19), channel_id=1, source_target_pairs={{0,8},{1,9},{2,10},{3,11},{4,12},{5,13},{6,14},{7,15},{8,0},{9,1},... | collective-permute-start | bytes 307208 | tf_op jit(solution)/shard_map/ppermute | solution.py:189
  65.9 1.4 %collective-permute-start.4 = (f32[200,128]{1,0:T(8,128)S(1)}, f32[200,128]{1,0:T(8,128)S(1)}, u32[]{:S(2)}, u32[]{:S(2)}) collective-permute-start(f32[200,128]{1,0:T(8,128)S(1)} %add.20), channel_id=1, source_target_pairs={{0,1},{1,0},{2,3},{3,2},{4,5},{5,4},{6,7},{7,6},{8,9},{9,8},{10,11... | collective-permute-start | bytes 307208 | tf_op jit(solution)/shard_map/ppermute | solution.py:189

commit v2 on v1

v2 whole, which is shorter than its diff:
```python
import functools

import jax
import jax.numpy as jnp
from jax import lax
from jax.experimental import pallas as pl
from jax.experimental.pallas import tpu as pltpu
from jax.sharding import PartitionSpec as P

DET_RANK = 64
SCAN_RANK = 8
SCAN_SCALE = 1.0 / (SCAN_RANK * DET_RANK * DET_RANK)
DET_SCALE = 1.0 / (SCAN_RANK * SCAN_RANK * DET_RANK)
LANES = 128
GROUP = 16
COST = pl.CostEstimate(flops=10**8, bytes_accessed=4 << 20, transcendentals=0)
BF16 = jnp.bfloat16
F32 = jnp.float32
LAST = (((1,), (1,)), ((), ()))
FIRST = (((0,), (0,)), ((), ()))


def dot(x, y, dims=None):
    if dims is None:
        return jnp.dot(x, y, preferred_element_type=F32)
    return lax.dot_general(x, y, dims, preferred_element_type=F32)


def paired(x):
    none = jnp.zeros_like(x)
    return jnp.concatenate([jnp.concatenate([x, none], 1), jnp.concatenate([none, x], 1)], 0)


def four_images(images, c):
    return jnp.concatenate(
        [
            jnp.concatenate([images[c], images[c + 1]], axis=1),
            jnp.concatenate([images[c + 2], images[c + 3]], axis=1),
        ],
        axis=0,
    )


def early_cubes(early, own, base, slab, dt_in, vt_in, *refs):
    *far, dd, dt, vt, images, right, arrived, ready = refs
    pixels = slab.shape[1]
    rank = own * far[0].shape[0] * len(far)
    pitch = early + 1
    cuts = [0, early // 2, early]
    copies = [
        pltpu.make_async_copy(slab.at[pl.ds(a, b - a)], images.at[pl.ds(a, b - a)], arrived.at[i])
        for i, (a, b) in enumerate(zip(cuts, cuts[1:]))
    ]
    factors = [pltpu.make_async_copy(x, y, ready.at[i]) for i, (x, y) in enumerate([(dt_in, dt), (vt_in, vt)])]
    for copy in factors + copies:
        copy.start()
    for copy in factors:
        copy.wait()
    vt2, dd[...] = paired(slot_order(vt[...], own, base, rank)), paired(dt[...].T)
    for at, copy in enumerate(copies):
        copy.wait()
        for c in range(cuts[at], cuts[at + 1], 4):
            rights = dot(vt2, four_images(images, c), LAST)
            for i in range(2):
                for j in range(2):
                    right[pl.ds(c + 2 * i + j, rank, stride=pitch), :] = rights[
                        j * rank : (j + 1) * rank, i * pixels : (i + 1) * pixels
                    ]
    owner_cubes(early, pitch, own, right, dd[...], far)


def slot_order(factor, own, base, count):
    shape = (count, factor.shape[0])
    r = lax.broadcasted_iota(jnp.int32, shape, 0) + base * own
    c = lax.broadcasted_iota(jnp.int32, shape, 1)
    take = (c // own == r // own ^ lax.axis_index("row")) & (c % own == r % own)
    return dot(take.astype(BF16), factor).astype(BF16)


def owner_cubes(early, pitch, own, right, dd, arrays):
    plane = arrays[0].shape[0]
    for slot in range(plane * len(arrays)):
        to = arrays[slot // plane].at[slot % plane]
        for h in range(own // 2):
            b = slot * own + 2 * h
            x = [right[pl.ds((b + k) * pitch, early), :] for k in range(2)]
            to[pl.ds(h * early, early), :] = dot(jnp.concatenate(x, axis=1).astype(BF16), dd).astype(BF16)


def late_cubes(early, own, images, cft, dt, vt, dd_in, *refs):
    *near, second, right, left, dd, ready = refs
    copy = pltpu.make_async_copy(dd_in, dd, ready)
    copy.start()
    cols, pixels, rank = images.shape[0], images.shape[1], dt.shape[0]
    pitch = cols + 1
    dt2, vt2 = (paired(slot_order(x[...], own, 0, rank)) for x in (dt, vt))
    for c in range(0, cols, 4):
        four = four_images(images, c)
        rights = dot(vt2, four, LAST)
        lefts = dot(dt2, four)
        for i in range(2):
            for j in range(2):
                at_c = pl.ds(c + 2 * i + j, rank, stride=pitch)
                right[at_c, :] = rights[j * rank : (j + 1) * rank, i * pixels : (i + 1) * pixels]
                left[at_c, :] = lefts[i * rank : (i + 1) * rank, j * pixels : (j + 1) * pixels]
    copy.wait()
    pairs, pair = own // 2, 2 * SCAN_RANK
    late = cols - early

    def two(ref, b):
        parts = [ref[pl.ds((b + k) * pitch, cols), :] for k in range(2)]
        return jnp.concatenate(parts, axis=1).astype(BF16)

    def stacked(sums):
        return jnp.concatenate([sums[:, :pixels], sums[:, pixels:]], axis=0).astype(BF16)

    me = lax.axis_index("row")
    for slot in range(rank // own):
        p = me ^ slot
        for h in range(pairs):
            x = two(right, slot * own + 2 * h)
            y = two(left, slot * own + 2 * h)
            at = pairs * late + h * pair
            second[p, pl.ds(h * late, late), :] = dot(x[early:], dd[...]).astype(BF16)
            second[p, pl.ds(at, pair), :] = stacked(dot(cft[...], x))
            second[p, pl.ds(at + pairs * pair, pair), :] = stacked(dot(cft[...], y))
    owner_cubes(early, pitch, own, right, dd[...], near)


def projections(n, plane, early, slab, cft, dt, vt):
    cols, pixels = slab.shape[0], slab.shape[1]
    rank = dt.shape[0]
    own = rank // n
    anywhere = pl.BlockSpec(memory_space=pl.ANY)
    in_vmem = pl.BlockSpec(memory_space=pltpu.VMEM)
    params = pltpu.CompilerParams(vmem_limit_bytes=56 << 20)
    half = n // plane // 2
    part = [jax.ShapeDtypeStruct((plane, own // 2 * early, pixels), BF16)] * half
    pair = jax.ShapeDtypeStruct((2 * pixels, 2 * rank), BF16)
    *far, dd = pl.pallas_call(
        functools.partial(early_cubes, early, own, n // 2),
        out_shape=part + [pair],
        in_specs=[anywhere] * 3,
        out_specs=[in_vmem] * (half + 1),
        scratch_shapes=[
            pltpu.VMEM(dt.shape, BF16),
            pltpu.VMEM(vt.shape, BF16),
            pltpu.VMEM((early,) + slab.shape[1:], BF16),
            pltpu.VMEM((rank // 2 * (early + 1), pixels), F32),
            pltpu.SemaphoreType.DMA((2,)),
            pltpu.SemaphoreType.DMA((2,)),
        ],
        compiler_params=params,
    )(slab, dt, vt)
    height = own // 2 * (cols - early) + 2 * own * SCAN_RANK
    *near, second = pl.pallas_call(
        functools.partial(late_cubes, early, own),
        out_shape=part + [jax.ShapeDtypeStruct((n, height, pixels), BF16)],
        in_specs=[in_vmem] * 4 + [anywhere],
        out_specs=[in_vmem] * (half + 1),
        scratch_shapes=[pltpu.VMEM((rank * (cols + 1), pixels), F32)] * 2
        + [pltpu.VMEM(dd.shape, BF16), pltpu.SemaphoreType.DMA],
        compiler_params=pltpu.CompilerParams(vmem_limit_bytes=32 << 20),
    )(slab, cft, dt, vt, dd)
    return near + far, second


def one_hot(shape, rows_per, cols_per):
    r = lax.broadcasted_iota(jnp.int32, shape, 0)
    c = lax.broadcasted_iota(jnp.int32, shape, 1)
    return r // rows_per == c // cols_per


def spread_weights(rft, rows, order=None):
    weights = rft[...]
    if order is not None:
        r = lax.broadcasted_iota(jnp.int32, (rows, rows), 0)
        c = lax.broadcasted_iota(jnp.int32, (rows, rows), 1)
        weights = dot(weights, (r == (c ^ order)).astype(BF16)).astype(BF16)
    tall = one_hot((SCAN_RANK * GROUP, SCAN_RANK), GROUP, 1).astype(BF16)
    wide = one_hot((rows, rows * GROUP), 1, GROUP).astype(BF16)
    weights = dot(dot(tall, weights).astype(BF16), wide)
    r = lax.broadcasted_iota(jnp.int32, weights.shape, 0)
    c = lax.broadcasted_iota(jnp.int32, weights.shape, 1)
    return jnp.where(r % GROUP == c % GROUP, weights, 0.0).astype(BF16)


def partial_grams(own, plane, early, rft, cft, second, *refs):
    *first, keep, send, unfold, rowbuf, total = refs
    rows, cols, pixels = rft.shape[1], cft.shape[1], second.shape[2]
    pairs, late = own // 2, cols - early
    me = lax.axis_index("row")
    mixed = spread_weights(rft, rows, me)
    plain = spread_weights(rft, rows)

    def old(s, at, size):
        return first[s % plane][s // plane, pl.ds(at, size), :]

    def new(s, at, size):
        return second[s, pl.ds(at, size), :]

    def wide(get, at, size, pitch):
        return jnp.concatenate([get(at + h * pitch, size) for h in range(pairs)], axis=1)

    def all_rows(get, at, size):
        return jnp.concatenate([get(s, at, size) for s in range(rows)], axis=0)

    for c in range(0, cols, GROUP):
        if c < early:
            u = dot(mixed, wide(functools.partial(all_rows, old), c, GROUP, early))
        else:
            u = dot(plain, wide(functools.partial(all_rows, new), c - early, GROUP, late))
        u = u.astype(BF16)
        for i in range(SCAN_RANK):
            unfold[i, pl.ds(c, GROUP), :] = u[i * GROUP : (i + 1) * GROUP]
    gram = jnp.zeros((cols, cols), F32)
    for i in range(SCAN_RANK):
        gram += dot(unfold[i], unfold[i], LAST)
    half = cols // 2
    pack(total, 0, gram * SCAN_SCALE)
    for s in range(rows):
        y = dot(cft[:, :early], wide(functools.partial(old, s), 0, early, early))
        z = dot(cft[:, early:], wide(functools.partial(new, s), 0, late, late))
        for h in range(pairs):
            lanes = slice(h * LANES, (h + 1) * LANES)
            rowbuf[0, h, pl.ds(me ^ s, SCAN_RANK, stride=rows), :] = y[:, lanes]
            rowbuf[1, h, pl.ds(s, SCAN_RANK, stride=rows), :] = z[:, lanes]
    gram = jnp.zeros((rows, rows), F32)
    for i in range(SCAN_RANK):
        for h in range(pairs):
            at = pl.ds(i * rows, rows)
            x = (rowbuf[0, h, at, :] + rowbuf[1, h, at, :]).astype(BF16)
            gram += dot(x, x, LAST)
    spare = jnp.concatenate([gram * SCAN_SCALE, jnp.zeros((rows, half - rows), F32)], axis=1)
    total[pl.ds(5 * half - rows, rows), pl.ds(half, half)] = spare
    n_part = own * SCAN_RANK
    for side in range(2):
        gram = jnp.zeros((pixels, pixels), F32)
        for g in range(n_part // GROUP):
            at = pairs * late + side * n_part + g * GROUP
            u = dot(plain, all_rows(new, at, GROUP)).astype(BF16)
            gram += dot(u, u, FIRST)
        pack(total, 1 + side, gram * DET_SCALE)
    size = keep.shape[0]
    core = me % 2
    keep[...] = total[pl.ds(pl.multiple_of(core * size, 8), size), :]
    send[...] = total[pl.ds(pl.multiple_of((1 - core) * size, 8), size), :]


def pack(total, k, gram):
    half = gram.shape[0] // 2
    total[pl.ds(k * half, half), :] = gram[:half]
    total[pl.ds((3 + k // 2) * half, half), pl.ds(k % 2 * half, half)] = gram[half:, half:]


def unpack(mine, other, row_out, col_out, right_out, left_out, row_gram, grams, sems):
    even = lax.axis_index("row") % 2 == 0
    total = jnp.concatenate(
        [jnp.where(even, mine[...], other[...]), jnp.where(even, other[...], mine[...])], axis=0
    )
    cols, rows = col_out.shape[0], row_out.shape[0]
    half = cols // 2
    copies = []
    for k, out in enumerate([col_out, right_out, left_out]):
        top = total[k * half : (k + 1) * half]
        corner = total[(3 + k // 2) * half : (4 + k // 2) * half, k % 2 * half : (k % 2 + 1) * half]
        grams[k, pl.ds(0, half), :] = top
        grams[k, pl.ds(half, half), :] = jnp.concatenate([top[:, half:].T, corner], axis=1)
        copies.append(pltpu.make_async_copy(grams.at[k], out, sems.at[k]))
        copies[-1].start()
    row_gram[...] = total[5 * half - rows : 5 * half, half : half + rows]
    copies.append(pltpu.make_async_copy(row_gram, row_out, sems.at[3]))
    copies[-1].start()
    for copy in copies:
        copy.wait()


def call(kernel, args, outs, scratch=(), flops=10**8):
    return pl.pallas_call(
        kernel,
        out_shape=[jax.ShapeDtypeStruct(shape, F32) for shape in outs],
        scratch_shapes=scratch,
        compiler_params=pltpu.CompilerParams(vmem_limit_bytes=40 << 20),
        cost_estimate=pl.CostEstimate(flops=flops, bytes_accessed=4 << 20, transcendentals=0),
    )(*args)


def swap(x, n, step):
    return lax.ppermute(x, "row", [(i, i ^ step) for i in range(n)])


def regroup(*refs):
    before, after = refs[: len(refs) // 2], refs[len(refs) // 2 :]
    for z, x in enumerate(before):
        for q, y in enumerate(after):
            y[z] = x[q]


def regrouped(first):
    planes, (plane, height, width) = len(first), first[0].shape
    return pl.pallas_call(
        regroup,
        out_shape=[jax.ShapeDtypeStruct((planes, height, width), BF16)] * plane,
        compiler_params=pltpu.CompilerParams(vmem_limit_bytes=40 << 20),
        cost_estimate=pl.CostEstimate(flops=4 * 10**10, bytes_accessed=4 << 20, transcendentals=0),
    )(*first)


def all_sum(mine, other, n):
    mine = mine + swap(other, n, 1)
    step = 2
    while step < n:
        mine = mine + swap(mine, n, step)
        step *= 2
    return mine, swap(mine, n, 1)


def local(n, plane, slab, row_factor, col_factor, det_row_factor, det_col_factor):
    slab = slab.reshape(slab.shape[-3:])
    cols, pixels = slab.shape[0], slab.shape[1]
    rows = row_factor.shape[0]
    own = DET_RANK // n
    rft, cft = row_factor.T, col_factor.T
    early = cols // 2
    first, second = projections(n, plane, early, slab, cft, det_row_factor.T, det_col_factor.T)
    first = [x if z == 0 else swap(x, n, z * plane) for z, x in enumerate(first)]
    second = lax.all_to_all(second, "row", split_axis=0, concat_axis=0, tiled=True)
    first = regrouped(first)
    first = [x if q == 0 else swap(x, n, q) for q, x in enumerate(first)]
    half = (5 * cols // 4, pixels)
    scratch = [
        pltpu.VMEM((SCAN_RANK, cols, own * DET_RANK), BF16),
        pltpu.VMEM((2, own // 2, SCAN_RANK * rows, LANES), F32),
        pltpu.VMEM((5 * cols // 2, pixels), F32),
    ]
    kernel = functools.partial(partial_grams, own, plane, early)
    mine, other = call(kernel, (rft, cft, second, *first), (half, half), scratch)
    mine, other = all_sum(mine, other, n)
    outs = [(rows, rows), (cols, cols), (pixels, pixels), (pixels, pixels)]
    in_vmem = pl.BlockSpec(memory_space=pltpu.VMEM)
    return pl.pallas_call(
        unpack,
        out_shape=[jax.ShapeDtypeStruct(shape, F32) for shape in outs],
        in_specs=[in_vmem] * 2,
        out_specs=[pl.BlockSpec(memory_space=pl.ANY)] * 4,
        scratch_shapes=[
            pltpu.VMEM((rows, rows), F32),
            pltpu.VMEM((3, cols, cols), F32),
            pltpu.SemaphoreType.DMA((4,)),
        ],
    )(mine, other)


def plain(n, slab, row_factor, col_factor, det_row_factor, det_col_factor):
    slab = slab.reshape(slab.shape[-3:])
    rows, own = row_factor.shape[0], DET_RANK // n
    half_right = jnp.einsum("ckl,lb->cbk", slab, det_col_factor, preferred_element_type=F32).astype(BF16)
    half_left = jnp.einsum("ckl,ka->cal", slab, det_row_factor, preferred_element_type=F32).astype(BF16)
    cubes = jnp.einsum("cbk,ka->bca", half_right, det_row_factor, preferred_element_type=F32).astype(BF16)
    right_cols = jnp.einsum("cbk,cj->bjk", half_right, col_factor, preferred_element_type=F32).astype(BF16)
    left_cols = jnp.einsum("cal,cj->ajl", half_left, col_factor, preferred_element_type=F32).astype(BF16)
    cubes, right_cols, left_cols = (
        lax.all_to_all(x.reshape((n, own) + x.shape[1:]), "row", split_axis=0, concat_axis=0, tiled=True)
        for x in (cubes, right_cols, left_cols)
    )
    row_unfold = jnp.einsum("rbca,cj->rjba", cubes, col_factor, preferred_element_type=F32).astype(BF16)
    col_unfold = jnp.einsum("rbca,ri->ibca", cubes, row_factor, preferred_element_type=F32).astype(BF16)
    det_right = jnp.einsum("rbjk,ri->ibjk", right_cols, row_factor, preferred_element_type=F32).astype(BF16)
    det_left = jnp.einsum("rajl,ri->iajl", left_cols, row_factor, preferred_element_type=F32).astype(BF16)
    row_gram = jnp.einsum("rjba,sjba->rs", row_unfold, row_unfold, preferred_element_type=F32)
    col_gram = jnp.einsum("ibca,ibda->cd", col_unfold, col_unfold, preferred_element_type=F32)
    right_gram = jnp.einsum("ibjk,ibjm->km", det_right, det_right, preferred_element_type=F32)
    left_gram = jnp.einsum("iajl,iajm->lm", det_left, det_left, preferred_element_type=F32)
    scaled = (row_gram * SCAN_SCALE, col_gram * SCAN_SCALE, right_gram * DET_SCALE, left_gram * DET_SCALE)
    return lax.psum(scaled, "row")


def solution(mesh):
    in_specs = (
        P(("slab", "row"), None, None, None),
        P("slab", None),
        P("slab", None),
        P("slab", None),
        P("slab", None),
    )
    out_specs = (P("slab", None), P("slab", None), P("slab", None), P("slab", None))
    n = mesh.shape["row"]
    plane = round(n**0.5)
    tuned = plane * plane == n and n & (n - 1) == 0 and DET_RANK % (2 * n) == 0
    run = functools.partial(local, n, plane) if tuned else functools.partial(plain, n)
    return jax.shard_map(run, mesh=mesh, in_specs=in_specs, out_specs=out_specs, check_vma=False)
```

time: 68.8 us -> 60.7 us (0.88)
  blocking collectives: 38.9 us -> 0 us
  starting transfers between devices: 4.33 us -> 20.6 us
  waiting for transfers between devices: 15.5 us -> 26.9 us
  Pallas kernels: 7.77 us -> 10.6 us
  local copies, waits for them, and re-layouts: 0.61 us -> 1.49 us
  other arithmetic: 0.75 us -> 0.04 us
    all_to_all x1 -> x0, blocking collectives: 38.9 us -> none  [local(): got = lax.all_to_all(packed, 'row', split_axis=0, concat_axis=0, tiled=True)]
    ppermute x5 -> x11, starting transfers between devices: 4.33 us -> 15.4 us  [swap(): return lax.ppermute(x, 'row', [(i, i ^ step) for i in range(n)])]
    ppermute x5 -> x11, waiting for transfers between devices: 15.5 us -> 22.8 us  [swap(): return lax.ppermute(x, 'row', [(i, i ^ step) for i in range(n)])]
    all_to_all x0 -> x1, starting transfers between devices: none -> 5.24 us  [local(): lax.all_to_all(second, 'row', split_axis=0, concat_axis=0, tiled=True)]
    all_to_all x0 -> x1, waiting for transfers between devices: none -> 4.12 us  [local(): lax.all_to_all(second, 'row', split_axis=0, concat_axis=0, tiled=True)]
    pallas_call x2 -> x5, Pallas kernels: 7.77 us -> 10.6 us  [the longest x1 3.89 us: projections(): pl.pallas_call(functools.partial(late_cubes, early, own), out_shape=part...]
    unnamed x4 -> x16, local copies, waits for them, and re-layouts: 0.01 us -> 1.49 us
  transfers between devices with their start and end apart: 5 -> 12, of which waited for: 5 -> 9; matrix products, arithmetic and copies ran while one was open for 0% -> 0% of each run, Pallas kernels for 0% -> 6%
where the time goes in v2:
time: 60.7 us; the launch traced here: 60.4 us
  waiting for transfers between devices  26.9 us (44%)
  starting transfers between devices  20.6 us (34%)
  Pallas kernels  10.6 us (17%)
  local copies, waits for them, and re-layouts  1.49 us (2%)
  between operations  0.78 us (1%)
    ppermute x11, waiting for transfers between devices, swap(): return lax.ppermute(x, 'row', [(i, i ^ step) for i in range(n)])  22.8 us
    ppermute x11, starting transfers between devices, swap(): return lax.ppermute(x, 'row', [(i, i ^ step) for i in range(n)])  15.4 us
    all_to_all x1, starting transfers between devices, local(): lax.all_to_all(second, 'row', split_axis=0, concat_axis=0, tiled=True)  5.24 us
    all_to_all x1, waiting for transfers between devices, local(): lax.all_to_all(second, 'row', split_axis=0, concat_axis=0, tiled=True)  4.12 us
    pallas_call x1, Pallas kernels, projections(): pl.pallas_call(functools.partial(late_cubes, early, own), out_shape=part...  3.89 us
    pallas_call x1, Pallas kernels, projections(): pl.pallas_call(functools.partial(early_cubes, early, own, n // 2), out_sh...  3.25 us
    pallas_call x1, Pallas kernels, local(): pl.pallas_call(unpack, out_shape=[jax.ShapeDtypeStruct(shape, F32) for sh...  1.81 us
    pallas_call x1, Pallas kernels, call(): pl.pallas_call(kernel, out_shape=[jax.ShapeDtypeStruct(shape, F32) for sh...  1.6 us
  transfers between devices with their start and end apart: 12, of which 9 were waited for; matrix products, arithmetic and copies ran while one was open for 0% of the time, Pallas kernels for 6%

profile of v2, /device:TPU:0, one launch (start us, length us, event | category | flops | bytes accessed | tf_op | source)
XLA Modules:
  0.0 60.4 jit_solution(13595326572427087843)
XLA Ops:
  0.7 3.2 %shard_map.84 = (bf16[4,128,128]{2,1,0:T(8,128)(2,1)}, bf16[4,128,128]{2,1,0:T(8,128)(2,1)}, bf16[256,128]{1,0:T(8,128)(2,1)}) custom-call(bf16[128,128,128]{2,1,0:T(8,128)(2,1)} %bitcast.5, bf16[64,128]{1,0:T(8,128)(2,1)} %bitcast.7, bf16[64,128]{1,0:T(8,128)(2,1)} %bitcast.9), custom_call_target="tpu_custom_call" | custom-call | tf_op jit(solution)/shard_map/pallas_call | solution.py:140
  3.9 4.1 %collective-permute-start.1 = (bf16[4,128,128]{2,1,0:T(8,128)(2,1)}, bf16[4,128,128]{2,1,0:T(8,128)(2,1)S(1)}, u32[]{:S(2)}, u32[]{:S(2)}) collective-permute-start(bf16[4,128,128]{2,1,0:T(8,128)(2,1)} %get-tuple-element.20), channel_id=1, source_target_pairs={{0,8},{1,9},{2,10},{3,11},{4,12},{5,13},{6,14},{7,15},{8,0},{9,1},... | collective-permute-start | bytes 393224 | tf_op jit(solution)/shard_map/ppermute | solution.py:289
  8.0 1.4 %collective-permute-start.2 = (bf16[4,128,128]{2,1,0:T(8,128)(2,1)}, bf16[4,128,128]{2,1,0:T(8,128)(2,1)S(1)}, u32[]{:S(2)}, u32[]{:S(2)}) collective-permute-start(bf16[4,128,128]{2,1,0:T(8,128)(2,1)} %get-tuple-element.21), channel_id=1, source_target_pairs={{0,12},{1,13},{2,14},{3,15},{4,8},{5,9},{6,10},{7,11},{8,4},{9,5},... | collective-permute-start | bytes 393224 | tf_op jit(solution)/shard_map/ppermute | solution.py:289
  9.4 0.8 %copy-done.1 = bf16[256,128]{1,0:T(8,128)(2,1)S(1)} copy-done((bf16[256,128]{1,0:T(8,128)(2,1)S(1)}, bf16[256,128]{1,0:T(8,128)(2,1)}, u32[]{:S(2)}) %copy-start.1) | copy-done | bytes 65560
  10.2 3.9 %shard_map.85 = (bf16[4,128,128]{2,1,0:T(8,128)(2,1)S(1)}, bf16[4,128,128]{2,1,0:T(8,128)(2,1)S(1)}, bf16[16,192,128]{2,1,0:T(8,128)(2,1)}) custom-call(bf16[128,128,128]{2,1,0:T(8,128)(2,1)S(1)} %bitcast.6, bf16[8,128]{1,0:T(8,128)(2,1)S(1)} %bitcast.11, bf16[64,128]{1,0:T(8,128)(2,1)S(1)} %bitcast.8, bf16[64,128]{1,0:T(8,128)(2,1)S(1)} %bitcast.10, ...), custom_call_target="tpu_custom_call" | custom-call | tf_op jit(solution)/shard_map/pallas_call | solution.py:156
  14.1 0.3 collective-permute-start
  14.4 5.2 %all-to-all-start = ((bf16[16,192,128]{2,1,0:T(8,128)(2,1)}), bf16[16,192,128]{2,1,0:T(8,128)(2,1)S(1)}, u32[]{:S(2)}, u32[]{:S(2)}) async-start(bf16[16,192,128]{2,1,0:T(8,128)(2,1)} %get-tuple-element.17), calls=%async_computation | async-start | bytes 1572864 | tf_op jit(solution)/shard_map/all_to_all | solution.py:327
  19.7 0.5 collective-permute-done.refs_1_
  20.3 1.6 %collective-permute-start.4 = (bf16[4,128,128]{2,1,0:T(8,128)(2,1)S(1)}, bf16[4,128,128]{2,1,0:T(8,128)(2,1)S(1)}, u32[]{:S(2)}, u32[]{:S(2)}) collective-permute-start(bf16[4,128,128]{2,1,0:T(8,128)(2,1)S(1)} %get-tuple-element.24), channel_id=1, source_target_pairs={{0,2},{1,3},{2,0},{3,1},{4,6},{5,7},{6,4},{7,5},{8,10},{9,11},{10,... | collective-permute-start | bytes 393224 | tf_op jit(solution)/shard_map/ppermute | solution.py:289
  22.2 10.1 %collective-permute-done.4.refs_2_ = bf16[4,128,128]{2,1,0:T(8,128)(2,1)S(1)} collective-permute-done((bf16[4,128,128]{2,1,0:T(8,128)(2,1)S(1)}, bf16[4,128,128]{2,1,0:T(8,128)(2,1)S(1)}, u32[]{:S(2)}, u32[]{:S(2)}) %collective-permute-start.4) | collective-permute-done | bytes 131104 | tf_op jit(solution)/shard_map/ppermute | solution.py:289
  32.3 2.0 %collective-permute-done.5.refs_3_ = bf16[4,128,128]{2,1,0:T(8,128)(2,1)S(1)} collective-permute-done((bf16[4,128,128]{2,1,0:T(8,128)(2,1)S(1)}, bf16[4,128,128]{2,1,0:T(8,128)(2,1)S(1)}, u32[]{:S(2)}, u32[]{:S(2)}) %collective-permute-start.5) | collective-permute-done | bytes 131104 | tf_op jit(solution)/shard_map/ppermute | solution.py:289
  34.3 4.1 %all-to-all-done.second = bf16[16,192,128]{2,1,0:T(8,128)(2,1)S(1)} async-done(((bf16[16,192,128]{2,1,0:T(8,128)(2,1)}), bf16[16,192,128]{2,1,0:T(8,128)(2,1)S(1)}, u32[]{:S(2)}, u32[]{:S(2)}) %all-to-all-start) | async-done | bytes 786464 | tf_op jit(solution)/shard_map/all_to_all | solution.py:327
  38.4 1.6 %shard_map.87 = (f32[160,128]{1,0:T(8,128)S(1)}, f32[160,128]{1,0:T(8,128)S(1)}) custom-call(bf16[8,16]{1,0:T(8,128)(2,1)S(1)} %bitcast.13, bf16[8,128]{1,0:T(8,128)(2,1)S(1)} %bitcast.12, bf16[16,192,128]{2,1,0:T(8,128)(2,1)S(1)} %all-to-all-done.second, bf16[4,128,128]{2,1,0:T(8,128)(2,1)S(1)} %get-tuple-element.22.refs_0_, ...), custom_call_target="tpu_custom_call" | custom-call | flops 100000000 | bytes 4194304 | tf_op jit(solution)/shard_map/pallas_call | solution.py:279
  40.0 0.3 collective-permute-start.6
  40.3 1.0 %collective-permute-done.6 = f32[160,128]{1,0:T(8,128)S(1)} collective-permute-done((f32[160,128]{1,0:T(8,128)S(1)}, f32[160,128]{1,0:T(8,128)S(1)}, u32[]{:S(2)}, u32[]{:S(2)}) %collective-permute-start.6) | collective-permute-done | bytes 81952 | tf_op jit(solution)/shard_map/ppermute | solution.py:289
  41.4 1.6 %collective-permute-start.7 = (f32[160,128]{1,0:T(8,128)S(1)}, f32[160,128]{1,0:T(8,128)S(1)}, u32[]{:S(2)}, u32[]{:S(2)}) collective-permute-start(f32[160,128]{1,0:T(8,128)S(1)} %add.12), channel_id=1, source_target_pairs={{0,2},{1,3},{2,0},{3,1},{4,6},{5,7},{6,4},{7,5},{8,10},{9,11},{10,... | collective-permute-start | bytes 245768 | tf_op jit(solution)/shard_map/ppermute | solution.py:289
  43.0 3.1 %collective-permute-done.7 = f32[160,128]{1,0:T(8,128)S(1)} collective-permute-done((f32[160,128]{1,0:T(8,128)S(1)}, f32[160,128]{1,0:T(8,128)S(1)}, u32[]{:S(2)}, u32[]{:S(2)}) %collective-permute-start.7) | collective-permute-done | bytes 81952 | tf_op jit(solution)/shard_map/ppermute | solution.py:289
  46.0 2.7 %collective-permute-start.8 = (f32[160,128]{1,0:T(8,128)S(1)}, f32[160,128]{1,0:T(8,128)S(1)}, u32[]{:S(2)}, u32[]{:S(2)}) collective-permute-start(f32[160,128]{1,0:T(8,128)S(1)} %add.13), channel_id=1, source_target_pairs={{0,4},{1,5},{2,6},{3,7},{4,0},{5,1},{6,2},{7,3},{8,12},{9,13},{10,... | collective-permute-start | bytes 245768 | tf_op jit(solution)/shard_map/ppermute | solution.py:289
  48.8 2.4 %collective-permute-done.8 = f32[160,128]{1,0:T(8,128)S(1)} collective-permute-done((f32[160,128]{1,0:T(8,128)S(1)}, f32[160,128]{1,0:T(8,128)S(1)}, u32[]{:S(2)}, u32[]{:S(2)}) %collective-permute-start.8) | collective-permute-done | bytes 81952 | tf_op jit(solution)/shard_map/ppermute | solution.py:289
  51.2 3.0 %collective-permute-start.9 = (f32[160,128]{1,0:T(8,128)S(1)}, f32[160,128]{1,0:T(8,128)S(1)}, u32[]{:S(2)}, u32[]{:S(2)}) collective-permute-start(f32[160,128]{1,0:T(8,128)S(1)} %add.14), channel_id=1, source_target_pairs={{0,8},{1,9},{2,10},{3,11},{4,12},{5,13},{6,14},{7,15},{8,0},{9,1},... | collective-permute-start | bytes 245768 | tf_op jit(solution)/shard_map/ppermute | solution.py:289
  54.2 2.4 %collective-permute-done.9 = f32[160,128]{1,0:T(8,128)S(1)} collective-permute-done((f32[160,128]{1,0:T(8,128)S(1)}, f32[160,128]{1,0:T(8,128)S(1)}, u32[]{:S(2)}, u32[]{:S(2)}) %collective-permute-start.9) | collective-permute-done | bytes 81952 | tf_op jit(solution)/shard_map/ppermute | solution.py:289
  56.7 1.3 %collective-permute-done.10.other = f32[160,128]{1,0:T(8,128)S(1)} collective-permute-done((f32[160,128]{1,0:T(8,128)S(1)}, f32[160,128]{1,0:T(8,128)S(1)}, u32[]{:S(2)}, u32[]{:S(2)}) %collective-permute-start.10) | collective-permute-done | bytes 81952 | tf_op jit(solution)/shard_map/ppermute | solution.py:289
  58.0 0.6 %copy-done.7 = f32[160,128]{1,0:T(8,128)} copy-done((f32[160,128]{1,0:T(8,128)}, f32[160,128]{1,0:T(8,128)S(1)}, u32[]{:S(2)}) %copy-start.7) | copy-done | bytes 81944
  58.6 1.8 %shard_map.88 = (f32[16,16]{1,0:T(8,128)}, f32[128,128]{1,0:T(8,128)}, f32[128,128]{1,0:T(8,128)}, f32[128,128]{1,0:T(8,128)}) custom-call(f32[160,128]{1,0:T(8,128)} %copy-done.6, f32[160,128]{1,0:T(8,128)} %copy-done.7), custom_call_target="tpu_custom_call" | custom-call | tf_op jit(solution)/shard_map/pallas_call | solution.py:341
  (25 shorter events, 0.5 us)
Async XLA Ops:
  0.6 8.8 %copy-start.3 = (bf16[128,64]{0,1:T(8,128)(2,1)S(1)}, bf16[128,64]{0,1:T(8,128)(2,1)}, u32[]{:S(2)}) copy-start(bf16[128,64]{0,1:T(8,128)(2,1)} %param.9) | copy-start | bytes 49156
  0.6 8.7 %copy-start.2 = (bf16[128,64]{0,1:T(8,128)(2,1)S(1)}, bf16[128,64]{0,1:T(8,128)(2,1)}, u32[]{:S(2)}) copy-start(bf16[128,64]{0,1:T(8,128)(2,1)} %param.8) | copy-start | bytes 49156
  0.7 8.7 %copy-start = (bf16[1,128,128,128]{3,2,1,0:T(8,128)(2,1)S(1)}, bf16[1,128,128,128]{3,2,1,0:T(8,128)(2,1)}, u32[]{:S(2)}) copy-start(bf16[1,128,128,128]{3,2,1,0:T(8,128)(2,1)} %param.5) | copy-start | bytes 12582916
  0.7 8.7 %copy-start.4 = (bf16[128,8]{0,1:T(8,128)(2,1)S(1)}, bf16[128,8]{0,1:T(8,128)(2,1)}, u32[]{:S(2)}) copy-start(bf16[128,8]{0,1:T(8,128)(2,1)} %param.7) | copy-start | bytes 6148
  3.9 15.8 %collective-permute-start.1 = (bf16[4,128,128]{2,1,0:T(8,128)(2,1)}, bf16[4,128,128]{2,1,0:T(8,128)(2,1)S(1)}, u32[]{:S(2)}, u32[]{:S(2)}) collective-permute-start(bf16[4,128,128]{2,1,0:T(8,128)(2,1)} %get-tuple-element.20), channel_id=1, source_target_pairs={{0,8},{1,9},{2,10},{3,11},{4,12},{5,13},{6,14},{7,15},{8,0},{9,1},... | collective-permute-start | bytes 393224 | tf_op jit(solution)/shard_map/ppermute | solution.py:289
  8.0 11.7 %collective-permute-start.2 = (bf16[4,128,128]{2,1,0:T(8,128)(2,1)}, bf16[4,128,128]{2,1,0:T(8,128)(2,1)S(1)}, u32[]{:S(2)}, u32[]{:S(2)}) collective-permute-start(bf16[4,128,128]{2,1,0:T(8,128)(2,1)} %get-tuple-element.21), channel_id=1, source_target_pairs={{0,12},{1,13},{2,14},{3,15},{4,8},{5,9},{6,10},{7,11},{8,4},{9,5},... | collective-permute-start | bytes 393224 | tf_op jit(solution)/shard_map/ppermute | solution.py:289
  9.4 0.8 %copy-start.1 = (bf16[256,128]{1,0:T(8,128)(2,1)S(1)}, bf16[256,128]{1,0:T(8,128)(2,1)}, u32[]{:S(2)}) copy-start(bf16[256,128]{1,0:T(8,128)(2,1)} %get-tuple-element.16.dd_in) | copy-start | bytes 196612
  14.1 6.0 %collective-permute-start = (bf16[4,128,128]{2,1,0:T(8,128)(2,1)S(1)}, bf16[4,128,128]{2,1,0:T(8,128)(2,1)S(1)}, u32[]{:S(2)}, u32[]{:S(2)}) collective-permute-start(bf16[4,128,128]{2,1,0:T(8,128)(2,1)S(1)} %get-tuple-element.19), channel_id=1, source_target_pairs={{0,4},{1,5},{2,6},{3,7},{4,0},{5,1},{6,2},{7,3},{8,12},{9,13},{10,... | collective-permute-start | bytes 393224 | tf_op jit(solution)/shard_map/ppermute | solution.py:289
  14.4 24.0 %all-to-all-start = ((bf16[16,192,128]{2,1,0:T(8,128)(2,1)}), bf16[16,192,128]{2,1,0:T(8,128)(2,1)S(1)}, u32[]{:S(2)}, u32[]{:S(2)}) async-start(bf16[16,192,128]{2,1,0:T(8,128)(2,1)} %get-tuple-element.17), calls=%async_computation | async-start | bytes 1572864 | tf_op jit(solution)/shard_map/all_to_all | solution.py:327
  20.2 18.2 %copy-start.5 = (bf16[16,8]{0,1:T(8,128)(2,1)S(1)}, bf16[16,8]{0,1:T(8,128)(2,1)}, u32[]{:S(2)}) copy-start(bf16[16,8]{0,1:T(8,128)(2,1)} %param.6) | copy-start | bytes 772
  20.2 1.9 %collective-permute-start.3 = (bf16[4,128,128]{2,1,0:T(8,128)(2,1)S(1)}, bf16[4,128,128]{2,1,0:T(8,128)(2,1)S(1)}, u32[]{:S(2)}, u32[]{:S(2)}) collective-permute-start(bf16[4,128,128]{2,1,0:T(8,128)(2,1)S(1)} %get-tuple-element.23), channel_id=1, source_target_pairs={{0,1},{1,0},{2,3},{3,2},{4,5},{5,4},{6,7},{7,6},{8,9},{9,8},{10,11... | collective-permute-start | bytes 393224 | tf_op jit(solution)/shard_map/ppermute | solution.py:289
  20.3 12.0 %collective-permute-start.4 = (bf16[4,128,128]{2,1,0:T(8,128)(2,1)S(1)}, bf16[4,128,128]{2,1,0:T(8,128)(2,1)S(1)}, u32[]{:S(2)}, u32[]{:S(2)}) collective-permute-start(bf16[4,128,128]{2,1,0:T(8,128)(2,1)S(1)} %get-tuple-element.24), channel_id=1, source_target_pairs={{0,2},{1,3},{2,0},{3,1},{4,6},{5,7},{6,4},{7,5},{8,10},{9,11},{10,... | collective-permute-start | bytes 393224 | tf_op jit(solution)/shard_map/ppermute | solution.py:289
  21.9 12.4 %collective-permute-start.5 = (bf16[4,128,128]{2,1,0:T(8,128)(2,1)S(1)}, bf16[4,128,128]{2,1,0:T(8,128)(2,1)S(1)}, u32[]{:S(2)}, u32[]{:S(2)}) collective-permute-start(bf16[4,128,128]{2,1,0:T(8,128)(2,1)S(1)} %get-tuple-element.25), channel_id=1, source_target_pairs={{0,3},{1,2},{2,1},{3,0},{4,7},{5,6},{6,5},{7,4},{8,11},{9,10},{10,... | collective-permute-start | bytes 393224 | tf_op jit(solution)/shard_map/ppermute | solution.py:289
  40.0 1.3 %collective-permute-start.6 = (f32[160,128]{1,0:T(8,128)S(1)}, f32[160,128]{1,0:T(8,128)S(1)}, u32[]{:S(2)}, u32[]{:S(2)}) collective-permute-start(f32[160,128]{1,0:T(8,128)S(1)} %get-tuple-element.27), channel_id=1, source_target_pairs={{0,1},{1,0},{2,3},{3,2},{4,5},{5,4},{6,7},{7,6},{8,9},{9,8},{10,11... | collective-permute-start | bytes 245768 | tf_op jit(solution)/shard_map/ppermute | solution.py:289
  41.4 4.7 %collective-permute-start.7 = (f32[160,128]{1,0:T(8,128)S(1)}, f32[160,128]{1,0:T(8,128)S(1)}, u32[]{:S(2)}, u32[]{:S(2)}) collective-permute-start(f32[160,128]{1,0:T(8,128)S(1)} %add.12), channel_id=1, source_target_pairs={{0,2},{1,3},{2,0},{3,1},{4,6},{5,7},{6,4},{7,5},{8,10},{9,11},{10,... | collective-permute-start | bytes 245768 | tf_op jit(solution)/shard_map/ppermute | solution.py:289
  46.0 5.2 %collective-permute-start.8 = (f32[160,128]{1,0:T(8,128)S(1)}, f32[160,128]{1,0:T(8,128)S(1)}, u32[]{:S(2)}, u32[]{:S(2)}) collective-permute-start(f32[160,128]{1,0:T(8,128)S(1)} %add.13), channel_id=1, source_target_pairs={{0,4},{1,5},{2,6},{3,7},{4,0},{5,1},{6,2},{7,3},{8,12},{9,13},{10,... | collective-permute-start | bytes 245768 | tf_op jit(solution)/shard_map/ppermute | solution.py:289
  51.2 5.4 %collective-permute-start.9 = (f32[160,128]{1,0:T(8,128)S(1)}, f32[160,128]{1,0:T(8,128)S(1)}, u32[]{:S(2)}, u32[]{:S(2)}) collective-permute-start(f32[160,128]{1,0:T(8,128)S(1)} %add.14), channel_id=1, source_target_pairs={{0,8},{1,9},{2,10},{3,11},{4,12},{5,13},{6,14},{7,15},{8,0},{9,1},... | collective-permute-start | bytes 245768 | tf_op jit(solution)/shard_map/ppermute | solution.py:289
  56.6 1.4 %copy-start.6 = (f32[160,128]{1,0:T(8,128)}, f32[160,128]{1,0:T(8,128)S(1)}, u32[]{:S(2)}) copy-start(f32[160,128]{1,0:T(8,128)S(1)} %add.15.mine) | copy-start | bytes 245764
  56.7 1.3 %collective-permute-start.10 = (f32[160,128]{1,0:T(8,128)S(1)}, f32[160,128]{1,0:T(8,128)S(1)}, u32[]{:S(2)}, u32[]{:S(2)}) collective-permute-start(f32[160,128]{1,0:T(8,128)S(1)} %add.15.mine), channel_id=1, source_target_pairs={{0,1},{1,0},{2,3},{3,2},{4,5},{5,4},{6,7},{7,6},{8,9},{9,8},{10,11... | collective-permute-start | bytes 245768 | tf_op jit(solution)/shard_map/ppermute | solution.py:289
  58.0 0.6 %copy-start.7 = (f32[160,128]{1,0:T(8,128)}, f32[160,128]{1,0:T(8,128)S(1)}, u32[]{:S(2)}) copy-start(f32[160,128]{1,0:T(8,128)S(1)} %collective-permute-done.10.other) | copy-start | bytes 245764

commit v3 on v2

--- a/solution.py
+++ b/solution.py
@@ -13,7 +13,6 @@
 DET_SCALE = 1.0 / (SCAN_RANK * SCAN_RANK * DET_RANK)
 LANES = 128
 GROUP = 16
-COST = pl.CostEstimate(flops=10**8, bytes_accessed=4 << 20, transcendentals=0)
 BF16 = jnp.bfloat16
 F32 = jnp.float32
 LAST = (((1,), (1,)), ((), ()))
@@ -42,9 +41,10 @@
 
 
 def early_cubes(early, own, base, slab, dt_in, vt_in, *refs):
-    *far, dd, dt, vt, images, right, arrived, ready = refs
+    *outs, dt, vt, images, right, far, arrived, ready, sent = refs
     pixels = slab.shape[1]
-    rank = own * far[0].shape[0] * len(far)
+    plane = outs[0].shape[0]
+    rank = own * plane * len(outs)
     pitch = early + 1
     cuts = [0, early // 2, early]
     copies = [
@@ -56,7 +56,7 @@
         copy.start()
     for copy in factors:
         copy.wait()
-    vt2, dd[...] = paired(slot_order(vt[...], own, base, rank)), paired(dt[...].T)
+    vt2, dd = paired(slot_order(vt[...], own, base, rank)), paired(dt[...].T)
     for at, copy in enumerate(copies):
         copy.wait()
         for c in range(cuts[at], cuts[at + 1], 4):
@@ -66,7 +66,14 @@
                     right[pl.ds(c + 2 * i + j, rank, stride=pitch), :] = rights[
                         j * rank : (j + 1) * rank, i * pixels : (i + 1) * pixels
                     ]
-    owner_cubes(early, pitch, own, right, dd[...], far)
+    copies = []
+    for slot in range(plane * len(outs)):
+        slot_cubes(slot, early, pitch, own, right, dd, far.at[slot])
+        out = outs[slot // plane].at[slot % plane]
+        copies.append(pltpu.make_async_copy(far.at[slot], out, sent.at[slot]))
+        copies[-1].start()
+    for copy in copies:
+        copy.wait()
 
 
 def slot_order(factor, own, base, count):
@@ -77,20 +84,15 @@
     return dot(take.astype(BF16), factor).astype(BF16)
 
 
-def owner_cubes(early, pitch, own, right, dd, arrays):
-    plane = arrays[0].shape[0]
-    for slot in range(plane * len(arrays)):
-        to = arrays[slot // plane].at[slot % plane]
-        for h in range(own // 2):
-            b = slot * own + 2 * h
-            x = [right[pl.ds((b + k) * pitch, early), :] for k in range(2)]
-            to[pl.ds(h * early, early), :] = dot(jnp.concatenate(x, axis=1).astype(BF16), dd).astype(BF16)
-
-
-def late_cubes(early, own, images, cft, dt, vt, dd_in, *refs):
-    *near, second, right, left, dd, ready = refs
-    copy = pltpu.make_async_copy(dd_in, dd, ready)
-    copy.start()
+def slot_cubes(slot, early, pitch, own, right, dd, to):
+    for h in range(own // 2):
+        b = slot * own + 2 * h
+        x = [right[pl.ds((b + k) * pitch, early), :] for k in range(2)]
+        to[pl.ds(h * early, early), :] = dot(jnp.concatenate(x, axis=1).astype(BF16), dd).astype(BF16)
+
+
+def late_cubes(early, own, images, cft, dt, vt, *refs):
+    *near, out, right, left, second, sent = refs
     cols, pixels, rank = images.shape[0], images.shape[1], dt.shape[0]
     pitch = cols + 1
     dt2, vt2 = (paired(slot_order(x[...], own, 0, rank)) for x in (dt, vt))
@@ -103,7 +105,7 @@
                 at_c = pl.ds(c + 2 * i + j, rank, stride=pitch)
                 right[at_c, :] = rights[j * rank : (j + 1) * rank, i * pixels : (i + 1) * pixels]
                 left[at_c, :] = lefts[i * rank : (i + 1) * rank, j * pixels : (j + 1) * pixels]
-    copy.wait()
+    dd = paired(dt[...].T)
     pairs, pair = own // 2, 2 * SCAN_RANK
     late = cols - early
 
@@ -115,16 +117,23 @@
         return jnp.concatenate([sums[:, :pixels], sums[:, pixels:]], axis=0).astype(BF16)
 
     me = lax.axis_index("row")
+    copies = []
     for slot in range(rank // own):
         p = me ^ slot
         for h in range(pairs):
             x = two(right, slot * own + 2 * h)
             y = two(left, slot * own + 2 * h)
             at = pairs * late + h * pair
-            second[p, pl.ds(h * late, late), :] = dot(x[early:], dd[...]).astype(BF16)
-            second[p, pl.ds(at, pair), :] = stacked(dot(cft[...], x))
-            second[p, pl.ds(at + pairs * pair, pair), :] = stacked(dot(cft[...], y))
-    owner_cubes(early, pitch, own, right, dd[...], near)
+            second[slot, pl.ds(h * late, late), :] = dot(x[early:], dd).astype(BF16)
+            second[slot, pl.ds(at, pair), :] = stacked(dot(cft[...], x))
+            second[slot, pl.ds(at + pairs * pair, pair), :] = stacked(dot(cft[...], y))
+        copies.append(pltpu.make_async_copy(second.at[slot], out.at[p], sent.at[slot]))
+        copies[-1].start()
+    plane = near[0].shape[0]
+    for slot in range(plane * len(near)):
+        slot_cubes(slot, early, pitch, own, right, dd, near[slot // plane].at[slot % plane])
+    for copy in copies:
+        copy.wait()
 
 
 def projections(n, plane, early, slab, cft, dt, vt):
@@ -136,19 +145,20 @@
     params = pltpu.CompilerParams(vmem_limit_bytes=56 << 20)
     half = n // plane // 2
     part = [jax.ShapeDtypeStruct((plane, own // 2 * early, pixels), BF16)] * half
-    pair = jax.ShapeDtypeStruct((2 * pixels, 2 * rank), BF16)
-    *far, dd = pl.pallas_call(
+    far = pl.pallas_call(
         functools.partial(early_cubes, early, own, n // 2),
-        out_shape=part + [pair],
+        out_shape=part,
         in_specs=[anywhere] * 3,
-        out_specs=[in_vmem] * (half + 1),
+        out_specs=[anywhere] * half,
         scratch_shapes=[
             pltpu.VMEM(dt.shape, BF16),
             pltpu.VMEM(vt.shape, BF16),
             pltpu.VMEM((early,) + slab.shape[1:], BF16),
             pltpu.VMEM((rank // 2 * (early + 1), pixels), F32),
+            pltpu.VMEM((n // 2, own // 2 * early, pixels), BF16),
             pltpu.SemaphoreType.DMA((2,)),
             pltpu.SemaphoreType.DMA((2,)),
+            pltpu.SemaphoreType.DMA((n // 2,)),
         ],
         compiler_params=params,
     )(slab, dt, vt)
@@ -156,13 +166,13 @@
     *near, second = pl.pallas_call(
         functools.partial(late_cubes, early, own),
         out_shape=part + [jax.ShapeDtypeStruct((n, height, pixels), BF16)],
-        in_specs=[in_vmem] * 4 + [anywhere],
-        out_specs=[in_vmem] * (half + 1),
+        in_specs=[in_vmem] * 4,
+        out_specs=[in_vmem] * half + [anywhere],
         scratch_shapes=[pltpu.VMEM((rank * (cols + 1), pixels), F32)] * 2
-        + [pltpu.VMEM(dd.shape, BF16), pltpu.SemaphoreType.DMA],
+        + [pltpu.VMEM((n, height, pixels), BF16), pltpu.SemaphoreType.DMA((n,))],
         compiler_params=pltpu.CompilerParams(vmem_limit_bytes=32 << 20),
-    )(slab, cft, dt, vt, dd)
-    return near + far, second
+    )(slab, cft, dt, vt)
+    return near + list(far), second
 
 
 def one_hot(shape, rows_per, cols_per):
@@ -185,72 +195,83 @@
     return jnp.where(r % GROUP == c % GROUP, weights, 0.0).astype(BF16)
 
 
-def partial_grams(own, plane, early, rft, cft, second, *refs):
-    *first, keep, send, unfold, rowbuf, total = refs
-    rows, cols, pixels = rft.shape[1], cft.shape[1], second.shape[2]
-    pairs, late = own // 2, cols - early
+def wide(get, at, size, pitch, pairs):
+    return jnp.concatenate([get(at + h * pitch, size) for h in range(pairs)], axis=1)
+
+
+def stack_rows(arrays, at, size):
+    return jnp.concatenate([x[pl.ds(at, size), :] for x in arrays], axis=0)
+
+
+def store_unfold(unfold, at, u):
+    for i in range(SCAN_RANK):
+        unfold[i, pl.ds(at, GROUP), :] = u[i * GROUP : (i + 1) * GROUP]
+
+
+def early_grams(own, plane, rft, cft, *refs):
+    *first, plain, unfold, rowpart, corner = refs
+    rows = rft.shape[1]
+    pairs = own // 2
+    early = first[0].shape[1] // pairs
     me = lax.axis_index("row")
     mixed = spread_weights(rft, rows, me)
-    plain = spread_weights(rft, rows)
-
-    def old(s, at, size):
-        return first[s % plane][s // plane, pl.ds(at, size), :]
-
-    def new(s, at, size):
-        return second[s, pl.ds(at, size), :]
-
-    def wide(get, at, size, pitch):
-        return jnp.concatenate([get(at + h * pitch, size) for h in range(pairs)], axis=1)
-
-    def all_rows(get, at, size):
-        return jnp.concatenate([get(s, at, size) for s in range(rows)], axis=0)
-
-    for c in range(0, cols, GROUP):
-        if c < early:
-            u = dot(mixed, wide(functools.partial(all_rows, old), c, GROUP, early))
-        else:
-            u = dot(plain, wide(functools.partial(all_rows, new), c - early, GROUP, late))
-        u = u.astype(BF16)
-        for i in range(SCAN_RANK):
-            unfold[i, pl.ds(c, GROUP), :] = u[i * GROUP : (i + 1) * GROUP]
-    gram = jnp.zeros((cols, cols), F32)
+    plain[...] = spread_weights(rft, rows)
+    slots = [first[s % plane].at[s // plane] for s in range(rows)]
+    for c in range(0, early, GROUP):
+        x = wide(functools.partial(stack_rows, slots), c, GROUP, early, pairs)
+        store_unfold(unfold, c, dot(mixed, x).astype(BF16))
+    gram = jnp.zeros((early, early), F32)
     for i in range(SCAN_RANK):
         gram += dot(unfold[i], unfold[i], LAST)
-    half = cols // 2
-    pack(total, 0, gram * SCAN_SCALE)
+    corner[...] = gram * SCAN_SCALE
     for s in range(rows):
-        y = dot(cft[:, :early], wide(functools.partial(old, s), 0, early, early))
-        z = dot(cft[:, early:], wide(functools.partial(new, s), 0, late, late))
+        x = wide(lambda at, size: slots[s][pl.ds(at, size), :], 0, early, early, pairs)
+        y = dot(cft[:, :early], x)
         for h in range(pairs):
-            lanes = slice(h * LANES, (h + 1) * LANES)
-            rowbuf[0, h, pl.ds(me ^ s, SCAN_RANK, stride=rows), :] = y[:, lanes]
-            rowbuf[1, h, pl.ds(s, SCAN_RANK, stride=rows), :] = z[:, lanes]
+            rowpart[h, pl.ds(me ^ s, SCAN_RANK, stride=rows), :] = y[:, h * LANES : (h + 1) * LANES]
+
+
+def partial_grams(own, cft, plain, early_unfold, rowpart, corner, second, keep, send, unfold, rowbuf, total):
+    rows, cols, pixels = second.shape[0], cft.shape[1], second.shape[2]
+    pairs, half = own // 2, cols // 2
+    slots = [second.at[s] for s in range(rows)]
+    for c in range(0, half, GROUP):
+        x = wide(functools.partial(stack_rows, slots), c, GROUP, half, pairs)
+        store_unfold(unfold, c, dot(plain[...], x).astype(BF16))
+    side = jnp.zeros((half, half), F32)
+    gram = jnp.zeros((half, half), F32)
+    for i in range(SCAN_RANK):
+        side += dot(early_unfold[i], unfold[i], LAST)
+        gram += dot(unfold[i], unfold[i], LAST)
+    total[pl.ds(0, half), :] = jnp.concatenate([corner[...], side * SCAN_SCALE], axis=1)
+    total[pl.ds(3 * half, half), pl.ds(0, half)] = gram * SCAN_SCALE
+    for s in range(rows):
+        x = wide(lambda at, size: slots[s][pl.ds(at, size), :], 0, half, half, pairs)
+        y = dot(cft[:, half:], x)
+        for h in range(pairs):
+            rowbuf[h, pl.ds(s, SCAN_RANK, stride=rows), :] = y[:, h * LANES : (h + 1) * LANES]
     gram = jnp.zeros((rows, rows), F32)
     for i in range(SCAN_RANK):
         for h in range(pairs):
             at = pl.ds(i * rows, rows)
-            x = (rowbuf[0, h, at, :] + rowbuf[1, h, at, :]).astype(BF16)
+            x = (rowbuf[h, at, :] + rowpart[h, at, :]).astype(BF16)
             gram += dot(x, x, LAST)
     spare = jnp.concatenate([gram * SCAN_SCALE, jnp.zeros((rows, half - rows), F32)], axis=1)
     total[pl.ds(5 * half - rows, rows), pl.ds(half, half)] = spare
     n_part = own * SCAN_RANK
-    for side in range(2):
+    for k in range(2):
         gram = jnp.zeros((pixels, pixels), F32)
         for g in range(n_part // GROUP):
-            at = pairs * late + side * n_part + g * GROUP
-            u = dot(plain, all_rows(new, at, GROUP)).astype(BF16)
+            at = pairs * half + k * n_part + g * GROUP
+            u = dot(plain[...], stack_rows(slots, at, GROUP)).astype(BF16)
             gram += dot(u, u, FIRST)
-        pack(total, 1 + side, gram * DET_SCALE)
+        gram *= DET_SCALE
+        total[pl.ds((1 + k) * half, half), :] = gram[:half]
+        total[pl.ds((3 + (1 + k) // 2) * half, half), pl.ds((1 + k) % 2 * half, half)] = gram[half:, half:]
     size = keep.shape[0]
-    core = me % 2
+    core = lax.axis_index("row") % 2
     keep[...] = total[pl.ds(pl.multiple_of(core * size, 8), size), :]
     send[...] = total[pl.ds(pl.multiple_of((1 - core) * size, 8), size), :]
-
-
-def pack(total, k, gram):
-    half = gram.shape[0] // 2
-    total[pl.ds(k * half, half), :] = gram[:half]
-    total[pl.ds((3 + k // 2) * half, half), pl.ds(k % 2 * half, half)] = gram[half:, half:]
 
 
 def unpack(mine, other, row_out, col_out, right_out, left_out, row_gram, grams, sems):
@@ -275,13 +296,13 @@
         copy.wait()
 
 
-def call(kernel, args, outs, scratch=(), flops=10**8):
+def call(kernel, args, outs, scratch=(), cost=10**8):
     return pl.pallas_call(
         kernel,
-        out_shape=[jax.ShapeDtypeStruct(shape, F32) for shape in outs],
+        out_shape=[jax.ShapeDtypeStruct(*out) for out in outs],
         scratch_shapes=scratch,
         compiler_params=pltpu.CompilerParams(vmem_limit_bytes=40 << 20),
-        cost_estimate=pl.CostEstimate(flops=flops, bytes_accessed=4 << 20, transcendentals=0),
+        cost_estimate=pl.CostEstimate(flops=cost, bytes_accessed=1 << 20, transcendentals=0),
     )(*args)
 
 
@@ -289,21 +310,28 @@
     return lax.ppermute(x, "row", [(i, i ^ step) for i in range(n)])
 
 
-def regroup(*refs):
-    before, after = refs[: len(refs) // 2], refs[len(refs) // 2 :]
+def by_place(plane, *refs):
+    before, after = refs[:-plane], refs[-plane:]
     for z, x in enumerate(before):
         for q, y in enumerate(after):
             y[z] = x[q]
 
 
-def regrouped(first):
-    planes, (plane, height, width) = len(first), first[0].shape
-    return pl.pallas_call(
-        regroup,
-        out_shape=[jax.ShapeDtypeStruct((planes, height, width), BF16)] * plane,
-        compiler_params=pltpu.CompilerParams(vmem_limit_bytes=40 << 20),
-        cost_estimate=pl.CostEstimate(flops=4 * 10**10, bytes_accessed=4 << 20, transcendentals=0),
-    )(*first)
+def join_planes(near, *refs):
+    plane = (len(refs) - near) // 2
+    before, far, after = refs[:near], refs[near : near + plane], refs[near + plane :]
+    for q, y in enumerate(after):
+        for z, x in enumerate(before):
+            y[z] = x[q]
+        y[pl.ds(near, y.shape[0] - near)] = far[q][...]
+
+
+def regrouped(near, far):
+    plane, height, width = near[0].shape
+    some = [((len(far), height, width), BF16)] * plane
+    every = [((len(near) + len(far), height, width), BF16)] * plane
+    far = call(functools.partial(by_place, plane), far, some, cost=4 * 10**10)
+    return call(functools.partial(join_planes, len(near)), (*near, *far), every)
 
 
 def all_sum(mine, other, n):
@@ -325,16 +353,25 @@
     first, second = projections(n, plane, early, slab, cft, det_row_factor.T, det_col_factor.T)
     first = [x if z == 0 else swap(x, n, z * plane) for z, x in enumerate(first)]
     second = lax.all_to_all(second, "row", split_axis=0, concat_axis=0, tiled=True)
-    first = regrouped(first)
+    first = regrouped(first[: plane // 2], first[plane // 2 :])
     first = [x if q == 0 else swap(x, n, q) for q, x in enumerate(first)]
-    half = (5 * cols // 4, pixels)
+    pairs, width = own // 2, own * DET_RANK
+    row_shape = (pairs, SCAN_RANK * rows, LANES)
+    shapes = [
+        ((SCAN_RANK * GROUP, rows * GROUP), BF16),
+        ((SCAN_RANK, early, width), BF16),
+        (row_shape, F32),
+        ((early, early), F32),
+    ]
+    known = call(functools.partial(early_grams, own, plane), (rft, cft, *first), shapes)
     scratch = [
-        pltpu.VMEM((SCAN_RANK, cols, own * DET_RANK), BF16),
-        pltpu.VMEM((2, own // 2, SCAN_RANK * rows, LANES), F32),
+        pltpu.VMEM((SCAN_RANK, early, width), BF16),
+        pltpu.VMEM(row_shape, F32),
         pltpu.VMEM((5 * cols // 2, pixels), F32),
     ]
-    kernel = functools.partial(partial_grams, own, plane, early)
-    mine, other = call(kernel, (rft, cft, second, *first), (half, half), scratch)
+    mine, other = call(
+        functools.partial(partial_grams, own), (cft, *known, second), [((5 * cols // 4, pixels), F32)] * 2, scratch
+    )
     mine, other = all_sum(mine, other, n)
     outs = [(rows, rows), (cols, cols), (pixels, pixels), (pixels, pixels)]
     in_vmem = pl.BlockSpec(memory_space=pltpu.VMEM)
@@ -348,6 +385,7 @@
             pltpu.VMEM((3, cols, cols), F32),
             pltpu.SemaphoreType.DMA((4,)),
         ],
+        compiler_params=pltpu.CompilerParams(vmem_limit_bytes=16 << 20),
     )(mine, other)
 
 

time: 60.7 us -> 57.5 us (0.947)
  local copies, waits for them, and re-layouts: 1.49 us -> 0.02 us
  Pallas kernels: 10.6 us -> 9.77 us
  waiting for transfers between devices: 26.9 us -> 26.1 us
    unnamed x16 -> x10, local copies, waits for them, and re-layouts: 1.49 us -> 0.02 us
    pallas_call x1, Pallas kernels: 1.81 us -> 0.89 us  [local(): pl.pallas_call(unpack, out_shape=[jax.ShapeDtypeStruct(shape, F32) for sh...]
    all_to_all x1, waiting for transfers between devices: 4.12 us -> 3.31 us  [local(): lax.all_to_all(second, 'row', split_axis=0, concat_axis=0, tiled=True)]
    pallas_call x2 -> x4, Pallas kernels: 1.64 us -> 1.98 us  [call(): pl.pallas_call(kernel, out_shape=[jax.ShapeDtypeStruct(*out) for out in o...]
  transfers between devices with their start and end apart: 12 -> 12, of which waited for: 9 -> 9; matrix products, arithmetic and copies ran while one was open for 0% -> 0% of each run, Pallas kernels for 6% -> 8%
where the time goes in v3:
time: 57.5 us; the launch traced here: 57.3 us
  waiting for transfers between devices  26.1 us (45%)
  starting transfers between devices  20.7 us (36%)
  Pallas kernels  9.77 us (17%)
  between operations  0.78 us (1%)
    ppermute x11, waiting for transfers between devices, swap(): return lax.ppermute(x, 'row', [(i, i ^ step) for i in range(n)])  22.8 us
    ppermute x11, starting transfers between devices, swap(): return lax.ppermute(x, 'row', [(i, i ^ step) for i in range(n)])  15.4 us
    all_to_all x1, starting transfers between devices, local(): lax.all_to_all(second, 'row', split_axis=0, concat_axis=0, tiled=True)  5.24 us
    pallas_call x1, Pallas kernels, projections(): pl.pallas_call(functools.partial(late_cubes, early, own), out_shape=part...  3.64 us
    all_to_all x1, waiting for transfers between devices, local(): lax.all_to_all(second, 'row', split_axis=0, concat_axis=0, tiled=True)  3.31 us
    pallas_call x1, Pallas kernels, projections(): pl.pallas_call(functools.partial(early_cubes, early, own, n // 2), out_sh...  3.25 us
    pallas_call x4, Pallas kernels, call(): pl.pallas_call(kernel, out_shape=[jax.ShapeDtypeStruct(*out) for out in o...  1.98 us
  transfers between devices with their start and end apart: 12, of which 9 were waited for; matrix products, arithmetic and copies ran while one was open for 0% of the time, Pallas kernels for 8%

profile of v3, /device:TPU:0, one launch (start us, length us, event | category | flops | bytes accessed | tf_op | source)
XLA Modules:
  0.0 57.3 jit_solution(16030500751849811871)
XLA Ops:
  0.7 3.3 %shard_map.85 = (bf16[4,128,128]{2,1,0:T(8,128)(2,1)}, bf16[4,128,128]{2,1,0:T(8,128)(2,1)}) custom-call(bf16[128,128,128]{2,1,0:T(8,128)(2,1)} %bitcast.5, bf16[64,128]{1,0:T(8,128)(2,1)} %bitcast.7, bf16[64,128]{1,0:T(8,128)(2,1)} %bitcast.9), custom_call_target="tpu_custom_call" | custom-call | tf_op jit(solution)/shard_map/pallas_call | solution.py:148
  3.9 4.1 %collective-permute-start.1 = (bf16[4,128,128]{2,1,0:T(8,128)(2,1)}, bf16[4,128,128]{2,1,0:T(8,128)(2,1)S(1)}, u32[]{:S(2)}, u32[]{:S(2)}) collective-permute-start(bf16[4,128,128]{2,1,0:T(8,128)(2,1)} %get-tuple-element.25), channel_id=1, source_target_pairs={{0,8},{1,9},{2,10},{3,11},{4,12},{5,13},{6,14},{7,15},{8,0},{9,1},... | collective-permute-start | bytes 393224 | tf_op jit(solution)/shard_map/ppermute | solution.py:310
  8.0 1.3 %collective-permute-start.2 = (bf16[4,128,128]{2,1,0:T(8,128)(2,1)}, bf16[4,128,128]{2,1,0:T(8,128)(2,1)S(1)}, u32[]{:S(2)}, u32[]{:S(2)}) collective-permute-start(bf16[4,128,128]{2,1,0:T(8,128)(2,1)} %get-tuple-element.26), channel_id=1, source_target_pairs={{0,12},{1,13},{2,14},{3,15},{4,8},{5,9},{6,10},{7,11},{8,4},{9,5},... | collective-permute-start | bytes 393224 | tf_op jit(solution)/shard_map/ppermute | solution.py:310
  9.4 3.6 %shard_map.84 = (bf16[4,128,128]{2,1,0:T(8,128)(2,1)S(1)}, bf16[4,128,128]{2,1,0:T(8,128)(2,1)S(1)}, bf16[16,192,128]{2,1,0:T(8,128)(2,1)}) custom-call(bf16[128,128,128]{2,1,0:T(8,128)(2,1)S(1)} %bitcast.6, bf16[8,128]{1,0:T(8,128)(2,1)S(1)} %bitcast.11, bf16[64,128]{1,0:T(8,128)(2,1)S(1)} %bitcast.8, bf16[64,128]{1,0:T(8,128)(2,1)S(1)} %bitcast.10), custom_call_target="tpu_custom_call" | custom-call | tf_op jit(solution)/shard_map/pallas_call | solution.py:166
  13.0 0.3 collective-permute-start
  13.4 5.2 %all-to-all-start = ((bf16[16,192,128]{2,1,0:T(8,128)(2,1)}), bf16[16,192,128]{2,1,0:T(8,128)(2,1)S(1)}, u32[]{:S(2)}, u32[]{:S(2)}) async-start(bf16[16,192,128]{2,1,0:T(8,128)(2,1)} %get-tuple-element.39), calls=%async_computation | async-start | bytes 1572864 | tf_op jit(solution)/shard_map/all_to_all | solution.py:355
  18.7 1.5 %collective-permute-done.refs_1_ = bf16[4,128,128]{2,1,0:T(8,128)(2,1)S(1)} collective-permute-done((bf16[4,128,128]{2,1,0:T(8,128)(2,1)S(1)}, bf16[4,128,128]{2,1,0:T(8,128)(2,1)S(1)}, u32[]{:S(2)}, u32[]{:S(2)}) %collective-permute-start) | collective-permute-done | bytes 131104 | tf_op jit(solution)/shard_map/ppermute | solution.py:310
  20.3 1.6 %collective-permute-start.4 = (bf16[4,128,128]{2,1,0:T(8,128)(2,1)S(1)}, bf16[4,128,128]{2,1,0:T(8,128)(2,1)S(1)}, u32[]{:S(2)}, u32[]{:S(2)}) collective-permute-start(bf16[4,128,128]{2,1,0:T(8,128)(2,1)S(1)} %get-tuple-element.33), channel_id=1, source_target_pairs={{0,2},{1,3},{2,0},{3,1},{4,6},{5,7},{6,4},{7,5},{8,10},{9,11},{10,... | collective-permute-start | bytes 393224 | tf_op jit(solution)/shard_map/ppermute | solution.py:310
  21.9 0.2 collective-permute-start.5
  22.2 9.0 %collective-permute-done.4.refs_2_ = bf16[4,128,128]{2,1,0:T(8,128)(2,1)S(1)} collective-permute-done((bf16[4,128,128]{2,1,0:T(8,128)(2,1)S(1)}, bf16[4,128,128]{2,1,0:T(8,128)(2,1)S(1)}, u32[]{:S(2)}, u32[]{:S(2)}) %collective-permute-start.4) | collective-permute-done | bytes 131104 | tf_op jit(solution)/shard_map/ppermute | solution.py:310
  31.2 2.0 %collective-permute-done.5.refs_3_ = bf16[4,128,128]{2,1,0:T(8,128)(2,1)S(1)} collective-permute-done((bf16[4,128,128]{2,1,0:T(8,128)(2,1)S(1)}, bf16[4,128,128]{2,1,0:T(8,128)(2,1)S(1)}, u32[]{:S(2)}, u32[]{:S(2)}) %collective-permute-start.5) | collective-permute-done | bytes 131104 | tf_op jit(solution)/shard_map/ppermute | solution.py:310
  33.2 0.8 %shard_map.88 = (bf16[128,256]{1,0:T(8,128)(2,1)S(1)}, bf16[8,64,256]{2,1,0:T(8,128)(2,1)S(1)}, f32[2,128,128]{2,1,0:T(8,128)S(1)}, f32[64,64]{1,0:T(8,128)S(1)}) custom-call(bf16[8,16]{1,0:T(8,128)(2,1)S(1)} %bitcast.14, bf16[8,128]{1,0:T(8,128)(2,1)S(1)} %bitcast.12, bf16[4,128,128]{2,1,0:T(8,128)(2,1)S(1)} %get-tuple-element.31.refs_0_, ...), custom_call_target="tpu_custom_call" | custom-call | flops 100000000 | bytes 1048576 | tf_op jit(solution)/shard_map/pallas_call | solution.py:300
  34.0 3.3 %all-to-all-done.second = bf16[16,192,128]{2,1,0:T(8,128)(2,1)S(1)} async-done(((bf16[16,192,128]{2,1,0:T(8,128)(2,1)}), bf16[16,192,128]{2,1,0:T(8,128)(2,1)S(1)}, u32[]{:S(2)}, u32[]{:S(2)}) %all-to-all-start) | async-done | bytes 786464 | tf_op jit(solution)/shard_map/all_to_all | solution.py:355
  37.3 1.1 %shard_map.89 = (f32[160,128]{1,0:T(8,128)S(1)}, f32[160,128]{1,0:T(8,128)S(1)}) custom-call(bf16[8,128]{1,0:T(8,128)(2,1)S(1)} %bitcast.13, bf16[128,256]{1,0:T(8,128)(2,1)S(1)} %get-tuple-element.35.plain, bf16[8,64,256]{2,1,0:T(8,128)(2,1)S(1)} %get-tuple-element.36.early_unfold, f32[2,128,128]{2,1,0:T(8,128)S(1)} %get-tuple-element.37.rowpart, ...), custom_call_target="tpu_custom_call" | custom-call | flops 100000000 | bytes 1048576 | tf_op jit(solution)/shard_map/pallas_call | solution.py:300
  38.5 0.3 collective-permute-start.6
  38.8 1.0 %collective-permute-done.6 = f32[160,128]{1,0:T(8,128)S(1)} collective-permute-done((f32[160,128]{1,0:T(8,128)S(1)}, f32[160,128]{1,0:T(8,128)S(1)}, u32[]{:S(2)}, u32[]{:S(2)}) %collective-permute-start.6) | collective-permute-done | bytes 81952 | tf_op jit(solution)/shard_map/ppermute | solution.py:310
  39.8 1.6 %collective-permute-start.7 = (f32[160,128]{1,0:T(8,128)S(1)}, f32[160,128]{1,0:T(8,128)S(1)}, u32[]{:S(2)}, u32[]{:S(2)}) collective-permute-start(f32[160,128]{1,0:T(8,128)S(1)} %add.12), channel_id=1, source_target_pairs={{0,2},{1,3},{2,0},{3,1},{4,6},{5,7},{6,4},{7,5},{8,10},{9,11},{10,... | collective-permute-start | bytes 245768 | tf_op jit(solution)/shard_map/ppermute | solution.py:310
  41.4 3.1 %collective-permute-done.7 = f32[160,128]{1,0:T(8,128)S(1)} collective-permute-done((f32[160,128]{1,0:T(8,128)S(1)}, f32[160,128]{1,0:T(8,128)S(1)}, u32[]{:S(2)}, u32[]{:S(2)}) %collective-permute-start.7) | collective-permute-done | bytes 81952 | tf_op jit(solution)/shard_map/ppermute | solution.py:310
  44.5 2.7 %collective-permute-start.8 = (f32[160,128]{1,0:T(8,128)S(1)}, f32[160,128]{1,0:T(8,128)S(1)}, u32[]{:S(2)}, u32[]{:S(2)}) collective-permute-start(f32[160,128]{1,0:T(8,128)S(1)} %add.13), channel_id=1, source_target_pairs={{0,4},{1,5},{2,6},{3,7},{4,0},{5,1},{6,2},{7,3},{8,12},{9,13},{10,... | collective-permute-start | bytes 245768 | tf_op jit(solution)/shard_map/ppermute | solution.py:310
  47.2 2.4 %collective-permute-done.8 = f32[160,128]{1,0:T(8,128)S(1)} collective-permute-done((f32[160,128]{1,0:T(8,128)S(1)}, f32[160,128]{1,0:T(8,128)S(1)}, u32[]{:S(2)}, u32[]{:S(2)}) %collective-permute-start.8) | collective-permute-done | bytes 81952 | tf_op jit(solution)/shard_map/ppermute | solution.py:310
  49.7 3.0 %collective-permute-start.9 = (f32[160,128]{1,0:T(8,128)S(1)}, f32[160,128]{1,0:T(8,128)S(1)}, u32[]{:S(2)}, u32[]{:S(2)}) collective-permute-start(f32[160,128]{1,0:T(8,128)S(1)} %add.14), channel_id=1, source_target_pairs={{0,8},{1,9},{2,10},{3,11},{4,12},{5,13},{6,14},{7,15},{8,0},{9,1},... | collective-permute-start | bytes 245768 | tf_op jit(solution)/shard_map/ppermute | solution.py:310
  52.7 2.4 %collective-permute-done.9 = f32[160,128]{1,0:T(8,128)S(1)} collective-permute-done((f32[160,128]{1,0:T(8,128)S(1)}, f32[160,128]{1,0:T(8,128)S(1)}, u32[]{:S(2)}, u32[]{:S(2)}) %collective-permute-start.9) | collective-permute-done | bytes 81952 | tf_op jit(solution)/shard_map/ppermute | solution.py:310
  55.2 1.3 %collective-permute-done.10.other = f32[160,128]{1,0:T(8,128)S(1)} collective-permute-done((f32[160,128]{1,0:T(8,128)S(1)}, f32[160,128]{1,0:T(8,128)S(1)}, u32[]{:S(2)}, u32[]{:S(2)}) %collective-permute-start.10) | collective-permute-done | bytes 81952 | tf_op jit(solution)/shard_map/ppermute | solution.py:310
  56.4 0.9 %shard_map.90 = (f32[16,16]{1,0:T(8,128)}, f32[128,128]{1,0:T(8,128)}, f32[128,128]{1,0:T(8,128)}, f32[128,128]{1,0:T(8,128)}) custom-call(f32[160,128]{1,0:T(8,128)S(1)} %add.15.mine, f32[160,128]{1,0:T(8,128)S(1)} %collective-permute-done.10.other), custom_call_target="tpu_custom_call" | custom-call | tf_op jit(solution)/shard_map/pallas_call | solution.py:378
  (21 shorter events, 0.3 us)
Async XLA Ops:
  0.6 8.8 %copy-start = (bf16[1,128,128,128]{3,2,1,0:T(8,128)(2,1)S(1)}, bf16[1,128,128,128]{3,2,1,0:T(8,128)(2,1)}, u32[]{:S(2)}) copy-start(bf16[1,128,128,128]{3,2,1,0:T(8,128)(2,1)} %param.5) | copy-start | bytes 12582916
  0.6 8.7 %copy-start.1 = (bf16[128,64]{0,1:T(8,128)(2,1)S(1)}, bf16[128,64]{0,1:T(8,128)(2,1)}, u32[]{:S(2)}) copy-start(bf16[128,64]{0,1:T(8,128)(2,1)} %param.8) | copy-start | bytes 49156
  0.7 8.7 %copy-start.2 = (bf16[128,64]{0,1:T(8,128)(2,1)S(1)}, bf16[128,64]{0,1:T(8,128)(2,1)}, u32[]{:S(2)}) copy-start(bf16[128,64]{0,1:T(8,128)(2,1)} %param.9) | copy-start | bytes 49156
  0.7 8.7 %copy-start.3 = (bf16[128,8]{0,1:T(8,128)(2,1)S(1)}, bf16[128,8]{0,1:T(8,128)(2,1)}, u32[]{:S(2)}) copy-start(bf16[128,8]{0,1:T(8,128)(2,1)} %param.7) | copy-start | bytes 6148
  3.9 14.7 %collective-permute-start.1 = (bf16[4,128,128]{2,1,0:T(8,128)(2,1)}, bf16[4,128,128]{2,1,0:T(8,128)(2,1)S(1)}, u32[]{:S(2)}, u32[]{:S(2)}) collective-permute-start(bf16[4,128,128]{2,1,0:T(8,128)(2,1)} %get-tuple-element.25), channel_id=1, source_target_pairs={{0,8},{1,9},{2,10},{3,11},{4,12},{5,13},{6,14},{7,15},{8,0},{9,1},... | collective-permute-start | bytes 393224 | tf_op jit(solution)/shard_map/ppermute | solution.py:310
  8.0 10.6 %collective-permute-start.2 = (bf16[4,128,128]{2,1,0:T(8,128)(2,1)}, bf16[4,128,128]{2,1,0:T(8,128)(2,1)S(1)}, u32[]{:S(2)}, u32[]{:S(2)}) collective-permute-start(bf16[4,128,128]{2,1,0:T(8,128)(2,1)} %get-tuple-element.26), channel_id=1, source_target_pairs={{0,12},{1,13},{2,14},{3,15},{4,8},{5,9},{6,10},{7,11},{8,4},{9,5},... | collective-permute-start | bytes 393224 | tf_op jit(solution)/shard_map/ppermute | solution.py:310
  13.0 7.1 %collective-permute-start = (bf16[4,128,128]{2,1,0:T(8,128)(2,1)S(1)}, bf16[4,128,128]{2,1,0:T(8,128)(2,1)S(1)}, u32[]{:S(2)}, u32[]{:S(2)}) collective-permute-start(bf16[4,128,128]{2,1,0:T(8,128)(2,1)S(1)} %get-tuple-element.24), channel_id=1, source_target_pairs={{0,4},{1,5},{2,6},{3,7},{4,0},{5,1},{6,2},{7,3},{8,12},{9,13},{10,... | collective-permute-start | bytes 393224 | tf_op jit(solution)/shard_map/ppermute | solution.py:310
  13.4 24.0 %all-to-all-start = ((bf16[16,192,128]{2,1,0:T(8,128)(2,1)}), bf16[16,192,128]{2,1,0:T(8,128)(2,1)S(1)}, u32[]{:S(2)}, u32[]{:S(2)}) async-start(bf16[16,192,128]{2,1,0:T(8,128)(2,1)} %get-tuple-element.39), calls=%async_computation | async-start | bytes 1572864 | tf_op jit(solution)/shard_map/all_to_all | solution.py:355
  18.6 14.6 %copy-start.4 = (bf16[16,8]{0,1:T(8,128)(2,1)S(1)}, bf16[16,8]{0,1:T(8,128)(2,1)}, u32[]{:S(2)}) copy-start(bf16[16,8]{0,1:T(8,128)(2,1)} %param.6) | copy-start | bytes 772
  20.2 1.9 %collective-permute-start.3 = (bf16[4,128,128]{2,1,0:T(8,128)(2,1)S(1)}, bf16[4,128,128]{2,1,0:T(8,128)(2,1)S(1)}, u32[]{:S(2)}, u32[]{:S(2)}) collective-permute-start(bf16[4,128,128]{2,1,0:T(8,128)(2,1)S(1)} %get-tuple-element.32), channel_id=1, source_target_pairs={{0,1},{1,0},{2,3},{3,2},{4,5},{5,4},{6,7},{7,6},{8,9},{9,8},{10,11... | collective-permute-start | bytes 393224 | tf_op jit(solution)/shard_map/ppermute | solution.py:310
  20.3 10.9 %collective-permute-start.4 = (bf16[4,128,128]{2,1,0:T(8,128)(2,1)S(1)}, bf16[4,128,128]{2,1,0:T(8,128)(2,1)S(1)}, u32[]{:S(2)}, u32[]{:S(2)}) collective-permute-start(bf16[4,128,128]{2,1,0:T(8,128)(2,1)S(1)} %get-tuple-element.33), channel_id=1, source_target_pairs={{0,2},{1,3},{2,0},{3,1},{4,6},{5,7},{6,4},{7,5},{8,10},{9,11},{10,... | collective-permute-start | bytes 393224 | tf_op jit(solution)/shard_map/ppermute | solution.py:310
  21.9 11.3 %collective-permute-start.5 = (bf16[4,128,128]{2,1,0:T(8,128)(2,1)S(1)}, bf16[4,128,128]{2,1,0:T(8,128)(2,1)S(1)}, u32[]{:S(2)}, u32[]{:S(2)}) collective-permute-start(bf16[4,128,128]{2,1,0:T(8,128)(2,1)S(1)} %get-tuple-element.34), channel_id=1, source_target_pairs={{0,3},{1,2},{2,1},{3,0},{4,7},{5,6},{6,5},{7,4},{8,11},{9,10},{10,... | collective-permute-start | bytes 393224 | tf_op jit(solution)/shard_map/ppermute | solution.py:310
  38.5 1.3 %collective-permute-start.6 = (f32[160,128]{1,0:T(8,128)S(1)}, f32[160,128]{1,0:T(8,128)S(1)}, u32[]{:S(2)}, u32[]{:S(2)}) collective-permute-start(f32[160,128]{1,0:T(8,128)S(1)} %get-tuple-element.41), channel_id=1, source_target_pairs={{0,1},{1,0},{2,3},{3,2},{4,5},{5,4},{6,7},{7,6},{8,9},{9,8},{10,11... | collective-permute-start | bytes 245768 | tf_op jit(solution)/shard_map/ppermute | solution.py:310
  39.8 4.7 %collective-permute-start.7 = (f32[160,128]{1,0:T(8,128)S(1)}, f32[160,128]{1,0:T(8,128)S(1)}, u32[]{:S(2)}, u32[]{:S(2)}) collective-permute-start(f32[160,128]{1,0:T(8,128)S(1)} %add.12), channel_id=1, source_target_pairs={{0,2},{1,3},{2,0},{3,1},{4,6},{5,7},{6,4},{7,5},{8,10},{9,11},{10,... | collective-permute-start | bytes 245768 | tf_op jit(solution)/shard_map/ppermute | solution.py:310
  44.5 5.2 %collective-permute-start.8 = (f32[160,128]{1,0:T(8,128)S(1)}, f32[160,128]{1,0:T(8,128)S(1)}, u32[]{:S(2)}, u32[]{:S(2)}) collective-permute-start(f32[160,128]{1,0:T(8,128)S(1)} %add.13), channel_id=1, source_target_pairs={{0,4},{1,5},{2,6},{3,7},{4,0},{5,1},{6,2},{7,3},{8,12},{9,13},{10,... | collective-permute-start | bytes 245768 | tf_op jit(solution)/shard_map/ppermute | solution.py:310
  49.7 5.4 %collective-permute-start.9 = (f32[160,128]{1,0:T(8,128)S(1)}, f32[160,128]{1,0:T(8,128)S(1)}, u32[]{:S(2)}, u32[]{:S(2)}) collective-permute-start(f32[160,128]{1,0:T(8,128)S(1)} %add.14), channel_id=1, source_target_pairs={{0,8},{1,9},{2,10},{3,11},{4,12},{5,13},{6,14},{7,15},{8,0},{9,1},... | collective-permute-start | bytes 245768 | tf_op jit(solution)/shard_map/ppermute | solution.py:310
  55.1 1.3 %collective-permute-start.10 = (f32[160,128]{1,0:T(8,128)S(1)}, f32[160,128]{1,0:T(8,128)S(1)}, u32[]{:S(2)}, u32[]{:S(2)}) collective-permute-start(f32[160,128]{1,0:T(8,128)S(1)} %add.15.mine), channel_id=1, source_target_pairs={{0,1},{1,0},{2,3},{3,2},{4,5},{5,4},{6,7},{7,6},{8,9},{9,8},{10,11... | collective-permute-start | bytes 245768 | tf_op jit(solution)/shard_map/ppermute | solution.py:310

commit v4 on v3

--- a/solution.py
+++ b/solution.py
@@ -41,10 +41,10 @@
 
 
 def early_cubes(early, own, base, slab, dt_in, vt_in, *refs):
-    *outs, dt, vt, images, right, far, arrived, ready, sent = refs
+    *far, dt, vt, images, right, arrived, ready = refs
     pixels = slab.shape[1]
-    plane = outs[0].shape[0]
-    rank = own * plane * len(outs)
+    plane = far[0].shape[0]
+    rank = own * plane * len(far)
     pitch = early + 1
     cuts = [0, early // 2, early]
     copies = [
@@ -66,14 +66,8 @@
                     right[pl.ds(c + 2 * i + j, rank, stride=pitch), :] = rights[
                         j * rank : (j + 1) * rank, i * pixels : (i + 1) * pixels
                     ]
-    copies = []
-    for slot in range(plane * len(outs)):
-        slot_cubes(slot, early, pitch, own, right, dd, far.at[slot])
-        out = outs[slot // plane].at[slot % plane]
-        copies.append(pltpu.make_async_copy(far.at[slot], out, sent.at[slot]))
-        copies[-1].start()
-    for copy in copies:
-        copy.wait()
+    for slot in range(plane * len(far)):
+        slot_cubes(slot, early, pitch, own, right, dd, far[slot // plane].at[slot % plane])
 
 
 def slot_order(factor, own, base, count):
@@ -147,18 +141,16 @@
     part = [jax.ShapeDtypeStruct((plane, own // 2 * early, pixels), BF16)] * half
     far = pl.pallas_call(
         functools.partial(early_cubes, early, own, n // 2),
-        out_shape=part,
+        out_shape=[pltpu.VMEM(part[0].shape, BF16)] * half,
         in_specs=[anywhere] * 3,
-        out_specs=[anywhere] * half,
+        out_specs=[in_vmem] * half,
         scratch_shapes=[
             pltpu.VMEM(dt.shape, BF16),
             pltpu.VMEM(vt.shape, BF16),
             pltpu.VMEM((early,) + slab.shape[1:], BF16),
             pltpu.VMEM((rank // 2 * (early + 1), pixels), F32),
-            pltpu.VMEM((n // 2, own // 2 * early, pixels), BF16),
             pltpu.SemaphoreType.DMA((2,)),
             pltpu.SemaphoreType.DMA((2,)),
-            pltpu.SemaphoreType.DMA((n // 2,)),
         ],
         compiler_params=params,
     )(slab, dt, vt)

time: 57.5 us -> 56.9 us (0.990)
  Pallas kernels: 9.77 us -> 9.09 us
    pallas_call x1, Pallas kernels: 3.25 us -> 2.58 us  [projections(): pl.pallas_call(functools.partial(early_cubes, early, own, n // 2), out_sh...]
where the time goes in v4:
time: 56.9 us; the launch traced here: 56.7 us
  waiting for transfers between devices  26.1 us (46%)
  starting transfers between devices  20.7 us (36%)
  Pallas kernels  9.09 us (16%)
  between operations  0.78 us (1%)
    ppermute x11, waiting for transfers between devices, swap(): return lax.ppermute(x, 'row', [(i, i ^ step) for i in range(n)])  22.8 us
    ppermute x11, starting transfers between devices, swap(): return lax.ppermute(x, 'row', [(i, i ^ step) for i in range(n)])  15.4 us
    all_to_all x1, starting transfers between devices, local(): lax.all_to_all(second, 'row', split_axis=0, concat_axis=0, tiled=True)  5.24 us
    pallas_call x1, Pallas kernels, projections(): pl.pallas_call(functools.partial(late_cubes, early, own), out_shape=part...  3.64 us
    all_to_all x1, waiting for transfers between devices, local(): lax.all_to_all(second, 'row', split_axis=0, concat_axis=0, tiled=True)  3.31 us
    pallas_call x1, Pallas kernels, projections(): pl.pallas_call(functools.partial(early_cubes, early, own, n // 2), out_sh...  2.58 us
    pallas_call x4, Pallas kernels, call(): pl.pallas_call(kernel, out_shape=[jax.ShapeDtypeStruct(*out) for out in o...  1.98 us
  transfers between devices with their start and end apart: 12, of which 9 were waited for; matrix products, arithmetic and copies ran while one was open for 0% of the time, Pallas kernels for 8%

profile of v4, /device:TPU:0, one launch (start us, length us, event | category | flops | bytes accessed | tf_op | source)
XLA Modules:
  0.0 56.7 jit_solution(4064878466779029628)
XLA Ops:
  0.7 2.6 %shard_map.85 = (bf16[4,128,128]{2,1,0:T(8,128)(2,1)S(1)}, bf16[4,128,128]{2,1,0:T(8,128)(2,1)S(1)}) custom-call(bf16[128,128,128]{2,1,0:T(8,128)(2,1)} %bitcast.5, bf16[64,128]{1,0:T(8,128)(2,1)} %bitcast.7, bf16[64,128]{1,0:T(8,128)(2,1)} %bitcast.9), custom_call_target="tpu_custom_call" | custom-call | tf_op jit(solution)/shard_map/pallas_call | solution.py:142
  3.3 4.1 %collective-permute-start.1 = (bf16[4,128,128]{2,1,0:T(8,128)(2,1)S(1)}, bf16[4,128,128]{2,1,0:T(8,128)(2,1)S(1)}, u32[]{:S(2)}, u32[]{:S(2)}) collective-permute-start(bf16[4,128,128]{2,1,0:T(8,128)(2,1)S(1)} %get-tuple-element.25), channel_id=1, source_target_pairs={{0,8},{1,9},{2,10},{3,11},{4,12},{5,13},{6,14},{7,15},{8,0},{9,1},... | collective-permute-start | bytes 393224 | tf_op jit(solution)/shard_map/ppermute | solution.py:302
  7.4 1.3 %collective-permute-start.2 = (bf16[4,128,128]{2,1,0:T(8,128)(2,1)S(1)}, bf16[4,128,128]{2,1,0:T(8,128)(2,1)S(1)}, u32[]{:S(2)}, u32[]{:S(2)}) collective-permute-start(bf16[4,128,128]{2,1,0:T(8,128)(2,1)S(1)} %get-tuple-element.26), channel_id=1, source_target_pairs={{0,12},{1,13},{2,14},{3,15},{4,8},{5,9},{6,10},{7,11},{8,4},{9,5},... | collective-permute-start | bytes 393224 | tf_op jit(solution)/shard_map/ppermute | solution.py:302
  8.7 3.6 %shard_map.84 = (bf16[4,128,128]{2,1,0:T(8,128)(2,1)S(1)}, bf16[4,128,128]{2,1,0:T(8,128)(2,1)S(1)}, bf16[16,192,128]{2,1,0:T(8,128)(2,1)}) custom-call(bf16[128,128,128]{2,1,0:T(8,128)(2,1)S(1)} %bitcast.6, bf16[8,128]{1,0:T(8,128)(2,1)S(1)} %bitcast.11, bf16[64,128]{1,0:T(8,128)(2,1)S(1)} %bitcast.8, bf16[64,128]{1,0:T(8,128)(2,1)S(1)} %bitcast.10), custom_call_target="tpu_custom_call" | custom-call | tf_op jit(solution)/shard_map/pallas_call | solution.py:158
  12.4 0.3 collective-permute-start
  12.7 5.2 %all-to-all-start = ((bf16[16,192,128]{2,1,0:T(8,128)(2,1)}), bf16[16,192,128]{2,1,0:T(8,128)(2,1)S(1)}, u32[]{:S(2)}, u32[]{:S(2)}) async-start(bf16[16,192,128]{2,1,0:T(8,128)(2,1)} %get-tuple-element.39), calls=%async_computation | async-start | bytes 1572864 | tf_op jit(solution)/shard_map/all_to_all | solution.py:347
  18.0 1.3 %collective-permute-done.refs_1_ = bf16[4,128,128]{2,1,0:T(8,128)(2,1)S(1)} collective-permute-done((bf16[4,128,128]{2,1,0:T(8,128)(2,1)S(1)}, bf16[4,128,128]{2,1,0:T(8,128)(2,1)S(1)}, u32[]{:S(2)}, u32[]{:S(2)}) %collective-permute-start) | collective-permute-done | bytes 131104 | tf_op jit(solution)/shard_map/ppermute | solution.py:302
  19.4 1.6 %collective-permute-start.4 = (bf16[4,128,128]{2,1,0:T(8,128)(2,1)S(1)}, bf16[4,128,128]{2,1,0:T(8,128)(2,1)S(1)}, u32[]{:S(2)}, u32[]{:S(2)}) collective-permute-start(bf16[4,128,128]{2,1,0:T(8,128)(2,1)S(1)} %get-tuple-element.33), channel_id=1, source_target_pairs={{0,2},{1,3},{2,0},{3,1},{4,6},{5,7},{6,4},{7,5},{8,10},{9,11},{10,... | collective-permute-start | bytes 393224 | tf_op jit(solution)/shard_map/ppermute | solution.py:302
  21.0 0.2 collective-permute-start.5
  21.3 9.3 %collective-permute-done.4.refs_2_ = bf16[4,128,128]{2,1,0:T(8,128)(2,1)S(1)} collective-permute-done((bf16[4,128,128]{2,1,0:T(8,128)(2,1)S(1)}, bf16[4,128,128]{2,1,0:T(8,128)(2,1)S(1)}, u32[]{:S(2)}, u32[]{:S(2)}) %collective-permute-start.4) | collective-permute-done | bytes 131104 | tf_op jit(solution)/shard_map/ppermute | solution.py:302
  30.5 2.0 %collective-permute-done.5.refs_3_ = bf16[4,128,128]{2,1,0:T(8,128)(2,1)S(1)} collective-permute-done((bf16[4,128,128]{2,1,0:T(8,128)(2,1)S(1)}, bf16[4,128,128]{2,1,0:T(8,128)(2,1)S(1)}, u32[]{:S(2)}, u32[]{:S(2)}) %collective-permute-start.5) | collective-permute-done | bytes 131104 | tf_op jit(solution)/shard_map/ppermute | solution.py:302
  32.5 0.8 %shard_map.88 = (bf16[128,256]{1,0:T(8,128)(2,1)S(1)}, bf16[8,64,256]{2,1,0:T(8,128)(2,1)S(1)}, f32[2,128,128]{2,1,0:T(8,128)S(1)}, f32[64,64]{1,0:T(8,128)S(1)}) custom-call(bf16[8,16]{1,0:T(8,128)(2,1)S(1)} %bitcast.14, bf16[8,128]{1,0:T(8,128)(2,1)S(1)} %bitcast.12, bf16[4,128,128]{2,1,0:T(8,128)(2,1)S(1)} %get-tuple-element.31.refs_0_, ...), custom_call_target="tpu_custom_call" | custom-call | flops 100000000 | bytes 1048576 | tf_op jit(solution)/shard_map/pallas_call | solution.py:292
  33.3 3.3 %all-to-all-done.second = bf16[16,192,128]{2,1,0:T(8,128)(2,1)S(1)} async-done(((bf16[16,192,128]{2,1,0:T(8,128)(2,1)}), bf16[16,192,128]{2,1,0:T(8,128)(2,1)S(1)}, u32[]{:S(2)}, u32[]{:S(2)}) %all-to-all-start) | async-done | bytes 786464 | tf_op jit(solution)/shard_map/all_to_all | solution.py:347
  36.7 1.1 %shard_map.89 = (f32[160,128]{1,0:T(8,128)S(1)}, f32[160,128]{1,0:T(8,128)S(1)}) custom-call(bf16[8,128]{1,0:T(8,128)(2,1)S(1)} %bitcast.13, bf16[128,256]{1,0:T(8,128)(2,1)S(1)} %get-tuple-element.35.plain, bf16[8,64,256]{2,1,0:T(8,128)(2,1)S(1)} %get-tuple-element.36.early_unfold, f32[2,128,128]{2,1,0:T(8,128)S(1)} %get-tuple-element.37.rowpart, ...), custom_call_target="tpu_custom_call" | custom-call | flops 100000000 | bytes 1048576 | tf_op jit(solution)/shard_map/pallas_call | solution.py:292
  37.8 0.3 collective-permute-start.6
  38.1 1.0 %collective-permute-done.6 = f32[160,128]{1,0:T(8,128)S(1)} collective-permute-done((f32[160,128]{1,0:T(8,128)S(1)}, f32[160,128]{1,0:T(8,128)S(1)}, u32[]{:S(2)}, u32[]{:S(2)}) %collective-permute-start.6) | collective-permute-done | bytes 81952 | tf_op jit(solution)/shard_map/ppermute | solution.py:302
  39.1 1.6 %collective-permute-start.7 = (f32[160,128]{1,0:T(8,128)S(1)}, f32[160,128]{1,0:T(8,128)S(1)}, u32[]{:S(2)}, u32[]{:S(2)}) collective-permute-start(f32[160,128]{1,0:T(8,128)S(1)} %add.12), channel_id=1, source_target_pairs={{0,2},{1,3},{2,0},{3,1},{4,6},{5,7},{6,4},{7,5},{8,10},{9,11},{10,... | collective-permute-start | bytes 245768 | tf_op jit(solution)/shard_map/ppermute | solution.py:302
  40.7 3.1 %collective-permute-done.7 = f32[160,128]{1,0:T(8,128)S(1)} collective-permute-done((f32[160,128]{1,0:T(8,128)S(1)}, f32[160,128]{1,0:T(8,128)S(1)}, u32[]{:S(2)}, u32[]{:S(2)}) %collective-permute-start.7) | collective-permute-done | bytes 81952 | tf_op jit(solution)/shard_map/ppermute | solution.py:302
  43.8 2.7 %collective-permute-start.8 = (f32[160,128]{1,0:T(8,128)S(1)}, f32[160,128]{1,0:T(8,128)S(1)}, u32[]{:S(2)}, u32[]{:S(2)}) collective-permute-start(f32[160,128]{1,0:T(8,128)S(1)} %add.13), channel_id=1, source_target_pairs={{0,4},{1,5},{2,6},{3,7},{4,0},{5,1},{6,2},{7,3},{8,12},{9,13},{10,... | collective-permute-start | bytes 245768 | tf_op jit(solution)/shard_map/ppermute | solution.py:302
  46.6 2.4 %collective-permute-done.8 = f32[160,128]{1,0:T(8,128)S(1)} collective-permute-done((f32[160,128]{1,0:T(8,128)S(1)}, f32[160,128]{1,0:T(8,128)S(1)}, u32[]{:S(2)}, u32[]{:S(2)}) %collective-permute-start.8) | collective-permute-done | bytes 81952 | tf_op jit(solution)/shard_map/ppermute | solution.py:302
  49.0 3.0 %collective-permute-start.9 = (f32[160,128]{1,0:T(8,128)S(1)}, f32[160,128]{1,0:T(8,128)S(1)}, u32[]{:S(2)}, u32[]{:S(2)}) collective-permute-start(f32[160,128]{1,0:T(8,128)S(1)} %add.14), channel_id=1, source_target_pairs={{0,8},{1,9},{2,10},{3,11},{4,12},{5,13},{6,14},{7,15},{8,0},{9,1},... | collective-permute-start | bytes 245768 | tf_op jit(solution)/shard_map/ppermute | solution.py:302
  52.0 2.4 %collective-permute-done.9 = f32[160,128]{1,0:T(8,128)S(1)} collective-permute-done((f32[160,128]{1,0:T(8,128)S(1)}, f32[160,128]{1,0:T(8,128)S(1)}, u32[]{:S(2)}, u32[]{:S(2)}) %collective-permute-start.9) | collective-permute-done | bytes 81952 | tf_op jit(solution)/shard_map/ppermute | solution.py:302
  54.5 1.3 %collective-permute-done.10.other = f32[160,128]{1,0:T(8,128)S(1)} collective-permute-done((f32[160,128]{1,0:T(8,128)S(1)}, f32[160,128]{1,0:T(8,128)S(1)}, u32[]{:S(2)}, u32[]{:S(2)}) %collective-permute-start.10) | collective-permute-done | bytes 81952 | tf_op jit(solution)/shard_map/ppermute | solution.py:302
  55.8 0.9 %shard_map.90 = (f32[16,16]{1,0:T(8,128)}, f32[128,128]{1,0:T(8,128)}, f32[128,128]{1,0:T(8,128)}, f32[128,128]{1,0:T(8,128)}) custom-call(f32[160,128]{1,0:T(8,128)S(1)} %add.15.mine, f32[160,128]{1,0:T(8,128)S(1)} %collective-permute-done.10.other), custom_call_target="tpu_custom_call" | custom-call | tf_op jit(solution)/shard_map/pallas_call | solution.py:370
  (21 shorter events, 0.3 us)
Async XLA Ops:
  0.6 8.1 %copy-start = (bf16[1,128,128,128]{3,2,1,0:T(8,128)(2,1)S(1)}, bf16[1,128,128,128]{3,2,1,0:T(8,128)(2,1)}, u32[]{:S(2)}) copy-start(bf16[1,128,128,128]{3,2,1,0:T(8,128)(2,1)} %param.5) | copy-start | bytes 12582916
  0.6 8.1 %copy-start.1 = (bf16[128,64]{0,1:T(8,128)(2,1)S(1)}, bf16[128,64]{0,1:T(8,128)(2,1)}, u32[]{:S(2)}) copy-start(bf16[128,64]{0,1:T(8,128)(2,1)} %param.8) | copy-start | bytes 49156
  0.7 8.1 %copy-start.2 = (bf16[128,64]{0,1:T(8,128)(2,1)S(1)}, bf16[128,64]{0,1:T(8,128)(2,1)}, u32[]{:S(2)}) copy-start(bf16[128,64]{0,1:T(8,128)(2,1)} %param.9) | copy-start | bytes 49156
  0.7 8.1 %copy-start.3 = (bf16[128,8]{0,1:T(8,128)(2,1)S(1)}, bf16[128,8]{0,1:T(8,128)(2,1)}, u32[]{:S(2)}) copy-start(bf16[128,8]{0,1:T(8,128)(2,1)} %param.7) | copy-start | bytes 6148
  3.3 14.7 %collective-permute-start.1 = (bf16[4,128,128]{2,1,0:T(8,128)(2,1)S(1)}, bf16[4,128,128]{2,1,0:T(8,128)(2,1)S(1)}, u32[]{:S(2)}, u32[]{:S(2)}) collective-permute-start(bf16[4,128,128]{2,1,0:T(8,128)(2,1)S(1)} %get-tuple-element.25), channel_id=1, source_target_pairs={{0,8},{1,9},{2,10},{3,11},{4,12},{5,13},{6,14},{7,15},{8,0},{9,1},... | collective-permute-start | bytes 393224 | tf_op jit(solution)/shard_map/ppermute | solution.py:302
  7.4 10.6 %collective-permute-start.2 = (bf16[4,128,128]{2,1,0:T(8,128)(2,1)S(1)}, bf16[4,128,128]{2,1,0:T(8,128)(2,1)S(1)}, u32[]{:S(2)}, u32[]{:S(2)}) collective-permute-start(bf16[4,128,128]{2,1,0:T(8,128)(2,1)S(1)} %get-tuple-element.26), channel_id=1, source_target_pairs={{0,12},{1,13},{2,14},{3,15},{4,8},{5,9},{6,10},{7,11},{8,4},{9,5},... | collective-permute-start | bytes 393224 | tf_op jit(solution)/shard_map/ppermute | solution.py:302
  12.4 6.9 %collective-permute-start = (bf16[4,128,128]{2,1,0:T(8,128)(2,1)S(1)}, bf16[4,128,128]{2,1,0:T(8,128)(2,1)S(1)}, u32[]{:S(2)}, u32[]{:S(2)}) collective-permute-start(bf16[4,128,128]{2,1,0:T(8,128)(2,1)S(1)} %get-tuple-element.24), channel_id=1, source_target_pairs={{0,4},{1,5},{2,6},{3,7},{4,0},{5,1},{6,2},{7,3},{8,12},{9,13},{10,... | collective-permute-start | bytes 393224 | tf_op jit(solution)/shard_map/ppermute | solution.py:302
  12.7 24.0 %all-to-all-start = ((bf16[16,192,128]{2,1,0:T(8,128)(2,1)}), bf16[16,192,128]{2,1,0:T(8,128)(2,1)S(1)}, u32[]{:S(2)}, u32[]{:S(2)}) async-start(bf16[16,192,128]{2,1,0:T(8,128)(2,1)} %get-tuple-element.39), calls=%async_computation | async-start | bytes 1572864 | tf_op jit(solution)/shard_map/all_to_all | solution.py:347
  17.9 14.6 %copy-start.4 = (bf16[16,8]{0,1:T(8,128)(2,1)S(1)}, bf16[16,8]{0,1:T(8,128)(2,1)}, u32[]{:S(2)}) copy-start(bf16[16,8]{0,1:T(8,128)(2,1)} %param.6) | copy-start | bytes 772
  19.3 1.9 %collective-permute-start.3 = (bf16[4,128,128]{2,1,0:T(8,128)(2,1)S(1)}, bf16[4,128,128]{2,1,0:T(8,128)(2,1)S(1)}, u32[]{:S(2)}, u32[]{:S(2)}) collective-permute-start(bf16[4,128,128]{2,1,0:T(8,128)(2,1)S(1)} %get-tuple-element.32), channel_id=1, source_target_pairs={{0,1},{1,0},{2,3},{3,2},{4,5},{5,4},{6,7},{7,6},{8,9},{9,8},{10,11... | collective-permute-start | bytes 393224 | tf_op jit(solution)/shard_map/ppermute | solution.py:302
  19.4 11.1 %collective-permute-start.4 = (bf16[4,128,128]{2,1,0:T(8,128)(2,1)S(1)}, bf16[4,128,128]{2,1,0:T(8,128)(2,1)S(1)}, u32[]{:S(2)}, u32[]{:S(2)}) collective-permute-start(bf16[4,128,128]{2,1,0:T(8,128)(2,1)S(1)} %get-tuple-element.33), channel_id=1, source_target_pairs={{0,2},{1,3},{2,0},{3,1},{4,6},{5,7},{6,4},{7,5},{8,10},{9,11},{10,... | collective-permute-start | bytes 393224 | tf_op jit(solution)/shard_map/ppermute | solution.py:302
  21.0 11.5 %collective-permute-start.5 = (bf16[4,128,128]{2,1,0:T(8,128)(2,1)S(1)}, bf16[4,128,128]{2,1,0:T(8,128)(2,1)S(1)}, u32[]{:S(2)}, u32[]{:S(2)}) collective-permute-start(bf16[4,128,128]{2,1,0:T(8,128)(2,1)S(1)} %get-tuple-element.34), channel_id=1, source_target_pairs={{0,3},{1,2},{2,1},{3,0},{4,7},{5,6},{6,5},{7,4},{8,11},{9,10},{10,... | collective-permute-start | bytes 393224 | tf_op jit(solution)/shard_map/ppermute | solution.py:302
  37.8 1.3 %collective-permute-start.6 = (f32[160,128]{1,0:T(8,128)S(1)}, f32[160,128]{1,0:T(8,128)S(1)}, u32[]{:S(2)}, u32[]{:S(2)}) collective-permute-start(f32[160,128]{1,0:T(8,128)S(1)} %get-tuple-element.41), channel_id=1, source_target_pairs={{0,1},{1,0},{2,3},{3,2},{4,5},{5,4},{6,7},{7,6},{8,9},{9,8},{10,11... | collective-permute-start | bytes 245768 | tf_op jit(solution)/shard_map/ppermute | solution.py:302
  39.1 4.7 %collective-permute-start.7 = (f32[160,128]{1,0:T(8,128)S(1)}, f32[160,128]{1,0:T(8,128)S(1)}, u32[]{:S(2)}, u32[]{:S(2)}) collective-permute-start(f32[160,128]{1,0:T(8,128)S(1)} %add.12), channel_id=1, source_target_pairs={{0,2},{1,3},{2,0},{3,1},{4,6},{5,7},{6,4},{7,5},{8,10},{9,11},{10,... | collective-permute-start | bytes 245768 | tf_op jit(solution)/shard_map/ppermute | solution.py:302
  43.8 5.2 %collective-permute-start.8 = (f32[160,128]{1,0:T(8,128)S(1)}, f32[160,128]{1,0:T(8,128)S(1)}, u32[]{:S(2)}, u32[]{:S(2)}) collective-permute-start(f32[160,128]{1,0:T(8,128)S(1)} %add.13), channel_id=1, source_target_pairs={{0,4},{1,5},{2,6},{3,7},{4,0},{5,1},{6,2},{7,3},{8,12},{9,13},{10,... | collective-permute-start | bytes 245768 | tf_op jit(solution)/shard_map/ppermute | solution.py:302
  49.0 5.4 %collective-permute-start.9 = (f32[160,128]{1,0:T(8,128)S(1)}, f32[160,128]{1,0:T(8,128)S(1)}, u32[]{:S(2)}, u32[]{:S(2)}) collective-permute-start(f32[160,128]{1,0:T(8,128)S(1)} %add.14), channel_id=1, source_target_pairs={{0,8},{1,9},{2,10},{3,11},{4,12},{5,13},{6,14},{7,15},{8,0},{9,1},... | collective-permute-start | bytes 245768 | tf_op jit(solution)/shard_map/ppermute | solution.py:302
  54.4 1.3 %collective-permute-start.10 = (f32[160,128]{1,0:T(8,128)S(1)}, f32[160,128]{1,0:T(8,128)S(1)}, u32[]{:S(2)}, u32[]{:S(2)}) collective-permute-start(f32[160,128]{1,0:T(8,128)S(1)} %add.15.mine), channel_id=1, source_target_pairs={{0,1},{1,0},{2,3},{3,2},{4,5},{5,4},{6,7},{7,6},{8,9},{9,8},{10,11... | collective-permute-start | bytes 245768 | tf_op jit(solution)/shard_map/ppermute | solution.py:302

commit v5 on v4

--- a/solution.py
+++ b/solution.py
@@ -235,8 +235,7 @@
     for i in range(SCAN_RANK):
         side += dot(early_unfold[i], unfold[i], LAST)
         gram += dot(unfold[i], unfold[i], LAST)
-    total[pl.ds(0, half), :] = jnp.concatenate([corner[...], side * SCAN_SCALE], axis=1)
-    total[pl.ds(3 * half, half), pl.ds(0, half)] = gram * SCAN_SCALE
+    pack(total, 0, jnp.concatenate([corner[...], side * SCAN_SCALE], axis=1), gram * SCAN_SCALE)
     for s in range(rows):
         x = wide(lambda at, size: slots[s][pl.ds(at, size), :], 0, half, half, pairs)
         y = dot(cft[:, half:], x)
@@ -249,7 +248,7 @@
             x = (rowbuf[h, at, :] + rowpart[h, at, :]).astype(BF16)
             gram += dot(x, x, LAST)
     spare = jnp.concatenate([gram * SCAN_SCALE, jnp.zeros((rows, half - rows), F32)], axis=1)
-    total[pl.ds(5 * half - rows, rows), pl.ds(half, half)] = spare
+    total[pl.ds(4 * half - rows, rows), pl.ds(half, half)] = spare
     n_part = own * SCAN_RANK
     for k in range(2):
         gram = jnp.zeros((pixels, pixels), F32)
@@ -258,12 +257,18 @@
             u = dot(plain[...], stack_rows(slots, at, GROUP)).astype(BF16)
             gram += dot(u, u, FIRST)
         gram *= DET_SCALE
-        total[pl.ds((1 + k) * half, half), :] = gram[:half]
-        total[pl.ds((3 + (1 + k) // 2) * half, half), pl.ds((1 + k) % 2 * half, half)] = gram[half:, half:]
+        pack(total, 1 + k, gram[:half], gram[half:, half:])
     size = keep.shape[0]
     core = lax.axis_index("row") % 2
     keep[...] = total[pl.ds(pl.multiple_of(core * size, 8), size), :]
     send[...] = total[pl.ds(pl.multiple_of((1 - core) * size, 8), size), :]
+
+
+def pack(total, k, top, low):
+    half, part = low.shape[0], low.shape[0] // 2
+    total[pl.ds(k * half, part), :] = top[:part]
+    total[pl.ds(k * half + part, part), :] = jnp.concatenate([low[part:, part:], top[part:, part:]], axis=1)
+    total[pl.ds(3 * half + k // 2 * part, part), pl.ds(k % 2 * half, half)] = low[:part]
 
 
 def unpack(mine, other, row_out, col_out, right_out, left_out, row_gram, grams, sems):
@@ -272,16 +277,21 @@
         [jnp.where(even, mine[...], other[...]), jnp.where(even, other[...], mine[...])], axis=0
     )
     cols, rows = col_out.shape[0], row_out.shape[0]
-    half = cols // 2
+    half, part = cols // 2, cols // 4
     copies = []
     for k, out in enumerate([col_out, right_out, left_out]):
-        top = total[k * half : (k + 1) * half]
-        corner = total[(3 + k // 2) * half : (4 + k // 2) * half, k % 2 * half : (k % 2 + 1) * half]
-        grams[k, pl.ds(0, half), :] = top
-        grams[k, pl.ds(half, half), :] = jnp.concatenate([top[:, half:].T, corner], axis=1)
+        top = total[k * half : k * half + part]
+        next_top = total[k * half + part : (k + 1) * half]
+        low = total[3 * half + k // 2 * part :][:part, k % 2 * half : (k % 2 + 1) * half]
+        side = jnp.concatenate([top[:, half:], next_top[:, half:]], axis=0).T
+        last = [side[part:], low[:, part:].T, next_top[:, :part]]
+        grams[k, pl.ds(0, part), :] = top
+        grams[k, pl.ds(part, part), :] = jnp.concatenate([top[:, part:half].T, next_top[:, part:]], axis=1)
+        grams[k, pl.ds(half, part), :] = jnp.concatenate([side[:part], low], axis=1)
+        grams[k, pl.ds(half + part, part), :] = jnp.concatenate(last, axis=1)
         copies.append(pltpu.make_async_copy(grams.at[k], out, sems.at[k]))
         copies[-1].start()
-    row_gram[...] = total[5 * half - rows : 5 * half, half : half + rows]
+    row_gram[...] = total[4 * half - rows : 4 * half, half : half + rows]
     copies.append(pltpu.make_async_copy(row_gram, row_out, sems.at[3]))
     copies[-1].start()
     for copy in copies:
@@ -359,10 +369,10 @@
     scratch = [
         pltpu.VMEM((SCAN_RANK, early, width), BF16),
         pltpu.VMEM(row_shape, F32),
-        pltpu.VMEM((5 * cols // 2, pixels), F32),
+        pltpu.VMEM((2 * cols, pixels), F32),
     ]
     mine, other = call(
-        functools.partial(partial_grams, own), (cft, *known, second), [((5 * cols // 4, pixels), F32)] * 2, scratch
+        functools.partial(partial_grams, own), (cft, *known, second), [((cols, pixels), F32)] * 2, scratch
     )
     mine, other = all_sum(mine, other, n)
     outs = [(rows, rows), (cols, cols), (pixels, pixels), (pixels, pixels)]

time: 56.9 us -> 56.5 us (level)
  waiting for transfers between devices: 26.1 us -> 25.3 us
    ppermute x11, waiting for transfers between devices: 22.8 us -> 22 us  [swap(): return lax.ppermute(x, 'row', [(i, i ^ step) for i in range(n)])]
where the time goes in v5:
time: 56.5 us; the launch traced here: 56.3 us
  waiting for transfers between devices  25.3 us (45%)
  starting transfers between devices  20.8 us (37%)
  Pallas kernels  9.33 us (17%)
  between operations  0.78 us (1%)
    ppermute x11, waiting for transfers between devices, swap(): return lax.ppermute(x, 'row', [(i, i ^ step) for i in range(n)])  22 us
    ppermute x11, starting transfers between devices, swap(): return lax.ppermute(x, 'row', [(i, i ^ step) for i in range(n)])  15.5 us
    all_to_all x1, starting transfers between devices, local(): lax.all_to_all(second, 'row', split_axis=0, concat_axis=0, tiled=True)  5.24 us
    pallas_call x1, Pallas kernels, projections(): pl.pallas_call(functools.partial(late_cubes, early, own), out_shape=part...  3.64 us
    all_to_all x1, waiting for transfers between devices, local(): lax.all_to_all(second, 'row', split_axis=0, concat_axis=0, tiled=True)  3.31 us
    pallas_call x1, Pallas kernels, projections(): pl.pallas_call(functools.partial(early_cubes, early, own, n // 2), out_sh...  2.58 us
    pallas_call x4, Pallas kernels, call(): pl.pallas_call(kernel, out_shape=[jax.ShapeDtypeStruct(*out) for out in o...  1.99 us
  transfers between devices with their start and end apart: 12, of which 9 were waited for; matrix products, arithmetic and copies ran while one was open for 0% of the time, Pallas kernels for 8%

profile of v5, /device:TPU:0, one launch (start us, length us, event | category | flops | bytes accessed | tf_op | source)
XLA Modules:
  0.0 56.3 jit_solution(12914897149948354343)
XLA Ops:
  0.7 2.6 %shard_map.85 = (bf16[4,128,128]{2,1,0:T(8,128)(2,1)S(1)}, bf16[4,128,128]{2,1,0:T(8,128)(2,1)S(1)}) custom-call(bf16[128,128,128]{2,1,0:T(8,128)(2,1)} %bitcast.5, bf16[64,128]{1,0:T(8,128)(2,1)} %bitcast.7, bf16[64,128]{1,0:T(8,128)(2,1)} %bitcast.9), custom_call_target="tpu_custom_call" | custom-call | tf_op jit(solution)/shard_map/pallas_call | solution.py:142
  3.3 4.1 %collective-permute-start.1 = (bf16[4,128,128]{2,1,0:T(8,128)(2,1)S(1)}, bf16[4,128,128]{2,1,0:T(8,128)(2,1)S(1)}, u32[]{:S(2)}, u32[]{:S(2)}) collective-permute-start(bf16[4,128,128]{2,1,0:T(8,128)(2,1)S(1)} %get-tuple-element.25), channel_id=1, source_target_pairs={{0,8},{1,9},{2,10},{3,11},{4,12},{5,13},{6,14},{7,15},{8,0},{9,1},... | collective-permute-start | bytes 393224 | tf_op jit(solution)/shard_map/ppermute | solution.py:312
  7.4 1.3 %collective-permute-start.2 = (bf16[4,128,128]{2,1,0:T(8,128)(2,1)S(1)}, bf16[4,128,128]{2,1,0:T(8,128)(2,1)S(1)}, u32[]{:S(2)}, u32[]{:S(2)}) collective-permute-start(bf16[4,128,128]{2,1,0:T(8,128)(2,1)S(1)} %get-tuple-element.26), channel_id=1, source_target_pairs={{0,12},{1,13},{2,14},{3,15},{4,8},{5,9},{6,10},{7,11},{8,4},{9,5},... | collective-permute-start | bytes 393224 | tf_op jit(solution)/shard_map/ppermute | solution.py:312
  8.7 3.6 %shard_map.84 = (bf16[4,128,128]{2,1,0:T(8,128)(2,1)S(1)}, bf16[4,128,128]{2,1,0:T(8,128)(2,1)S(1)}, bf16[16,192,128]{2,1,0:T(8,128)(2,1)}) custom-call(bf16[128,128,128]{2,1,0:T(8,128)(2,1)S(1)} %bitcast.6, bf16[8,128]{1,0:T(8,128)(2,1)S(1)} %bitcast.11, bf16[64,128]{1,0:T(8,128)(2,1)S(1)} %bitcast.8, bf16[64,128]{1,0:T(8,128)(2,1)S(1)} %bitcast.10), custom_call_target="tpu_custom_call" | custom-call | tf_op jit(solution)/shard_map/pallas_call | solution.py:158
  12.4 0.3 collective-permute-start
  12.7 5.2 %all-to-all-start = ((bf16[16,192,128]{2,1,0:T(8,128)(2,1)}), bf16[16,192,128]{2,1,0:T(8,128)(2,1)S(1)}, u32[]{:S(2)}, u32[]{:S(2)}) async-start(bf16[16,192,128]{2,1,0:T(8,128)(2,1)} %get-tuple-element.39), calls=%async_computation | async-start | bytes 1572864 | tf_op jit(solution)/shard_map/all_to_all | solution.py:357
  18.0 1.3 %collective-permute-done.refs_1_ = bf16[4,128,128]{2,1,0:T(8,128)(2,1)S(1)} collective-permute-done((bf16[4,128,128]{2,1,0:T(8,128)(2,1)S(1)}, bf16[4,128,128]{2,1,0:T(8,128)(2,1)S(1)}, u32[]{:S(2)}, u32[]{:S(2)}) %collective-permute-start) | collective-permute-done | bytes 131104 | tf_op jit(solution)/shard_map/ppermute | solution.py:312
  19.4 1.6 %collective-permute-start.4 = (bf16[4,128,128]{2,1,0:T(8,128)(2,1)S(1)}, bf16[4,128,128]{2,1,0:T(8,128)(2,1)S(1)}, u32[]{:S(2)}, u32[]{:S(2)}) collective-permute-start(bf16[4,128,128]{2,1,0:T(8,128)(2,1)S(1)} %get-tuple-element.33), channel_id=1, source_target_pairs={{0,2},{1,3},{2,0},{3,1},{4,6},{5,7},{6,4},{7,5},{8,10},{9,11},{10,... | collective-permute-start | bytes 393224 | tf_op jit(solution)/shard_map/ppermute | solution.py:312
  21.0 0.2 collective-permute-start.5
  21.3 9.3 %collective-permute-done.4.refs_2_ = bf16[4,128,128]{2,1,0:T(8,128)(2,1)S(1)} collective-permute-done((bf16[4,128,128]{2,1,0:T(8,128)(2,1)S(1)}, bf16[4,128,128]{2,1,0:T(8,128)(2,1)S(1)}, u32[]{:S(2)}, u32[]{:S(2)}) %collective-permute-start.4) | collective-permute-done | bytes 131104 | tf_op jit(solution)/shard_map/ppermute | solution.py:312
  30.5 2.0 %collective-permute-done.5.refs_3_ = bf16[4,128,128]{2,1,0:T(8,128)(2,1)S(1)} collective-permute-done((bf16[4,128,128]{2,1,0:T(8,128)(2,1)S(1)}, bf16[4,128,128]{2,1,0:T(8,128)(2,1)S(1)}, u32[]{:S(2)}, u32[]{:S(2)}) %collective-permute-start.5) | collective-permute-done | bytes 131104 | tf_op jit(solution)/shard_map/ppermute | solution.py:312
  32.5 0.8 %shard_map.88 = (bf16[128,256]{1,0:T(8,128)(2,1)S(1)}, bf16[8,64,256]{2,1,0:T(8,128)(2,1)S(1)}, f32[2,128,128]{2,1,0:T(8,128)S(1)}, f32[64,64]{1,0:T(8,128)S(1)}) custom-call(bf16[8,16]{1,0:T(8,128)(2,1)S(1)} %bitcast.14, bf16[8,128]{1,0:T(8,128)(2,1)S(1)} %bitcast.12, bf16[4,128,128]{2,1,0:T(8,128)(2,1)S(1)} %get-tuple-element.31.refs_0_, ...), custom_call_target="tpu_custom_call" | custom-call | flops 100000000 | bytes 1048576 | tf_op jit(solution)/shard_map/pallas_call | solution.py:302
  33.3 3.3 %all-to-all-done.second = bf16[16,192,128]{2,1,0:T(8,128)(2,1)S(1)} async-done(((bf16[16,192,128]{2,1,0:T(8,128)(2,1)}), bf16[16,192,128]{2,1,0:T(8,128)(2,1)S(1)}, u32[]{:S(2)}, u32[]{:S(2)}) %all-to-all-start) | async-done | bytes 786464 | tf_op jit(solution)/shard_map/all_to_all | solution.py:357
  36.7 1.1 %shard_map.89 = (f32[128,128]{1,0:T(8,128)S(1)}, f32[128,128]{1,0:T(8,128)S(1)}) custom-call(bf16[8,128]{1,0:T(8,128)(2,1)S(1)} %bitcast.13, bf16[128,256]{1,0:T(8,128)(2,1)S(1)} %get-tuple-element.35.plain, bf16[8,64,256]{2,1,0:T(8,128)(2,1)S(1)} %get-tuple-element.36.early_unfold, f32[2,128,128]{2,1,0:T(8,128)S(1)} %get-tuple-element.37.rowpart, ...), custom_call_target="tpu_custom_call" | custom-call | flops 100000000 | bytes 1048576 | tf_op jit(solution)/shard_map/pallas_call | solution.py:302
  37.8 0.3 collective-permute-start.6
  38.1 1.0 %collective-permute-done.6 = f32[128,128]{1,0:T(8,128)S(1)} collective-permute-done((f32[128,128]{1,0:T(8,128)S(1)}, f32[128,128]{1,0:T(8,128)S(1)}, u32[]{:S(2)}, u32[]{:S(2)}) %collective-permute-start.6) | collective-permute-done | bytes 65568 | tf_op jit(solution)/shard_map/ppermute | solution.py:312
  39.1 1.6 %collective-permute-start.7 = (f32[128,128]{1,0:T(8,128)S(1)}, f32[128,128]{1,0:T(8,128)S(1)}, u32[]{:S(2)}, u32[]{:S(2)}) collective-permute-start(f32[128,128]{1,0:T(8,128)S(1)} %add.12), channel_id=1, source_target_pairs={{0,2},{1,3},{2,0},{3,1},{4,6},{5,7},{6,4},{7,5},{8,10},{9,11},{10,... | collective-permute-start | bytes 196616 | tf_op jit(solution)/shard_map/ppermute | solution.py:312
  40.7 2.7 %collective-permute-done.7 = f32[128,128]{1,0:T(8,128)S(1)} collective-permute-done((f32[128,128]{1,0:T(8,128)S(1)}, f32[128,128]{1,0:T(8,128)S(1)}, u32[]{:S(2)}, u32[]{:S(2)}) %collective-permute-start.7) | collective-permute-done | bytes 65568 | tf_op jit(solution)/shard_map/ppermute | solution.py:312
  43.5 2.7 %collective-permute-start.8 = (f32[128,128]{1,0:T(8,128)S(1)}, f32[128,128]{1,0:T(8,128)S(1)}, u32[]{:S(2)}, u32[]{:S(2)}) collective-permute-start(f32[128,128]{1,0:T(8,128)S(1)} %add.13), channel_id=1, source_target_pairs={{0,4},{1,5},{2,6},{3,7},{4,0},{5,1},{6,2},{7,3},{8,12},{9,13},{10,... | collective-permute-start | bytes 196616 | tf_op jit(solution)/shard_map/ppermute | solution.py:312
  46.2 2.2 %collective-permute-done.8 = f32[128,128]{1,0:T(8,128)S(1)} collective-permute-done((f32[128,128]{1,0:T(8,128)S(1)}, f32[128,128]{1,0:T(8,128)S(1)}, u32[]{:S(2)}, u32[]{:S(2)}) %collective-permute-start.8) | collective-permute-done | bytes 65568 | tf_op jit(solution)/shard_map/ppermute | solution.py:312
  48.4 3.1 %collective-permute-start.9 = (f32[128,128]{1,0:T(8,128)S(1)}, f32[128,128]{1,0:T(8,128)S(1)}, u32[]{:S(2)}, u32[]{:S(2)}) collective-permute-start(f32[128,128]{1,0:T(8,128)S(1)} %add.14), channel_id=1, source_target_pairs={{0,8},{1,9},{2,10},{3,11},{4,12},{5,13},{6,14},{7,15},{8,0},{9,1},... | collective-permute-start | bytes 196616 | tf_op jit(solution)/shard_map/ppermute | solution.py:312
  51.6 2.2 %collective-permute-done.9 = f32[128,128]{1,0:T(8,128)S(1)} collective-permute-done((f32[128,128]{1,0:T(8,128)S(1)}, f32[128,128]{1,0:T(8,128)S(1)}, u32[]{:S(2)}, u32[]{:S(2)}) %collective-permute-start.9) | collective-permute-done | bytes 65568 | tf_op jit(solution)/shard_map/ppermute | solution.py:312
  53.9 1.2 %collective-permute-done.10.other = f32[128,128]{1,0:T(8,128)S(1)} collective-permute-done((f32[128,128]{1,0:T(8,128)S(1)}, f32[128,128]{1,0:T(8,128)S(1)}, u32[]{:S(2)}, u32[]{:S(2)}) %collective-permute-start.10) | collective-permute-done | bytes 65568 | tf_op jit(solution)/shard_map/ppermute | solution.py:312
  55.1 1.1 %shard_map.90 = (f32[16,16]{1,0:T(8,128)}, f32[128,128]{1,0:T(8,128)}, f32[128,128]{1,0:T(8,128)}, f32[128,128]{1,0:T(8,128)}) custom-call(f32[128,128]{1,0:T(8,128)S(1)} %add.15.mine, f32[128,128]{1,0:T(8,128)S(1)} %collective-permute-done.10.other), custom_call_target="tpu_custom_call" | custom-call | tf_op jit(solution)/shard_map/pallas_call | solution.py:380
  (21 shorter events, 0.3 us)
Async XLA Ops:
  0.6 8.1 %copy-start = (bf16[1,128,128,128]{3,2,1,0:T(8,128)(2,1)S(1)}, bf16[1,128,128,128]{3,2,1,0:T(8,128)(2,1)}, u32[]{:S(2)}) copy-start(bf16[1,128,128,128]{3,2,1,0:T(8,128)(2,1)} %param.5) | copy-start | bytes 12582916
  0.6 8.1 %copy-start.1 = (bf16[128,64]{0,1:T(8,128)(2,1)S(1)}, bf16[128,64]{0,1:T(8,128)(2,1)}, u32[]{:S(2)}) copy-start(bf16[128,64]{0,1:T(8,128)(2,1)} %param.8) | copy-start | bytes 49156
  0.7 8.1 %copy-start.2 = (bf16[128,64]{0,1:T(8,128)(2,1)S(1)}, bf16[128,64]{0,1:T(8,128)(2,1)}, u32[]{:S(2)}) copy-start(bf16[128,64]{0,1:T(8,128)(2,1)} %param.9) | copy-start | bytes 49156
  0.7 8.1 %copy-start.3 = (bf16[128,8]{0,1:T(8,128)(2,1)S(1)}, bf16[128,8]{0,1:T(8,128)(2,1)}, u32[]{:S(2)}) copy-start(bf16[128,8]{0,1:T(8,128)(2,1)} %param.7) | copy-start | bytes 6148
  3.3 14.7 %collective-permute-start.1 = (bf16[4,128,128]{2,1,0:T(8,128)(2,1)S(1)}, bf16[4,128,128]{2,1,0:T(8,128)(2,1)S(1)}, u32[]{:S(2)}, u32[]{:S(2)}) collective-permute-start(bf16[4,128,128]{2,1,0:T(8,128)(2,1)S(1)} %get-tuple-element.25), channel_id=1, source_target_pairs={{0,8},{1,9},{2,10},{3,11},{4,12},{5,13},{6,14},{7,15},{8,0},{9,1},... | collective-permute-start | bytes 393224 | tf_op jit(solution)/shard_map/ppermute | solution.py:312
  7.4 10.6 %collective-permute-start.2 = (bf16[4,128,128]{2,1,0:T(8,128)(2,1)S(1)}, bf16[4,128,128]{2,1,0:T(8,128)(2,1)S(1)}, u32[]{:S(2)}, u32[]{:S(2)}) collective-permute-start(bf16[4,128,128]{2,1,0:T(8,128)(2,1)S(1)} %get-tuple-element.26), channel_id=1, source_target_pairs={{0,12},{1,13},{2,14},{3,15},{4,8},{5,9},{6,10},{7,11},{8,4},{9,5},... | collective-permute-start | bytes 393224 | tf_op jit(solution)/shard_map/ppermute | solution.py:312
  12.4 6.9 %collective-permute-start = (bf16[4,128,128]{2,1,0:T(8,128)(2,1)S(1)}, bf16[4,128,128]{2,1,0:T(8,128)(2,1)S(1)}, u32[]{:S(2)}, u32[]{:S(2)}) collective-permute-start(bf16[4,128,128]{2,1,0:T(8,128)(2,1)S(1)} %get-tuple-element.24), channel_id=1, source_target_pairs={{0,4},{1,5},{2,6},{3,7},{4,0},{5,1},{6,2},{7,3},{8,12},{9,13},{10,... | collective-permute-start | bytes 393224 | tf_op jit(solution)/shard_map/ppermute | solution.py:312
  12.7 24.0 %all-to-all-start = ((bf16[16,192,128]{2,1,0:T(8,128)(2,1)}), bf16[16,192,128]{2,1,0:T(8,128)(2,1)S(1)}, u32[]{:S(2)}, u32[]{:S(2)}) async-start(bf16[16,192,128]{2,1,0:T(8,128)(2,1)} %get-tuple-element.39), calls=%async_computation | async-start | bytes 1572864 | tf_op jit(solution)/shard_map/all_to_all | solution.py:357
  17.9 14.6 %copy-start.4 = (bf16[16,8]{0,1:T(8,128)(2,1)S(1)}, bf16[16,8]{0,1:T(8,128)(2,1)}, u32[]{:S(2)}) copy-start(bf16[16,8]{0,1:T(8,128)(2,1)} %param.6) | copy-start | bytes 772
  19.3 1.9 %collective-permute-start.3 = (bf16[4,128,128]{2,1,0:T(8,128)(2,1)S(1)}, bf16[4,128,128]{2,1,0:T(8,128)(2,1)S(1)}, u32[]{:S(2)}, u32[]{:S(2)}) collective-permute-start(bf16[4,128,128]{2,1,0:T(8,128)(2,1)S(1)} %get-tuple-element.32), channel_id=1, source_target_pairs={{0,1},{1,0},{2,3},{3,2},{4,5},{5,4},{6,7},{7,6},{8,9},{9,8},{10,11... | collective-permute-start | bytes 393224 | tf_op jit(solution)/shard_map/ppermute | solution.py:312
  19.4 11.1 %collective-permute-start.4 = (bf16[4,128,128]{2,1,0:T(8,128)(2,1)S(1)}, bf16[4,128,128]{2,1,0:T(8,128)(2,1)S(1)}, u32[]{:S(2)}, u32[]{:S(2)}) collective-permute-start(bf16[4,128,128]{2,1,0:T(8,128)(2,1)S(1)} %get-tuple-element.33), channel_id=1, source_target_pairs={{0,2},{1,3},{2,0},{3,1},{4,6},{5,7},{6,4},{7,5},{8,10},{9,11},{10,... | collective-permute-start | bytes 393224 | tf_op jit(solution)/shard_map/ppermute | solution.py:312
  21.0 11.5 %collective-permute-start.5 = (bf16[4,128,128]{2,1,0:T(8,128)(2,1)S(1)}, bf16[4,128,128]{2,1,0:T(8,128)(2,1)S(1)}, u32[]{:S(2)}, u32[]{:S(2)}) collective-permute-start(bf16[4,128,128]{2,1,0:T(8,128)(2,1)S(1)} %get-tuple-element.34), channel_id=1, source_target_pairs={{0,3},{1,2},{2,1},{3,0},{4,7},{5,6},{6,5},{7,4},{8,11},{9,10},{10,... | collective-permute-start | bytes 393224 | tf_op jit(solution)/shard_map/ppermute | solution.py:312
  37.8 1.3 %collective-permute-start.6 = (f32[128,128]{1,0:T(8,128)S(1)}, f32[128,128]{1,0:T(8,128)S(1)}, u32[]{:S(2)}, u32[]{:S(2)}) collective-permute-start(f32[128,128]{1,0:T(8,128)S(1)} %get-tuple-element.41), channel_id=1, source_target_pairs={{0,1},{1,0},{2,3},{3,2},{4,5},{5,4},{6,7},{7,6},{8,9},{9,8},{10,11... | collective-permute-start | bytes 196616 | tf_op jit(solution)/shard_map/ppermute | solution.py:312
  39.1 4.3 %collective-permute-start.7 = (f32[128,128]{1,0:T(8,128)S(1)}, f32[128,128]{1,0:T(8,128)S(1)}, u32[]{:S(2)}, u32[]{:S(2)}) collective-permute-start(f32[128,128]{1,0:T(8,128)S(1)} %add.12), channel_id=1, source_target_pairs={{0,2},{1,3},{2,0},{3,1},{4,6},{5,7},{6,4},{7,5},{8,10},{9,11},{10,... | collective-permute-start | bytes 196616 | tf_op jit(solution)/shard_map/ppermute | solution.py:312
  43.5 5.0 %collective-permute-start.8 = (f32[128,128]{1,0:T(8,128)S(1)}, f32[128,128]{1,0:T(8,128)S(1)}, u32[]{:S(2)}, u32[]{:S(2)}) collective-permute-start(f32[128,128]{1,0:T(8,128)S(1)} %add.13), channel_id=1, source_target_pairs={{0,4},{1,5},{2,6},{3,7},{4,0},{5,1},{6,2},{7,3},{8,12},{9,13},{10,... | collective-permute-start | bytes 196616 | tf_op jit(solution)/shard_map/ppermute | solution.py:312
  48.4 5.4 %collective-permute-start.9 = (f32[128,128]{1,0:T(8,128)S(1)}, f32[128,128]{1,0:T(8,128)S(1)}, u32[]{:S(2)}, u32[]{:S(2)}) collective-permute-start(f32[128,128]{1,0:T(8,128)S(1)} %add.14), channel_id=1, source_target_pairs={{0,8},{1,9},{2,10},{3,11},{4,12},{5,13},{6,14},{7,15},{8,0},{9,1},... | collective-permute-start | bytes 196616 | tf_op jit(solution)/shard_map/ppermute | solution.py:312
  53.8 1.3 %collective-permute-start.10 = (f32[128,128]{1,0:T(8,128)S(1)}, f32[128,128]{1,0:T(8,128)S(1)}, u32[]{:S(2)}, u32[]{:S(2)}) collective-permute-start(f32[128,128]{1,0:T(8,128)S(1)} %add.15.mine), channel_id=1, source_target_pairs={{0,1},{1,0},{2,3},{3,2},{4,5},{5,4},{6,7},{7,6},{8,9},{9,8},{10,11... | collective-permute-start | bytes 196616 | tf_op jit(solution)/shard_map/ppermute | solution.py:312

commit v6 on v5

--- a/solution.py
+++ b/solution.py
@@ -40,11 +40,10 @@
     )
 
 
-def early_cubes(early, own, base, slab, dt_in, vt_in, *refs):
-    *far, dt, vt, images, right, arrived, ready = refs
+def early_cubes(early, own, slab, dt_in, vt_in, *refs):
+    *first, kept, dt, vt, images, right, arrived, ready = refs
     pixels = slab.shape[1]
-    plane = far[0].shape[0]
-    rank = own * plane * len(far)
+    plane, rank = first[0].shape[0], dt.shape[0]
     pitch = early + 1
     cuts = [0, early // 2, early]
     copies = [
@@ -56,7 +55,7 @@
         copy.start()
     for copy in factors:
         copy.wait()
-    vt2, dd = paired(slot_order(vt[...], own, base, rank)), paired(dt[...].T)
+    vt2, dd = paired(slot_order(vt[...], own)), paired(dt[...].T)
     for at, copy in enumerate(copies):
         copy.wait()
         for c in range(cuts[at], cuts[at + 1], 4):
@@ -66,45 +65,49 @@
                     right[pl.ds(c + 2 * i + j, rank, stride=pitch), :] = rights[
                         j * rank : (j + 1) * rank, i * pixels : (i + 1) * pixels
                     ]
-    for slot in range(plane * len(far)):
-        slot_cubes(slot, early, pitch, own, right, dd, far[slot // plane].at[slot % plane])
-
-
-def slot_order(factor, own, base, count):
-    shape = (count, factor.shape[0])
-    r = lax.broadcasted_iota(jnp.int32, shape, 0) + base * own
+    for slot in range(rank // own):
+        to = first[slot // plane].at[slot % plane]
+        for h in range(own // 2):
+            b = slot * own + 2 * h
+            x = [right[pl.ds((b + k) * pitch, early), :] for k in range(2)]
+            x = jnp.concatenate(x, axis=1).astype(BF16)
+            kept[b // 2] = x
+            to[pl.ds(h * early, early), :] = dot(x, dd).astype(BF16)
+
+
+def slot_order(factor, own):
+    shape = (factor.shape[0], factor.shape[0])
+    r = lax.broadcasted_iota(jnp.int32, shape, 0)
     c = lax.broadcasted_iota(jnp.int32, shape, 1)
     take = (c // own == r // own ^ lax.axis_index("row")) & (c % own == r % own)
     return dot(take.astype(BF16), factor).astype(BF16)
 
 
-def slot_cubes(slot, early, pitch, own, right, dd, to):
-    for h in range(own // 2):
-        b = slot * own + 2 * h
-        x = [right[pl.ds((b + k) * pitch, early), :] for k in range(2)]
-        to[pl.ds(h * early, early), :] = dot(jnp.concatenate(x, axis=1).astype(BF16), dd).astype(BF16)
-
-
-def late_cubes(early, own, images, cft, dt, vt, *refs):
-    *near, out, right, left, second, sent = refs
+def late_cubes(own, images, cft, dt, vt, kept, out, right, left, second, sent):
     cols, pixels, rank = images.shape[0], images.shape[1], dt.shape[0]
-    pitch = cols + 1
-    dt2, vt2 = (paired(slot_order(x[...], own, 0, rank)) for x in (dt, vt))
+    early = kept.shape[1]
+    late = cols - early
+    dt2, vt2 = (paired(slot_order(x[...], own)) for x in (dt, vt))
     for c in range(0, cols, 4):
         four = four_images(images, c)
-        rights = dot(vt2, four, LAST)
         lefts = dot(dt2, four)
+        if c >= early:
+            rights = dot(vt2, four, LAST)
         for i in range(2):
             for j in range(2):
-                at_c = pl.ds(c + 2 * i + j, rank, stride=pitch)
-                right[at_c, :] = rights[j * rank : (j + 1) * rank, i * pixels : (i + 1) * pixels]
-                left[at_c, :] = lefts[i * rank : (i + 1) * rank, j * pixels : (j + 1) * pixels]
+                at = c + 2 * i + j
+                left[pl.ds(at, rank, stride=cols + 1), :] = lefts[
+                    i * rank : (i + 1) * rank, j * pixels : (j + 1) * pixels
+                ]
+                if c >= early:
+                    right[pl.ds(at - early, rank, stride=late + 1), :] = rights[
+                        j * rank : (j + 1) * rank, i * pixels : (i + 1) * pixels
+                    ]
     dd = paired(dt[...].T)
     pairs, pair = own // 2, 2 * SCAN_RANK
-    late = cols - early
-
-    def two(ref, b):
-        parts = [ref[pl.ds((b + k) * pitch, cols), :] for k in range(2)]
+
+    def two(ref, b, count):
+        parts = [ref[pl.ds((b + k) * (count + 1), count), :] for k in range(2)]
         return jnp.concatenate(parts, axis=1).astype(BF16)
 
     def stacked(sums):
@@ -113,19 +116,17 @@
     me = lax.axis_index("row")
     copies = []
     for slot in range(rank // own):
-        p = me ^ slot
         for h in range(pairs):
-            x = two(right, slot * own + 2 * h)
-            y = two(left, slot * own + 2 * h)
+            b = slot * own + 2 * h
+            x = two(right, b, late)
+            y = two(left, b, cols)
             at = pairs * late + h * pair
-            second[slot, pl.ds(h * late, late), :] = dot(x[early:], dd).astype(BF16)
+            second[slot, pl.ds(h * late, late), :] = dot(x, dd).astype(BF16)
+            x = jnp.concatenate([kept[b // 2], x], axis=0)
             second[slot, pl.ds(at, pair), :] = stacked(dot(cft[...], x))
             second[slot, pl.ds(at + pairs * pair, pair), :] = stacked(dot(cft[...], y))
-        copies.append(pltpu.make_async_copy(second.at[slot], out.at[p], sent.at[slot]))
+        copies.append(pltpu.make_async_copy(second.at[slot], out.at[me ^ slot], sent.at[slot]))
         copies[-1].start()
-    plane = near[0].shape[0]
-    for slot in range(plane * len(near)):
-        slot_cubes(slot, early, pitch, own, right, dd, near[slot // plane].at[slot % plane])
     for copy in copies:
         copy.wait()
 
@@ -137,34 +138,38 @@
     anywhere = pl.BlockSpec(memory_space=pl.ANY)
     in_vmem = pl.BlockSpec(memory_space=pltpu.VMEM)
     params = pltpu.CompilerParams(vmem_limit_bytes=56 << 20)
-    half = n // plane // 2
-    part = [jax.ShapeDtypeStruct((plane, own // 2 * early, pixels), BF16)] * half
-    far = pl.pallas_call(
-        functools.partial(early_cubes, early, own, n // 2),
-        out_shape=[pltpu.VMEM(part[0].shape, BF16)] * half,
+    *first, kept = pl.pallas_call(
+        functools.partial(early_cubes, early, own),
+        out_shape=[pltpu.VMEM((plane, own // 2 * early, pixels), BF16)] * (n // plane)
+        + [pltpu.VMEM((rank // 2, early, 2 * pixels), BF16)],
         in_specs=[anywhere] * 3,
-        out_specs=[in_vmem] * half,
+        out_specs=[in_vmem] * (n // plane + 1),
         scratch_shapes=[
             pltpu.VMEM(dt.shape, BF16),
             pltpu.VMEM(vt.shape, BF16),
             pltpu.VMEM((early,) + slab.shape[1:], BF16),
-            pltpu.VMEM((rank // 2 * (early + 1), pixels), F32),
+            pltpu.VMEM((rank * (early + 1), pixels), F32),
             pltpu.SemaphoreType.DMA((2,)),
             pltpu.SemaphoreType.DMA((2,)),
         ],
         compiler_params=params,
     )(slab, dt, vt)
-    height = own // 2 * (cols - early) + 2 * own * SCAN_RANK
-    *near, second = pl.pallas_call(
-        functools.partial(late_cubes, early, own),
-        out_shape=part + [jax.ShapeDtypeStruct((n, height, pixels), BF16)],
-        in_specs=[in_vmem] * 4,
-        out_specs=[in_vmem] * half + [anywhere],
-        scratch_shapes=[pltpu.VMEM((rank * (cols + 1), pixels), F32)] * 2
-        + [pltpu.VMEM((n, height, pixels), BF16), pltpu.SemaphoreType.DMA((n,))],
+    late = cols - early
+    height = own // 2 * late + 2 * own * SCAN_RANK
+    second = pl.pallas_call(
+        functools.partial(late_cubes, own),
+        out_shape=jax.ShapeDtypeStruct((n, height, pixels), BF16),
+        in_specs=[in_vmem] * 5,
+        out_specs=anywhere,
+        scratch_shapes=[
+            pltpu.VMEM((rank * (late + 1), pixels), F32),
+            pltpu.VMEM((rank * (cols + 1), pixels), F32),
+            pltpu.VMEM((n, height, pixels), BF16),
+            pltpu.SemaphoreType.DMA((n,)),
+        ],
         compiler_params=pltpu.CompilerParams(vmem_limit_bytes=32 << 20),
-    )(slab, cft, dt, vt)
-    return near + list(far), second
+    )(slab, cft, dt, vt, kept)
+    return first, second
 
 
 def one_hot(shape, rows_per, cols_per):

time: 56.5 us -> 56.2 us (level)
  transfers between devices with their start and end apart: 12 -> 12, of which waited for: 9 -> 9; matrix products, arithmetic and copies ran while one was open for 0% -> 0% of each run, Pallas kernels for 8% -> 7%
where the time goes in v6:
time: 56.2 us; the launch traced here: 56 us
  waiting for transfers between devices  25.3 us (45%)
  starting transfers between devices  20.7 us (37%)
  Pallas kernels  9.04 us (16%)
  between operations  0.78 us (1%)
    ppermute x11, waiting for transfers between devices, swap(): return lax.ppermute(x, 'row', [(i, i ^ step) for i in range(n)])  22 us
    ppermute x11, starting transfers between devices, swap(): return lax.ppermute(x, 'row', [(i, i ^ step) for i in range(n)])  15.5 us
    all_to_all x1, starting transfers between devices, local(): lax.all_to_all(second, 'row', split_axis=0, concat_axis=0, tiled=True)  5.27 us
    all_to_all x1, waiting for transfers between devices, local(): lax.all_to_all(second, 'row', split_axis=0, concat_axis=0, tiled=True)  3.31 us
    pallas_call x1, Pallas kernels, projections(): pl.pallas_call(functools.partial(late_cubes, own), out_shape=jax.ShapeDty...  3.14 us
    pallas_call x1, Pallas kernels, projections(): pl.pallas_call(functools.partial(early_cubes, early, own), out_shape=[plt...  2.8 us
    pallas_call x4, Pallas kernels, call(): pl.pallas_call(kernel, out_shape=[jax.ShapeDtypeStruct(*out) for out in o...  1.98 us
  transfers between devices with their start and end apart: 12, of which 9 were waited for; matrix products, arithmetic and copies ran while one was open for 0% of the time, Pallas kernels for 7%

profile of v6, /device:TPU:0, one launch (start us, length us, event | category | flops | bytes accessed | tf_op | source)
XLA Modules:
  0.0 56.0 jit_solution(4850846895725677153)
XLA Ops:
  0.7 2.8 %shard_map.84 = (bf16[4,128,128]{2,1,0:T(8,128)(2,1)S(1)}, bf16[4,128,128]{2,1,0:T(8,128)(2,1)S(1)}, bf16[4,128,128]{2,1,0:T(8,128)(2,1)S(1)}, bf16[4,128,128]{2,1,0:T(8,128)(2,1)S(1)}, bf16[32,64,256]{2,1,0:T(8,128)(2,1)S(1)}) custom-call(bf16[128,128,128]{2,1,0:T(8,128)(2,1)} %bitcast.5, bf16[64,128]{1,0:T(8,128)(2,1)} %bitcast.7, bf16[64,128]{1,0:T(8,128)(2,1)} %bitcast.9), custom_call_target="tpu_custom_call" | custom-call | tf_op jit(solution)/shard_map/pallas_call | solution.py:141
  3.5 4.1 %collective-permute-start.1 = (bf16[4,128,128]{2,1,0:T(8,128)(2,1)S(1)}, bf16[4,128,128]{2,1,0:T(8,128)(2,1)S(1)}, u32[]{:S(2)}, u32[]{:S(2)}) collective-permute-start(bf16[4,128,128]{2,1,0:T(8,128)(2,1)S(1)} %get-tuple-element.25), channel_id=1, source_target_pairs={{0,8},{1,9},{2,10},{3,11},{4,12},{5,13},{6,14},{7,15},{8,0},{9,1},... | collective-permute-start | bytes 393224 | tf_op jit(solution)/shard_map/ppermute | solution.py:317
  7.6 1.4 %collective-permute-start.2 = (bf16[4,128,128]{2,1,0:T(8,128)(2,1)S(1)}, bf16[4,128,128]{2,1,0:T(8,128)(2,1)S(1)}, u32[]{:S(2)}, u32[]{:S(2)}) collective-permute-start(bf16[4,128,128]{2,1,0:T(8,128)(2,1)S(1)} %get-tuple-element.26), channel_id=1, source_target_pairs={{0,12},{1,13},{2,14},{3,15},{4,8},{5,9},{6,10},{7,11},{8,4},{9,5},... | collective-permute-start | bytes 393224 | tf_op jit(solution)/shard_map/ppermute | solution.py:317
  8.9 0.2 collective-permute-start
  9.2 3.1 %shard_map.88 = bf16[16,192,128]{2,1,0:T(8,128)(2,1)} custom-call(bf16[128,128,128]{2,1,0:T(8,128)(2,1)S(1)} %bitcast.6, bf16[8,128]{1,0:T(8,128)(2,1)S(1)} %bitcast.11, bf16[64,128]{1,0:T(8,128)(2,1)S(1)} %bitcast.8, bf16[64,128]{1,0:T(8,128)(2,1)S(1)} %bitcast.10, bf16[32,64,256]{2,1,0:T(8,128)(2,1)S(1)} %get-tuple-element.39.kept), custom_call_target="tpu_custom_call" | custom-call | tf_op jit(solution)/shard_map/pallas_call | solution.py:159
  12.3 5.3 %all-to-all-start = ((bf16[16,192,128]{2,1,0:T(8,128)(2,1)}), bf16[16,192,128]{2,1,0:T(8,128)(2,1)S(1)}, u32[]{:S(2)}, u32[]{:S(2)}) async-start(bf16[16,192,128]{2,1,0:T(8,128)(2,1)} %shard_map.88), calls=%async_computation | async-start | bytes 1572864 | tf_op jit(solution)/shard_map/all_to_all | solution.py:362
  17.6 0.4 collective-permute-done.refs_1_
  18.2 1.6 %collective-permute-start.4 = (bf16[4,128,128]{2,1,0:T(8,128)(2,1)S(1)}, bf16[4,128,128]{2,1,0:T(8,128)(2,1)S(1)}, u32[]{:S(2)}, u32[]{:S(2)}) collective-permute-start(bf16[4,128,128]{2,1,0:T(8,128)(2,1)S(1)} %get-tuple-element.33), channel_id=1, source_target_pairs={{0,2},{1,3},{2,0},{3,1},{4,6},{5,7},{6,4},{7,5},{8,10},{9,11},{10,... | collective-permute-start | bytes 393224 | tf_op jit(solution)/shard_map/ppermute | solution.py:317
  19.8 0.2 collective-permute-start.5
  20.1 10.1 %collective-permute-done.4.refs_2_ = bf16[4,128,128]{2,1,0:T(8,128)(2,1)S(1)} collective-permute-done((bf16[4,128,128]{2,1,0:T(8,128)(2,1)S(1)}, bf16[4,128,128]{2,1,0:T(8,128)(2,1)S(1)}, u32[]{:S(2)}, u32[]{:S(2)}) %collective-permute-start.4) | collective-permute-done | bytes 131104 | tf_op jit(solution)/shard_map/ppermute | solution.py:317
  30.2 2.0 %collective-permute-done.5.refs_3_ = bf16[4,128,128]{2,1,0:T(8,128)(2,1)S(1)} collective-permute-done((bf16[4,128,128]{2,1,0:T(8,128)(2,1)S(1)}, bf16[4,128,128]{2,1,0:T(8,128)(2,1)S(1)}, u32[]{:S(2)}, u32[]{:S(2)}) %collective-permute-start.5) | collective-permute-done | bytes 131104 | tf_op jit(solution)/shard_map/ppermute | solution.py:317
  32.2 0.8 %shard_map.87 = (bf16[128,256]{1,0:T(8,128)(2,1)S(1)}, bf16[8,64,256]{2,1,0:T(8,128)(2,1)S(1)}, f32[2,128,128]{2,1,0:T(8,128)S(1)}, f32[64,64]{1,0:T(8,128)S(1)}) custom-call(bf16[8,16]{1,0:T(8,128)(2,1)S(1)} %bitcast.14, bf16[8,128]{1,0:T(8,128)(2,1)S(1)} %bitcast.12, bf16[4,128,128]{2,1,0:T(8,128)(2,1)S(1)} %get-tuple-element.31.refs_0_, ...), custom_call_target="tpu_custom_call" | custom-call | flops 100000000 | bytes 1048576 | tf_op jit(solution)/shard_map/pallas_call | solution.py:307
  33.0 3.3 %all-to-all-done.second = bf16[16,192,128]{2,1,0:T(8,128)(2,1)S(1)} async-done(((bf16[16,192,128]{2,1,0:T(8,128)(2,1)}), bf16[16,192,128]{2,1,0:T(8,128)(2,1)S(1)}, u32[]{:S(2)}, u32[]{:S(2)}) %all-to-all-start) | async-done | bytes 786464 | tf_op jit(solution)/shard_map/all_to_all | solution.py:362
  36.3 1.1 %shard_map.89 = (f32[128,128]{1,0:T(8,128)S(1)}, f32[128,128]{1,0:T(8,128)S(1)}) custom-call(bf16[8,128]{1,0:T(8,128)(2,1)S(1)} %bitcast.13, bf16[128,256]{1,0:T(8,128)(2,1)S(1)} %get-tuple-element.35.plain, bf16[8,64,256]{2,1,0:T(8,128)(2,1)S(1)} %get-tuple-element.36.early_unfold, f32[2,128,128]{2,1,0:T(8,128)S(1)} %get-tuple-element.37.rowpart, ...), custom_call_target="tpu_custom_call" | custom-call | flops 100000000 | bytes 1048576 | tf_op jit(solution)/shard_map/pallas_call | solution.py:307
  37.4 0.3 collective-permute-start.6
  37.8 1.0 %collective-permute-done.6 = f32[128,128]{1,0:T(8,128)S(1)} collective-permute-done((f32[128,128]{1,0:T(8,128)S(1)}, f32[128,128]{1,0:T(8,128)S(1)}, u32[]{:S(2)}, u32[]{:S(2)}) %collective-permute-start.6) | collective-permute-done | bytes 65568 | tf_op jit(solution)/shard_map/ppermute | solution.py:317
  38.8 1.6 %collective-permute-start.7 = (f32[128,128]{1,0:T(8,128)S(1)}, f32[128,128]{1,0:T(8,128)S(1)}, u32[]{:S(2)}, u32[]{:S(2)}) collective-permute-start(f32[128,128]{1,0:T(8,128)S(1)} %add.12), channel_id=1, source_target_pairs={{0,2},{1,3},{2,0},{3,1},{4,6},{5,7},{6,4},{7,5},{8,10},{9,11},{10,... | collective-permute-start | bytes 196616 | tf_op jit(solution)/shard_map/ppermute | solution.py:317
  40.3 2.7 %collective-permute-done.7 = f32[128,128]{1,0:T(8,128)S(1)} collective-permute-done((f32[128,128]{1,0:T(8,128)S(1)}, f32[128,128]{1,0:T(8,128)S(1)}, u32[]{:S(2)}, u32[]{:S(2)}) %collective-permute-start.7) | collective-permute-done | bytes 65568 | tf_op jit(solution)/shard_map/ppermute | solution.py:317
  43.1 2.7 %collective-permute-start.8 = (f32[128,128]{1,0:T(8,128)S(1)}, f32[128,128]{1,0:T(8,128)S(1)}, u32[]{:S(2)}, u32[]{:S(2)}) collective-permute-start(f32[128,128]{1,0:T(8,128)S(1)} %add.13), channel_id=1, source_target_pairs={{0,4},{1,5},{2,6},{3,7},{4,0},{5,1},{6,2},{7,3},{8,12},{9,13},{10,... | collective-permute-start | bytes 196616 | tf_op jit(solution)/shard_map/ppermute | solution.py:317
  45.8 2.2 %collective-permute-done.8 = f32[128,128]{1,0:T(8,128)S(1)} collective-permute-done((f32[128,128]{1,0:T(8,128)S(1)}, f32[128,128]{1,0:T(8,128)S(1)}, u32[]{:S(2)}, u32[]{:S(2)}) %collective-permute-start.8) | collective-permute-done | bytes 65568 | tf_op jit(solution)/shard_map/ppermute | solution.py:317
  48.1 3.2 %collective-permute-start.9 = (f32[128,128]{1,0:T(8,128)S(1)}, f32[128,128]{1,0:T(8,128)S(1)}, u32[]{:S(2)}, u32[]{:S(2)}) collective-permute-start(f32[128,128]{1,0:T(8,128)S(1)} %add.14), channel_id=1, source_target_pairs={{0,8},{1,9},{2,10},{3,11},{4,12},{5,13},{6,14},{7,15},{8,0},{9,1},... | collective-permute-start | bytes 196616 | tf_op jit(solution)/shard_map/ppermute | solution.py:317
  51.3 2.2 %collective-permute-done.9 = f32[128,128]{1,0:T(8,128)S(1)} collective-permute-done((f32[128,128]{1,0:T(8,128)S(1)}, f32[128,128]{1,0:T(8,128)S(1)}, u32[]{:S(2)}, u32[]{:S(2)}) %collective-permute-start.9) | collective-permute-done | bytes 65568 | tf_op jit(solution)/shard_map/ppermute | solution.py:317
  53.6 1.2 %collective-permute-done.10.other = f32[128,128]{1,0:T(8,128)S(1)} collective-permute-done((f32[128,128]{1,0:T(8,128)S(1)}, f32[128,128]{1,0:T(8,128)S(1)}, u32[]{:S(2)}, u32[]{:S(2)}) %collective-permute-start.10) | collective-permute-done | bytes 65568 | tf_op jit(solution)/shard_map/ppermute | solution.py:317
  54.8 1.1 %shard_map.90 = (f32[16,16]{1,0:T(8,128)}, f32[128,128]{1,0:T(8,128)}, f32[128,128]{1,0:T(8,128)}, f32[128,128]{1,0:T(8,128)}) custom-call(f32[128,128]{1,0:T(8,128)S(1)} %add.15.mine, f32[128,128]{1,0:T(8,128)S(1)} %collective-permute-done.10.other), custom_call_target="tpu_custom_call" | custom-call | tf_op jit(solution)/shard_map/pallas_call | solution.py:385
  (21 shorter events, 0.3 us)
Async XLA Ops:
  0.6 8.5 %copy-start.2 = (bf16[128,64]{0,1:T(8,128)(2,1)S(1)}, bf16[128,64]{0,1:T(8,128)(2,1)}, u32[]{:S(2)}) copy-start(bf16[128,64]{0,1:T(8,128)(2,1)} %param.9) | copy-start | bytes 49156
  0.6 8.5 %copy-start.1 = (bf16[128,64]{0,1:T(8,128)(2,1)S(1)}, bf16[128,64]{0,1:T(8,128)(2,1)}, u32[]{:S(2)}) copy-start(bf16[128,64]{0,1:T(8,128)(2,1)} %param.8) | copy-start | bytes 49156
  0.7 8.5 %copy-start = (bf16[1,128,128,128]{3,2,1,0:T(8,128)(2,1)S(1)}, bf16[1,128,128,128]{3,2,1,0:T(8,128)(2,1)}, u32[]{:S(2)}) copy-start(bf16[1,128,128,128]{3,2,1,0:T(8,128)(2,1)} %param.5) | copy-start | bytes 12582916
  0.7 8.5 %copy-start.3 = (bf16[128,8]{0,1:T(8,128)(2,1)S(1)}, bf16[128,8]{0,1:T(8,128)(2,1)}, u32[]{:S(2)}) copy-start(bf16[128,8]{0,1:T(8,128)(2,1)} %param.7) | copy-start | bytes 6148
  3.5 14.1 %collective-permute-start.1 = (bf16[4,128,128]{2,1,0:T(8,128)(2,1)S(1)}, bf16[4,128,128]{2,1,0:T(8,128)(2,1)S(1)}, u32[]{:S(2)}, u32[]{:S(2)}) collective-permute-start(bf16[4,128,128]{2,1,0:T(8,128)(2,1)S(1)} %get-tuple-element.25), channel_id=1, source_target_pairs={{0,8},{1,9},{2,10},{3,11},{4,12},{5,13},{6,14},{7,15},{8,0},{9,1},... | collective-permute-start | bytes 393224 | tf_op jit(solution)/shard_map/ppermute | solution.py:317
  7.6 10.0 %collective-permute-start.2 = (bf16[4,128,128]{2,1,0:T(8,128)(2,1)S(1)}, bf16[4,128,128]{2,1,0:T(8,128)(2,1)S(1)}, u32[]{:S(2)}, u32[]{:S(2)}) collective-permute-start(bf16[4,128,128]{2,1,0:T(8,128)(2,1)S(1)} %get-tuple-element.26), channel_id=1, source_target_pairs={{0,12},{1,13},{2,14},{3,15},{4,8},{5,9},{6,10},{7,11},{8,4},{9,5},... | collective-permute-start | bytes 393224 | tf_op jit(solution)/shard_map/ppermute | solution.py:317
  8.9 9.1 %collective-permute-start = (bf16[4,128,128]{2,1,0:T(8,128)(2,1)S(1)}, bf16[4,128,128]{2,1,0:T(8,128)(2,1)S(1)}, u32[]{:S(2)}, u32[]{:S(2)}) collective-permute-start(bf16[4,128,128]{2,1,0:T(8,128)(2,1)S(1)} %get-tuple-element.24), channel_id=1, source_target_pairs={{0,4},{1,5},{2,6},{3,7},{4,0},{5,1},{6,2},{7,3},{8,12},{9,13},{10,... | collective-permute-start | bytes 393224 | tf_op jit(solution)/shard_map/ppermute | solution.py:317
  12.3 24.0 %all-to-all-start = ((bf16[16,192,128]{2,1,0:T(8,128)(2,1)}), bf16[16,192,128]{2,1,0:T(8,128)(2,1)S(1)}, u32[]{:S(2)}, u32[]{:S(2)}) async-start(bf16[16,192,128]{2,1,0:T(8,128)(2,1)} %shard_map.88), calls=%async_computation | async-start | bytes 1572864 | tf_op jit(solution)/shard_map/all_to_all | solution.py:362
  17.6 14.6 %copy-start.4 = (bf16[16,8]{0,1:T(8,128)(2,1)S(1)}, bf16[16,8]{0,1:T(8,128)(2,1)}, u32[]{:S(2)}) copy-start(bf16[16,8]{0,1:T(8,128)(2,1)} %param.6) | copy-start | bytes 772
  18.1 1.9 %collective-permute-start.3 = (bf16[4,128,128]{2,1,0:T(8,128)(2,1)S(1)}, bf16[4,128,128]{2,1,0:T(8,128)(2,1)S(1)}, u32[]{:S(2)}, u32[]{:S(2)}) collective-permute-start(bf16[4,128,128]{2,1,0:T(8,128)(2,1)S(1)} %get-tuple-element.32), channel_id=1, source_target_pairs={{0,1},{1,0},{2,3},{3,2},{4,5},{5,4},{6,7},{7,6},{8,9},{9,8},{10,11... | collective-permute-start | bytes 393224 | tf_op jit(solution)/shard_map/ppermute | solution.py:317
  18.2 12.0 %collective-permute-start.4 = (bf16[4,128,128]{2,1,0:T(8,128)(2,1)S(1)}, bf16[4,128,128]{2,1,0:T(8,128)(2,1)S(1)}, u32[]{:S(2)}, u32[]{:S(2)}) collective-permute-start(bf16[4,128,128]{2,1,0:T(8,128)(2,1)S(1)} %get-tuple-element.33), channel_id=1, source_target_pairs={{0,2},{1,3},{2,0},{3,1},{4,6},{5,7},{6,4},{7,5},{8,10},{9,11},{10,... | collective-permute-start | bytes 393224 | tf_op jit(solution)/shard_map/ppermute | solution.py:317
  19.8 12.3 %collective-permute-start.5 = (bf16[4,128,128]{2,1,0:T(8,128)(2,1)S(1)}, bf16[4,128,128]{2,1,0:T(8,128)(2,1)S(1)}, u32[]{:S(2)}, u32[]{:S(2)}) collective-permute-start(bf16[4,128,128]{2,1,0:T(8,128)(2,1)S(1)} %get-tuple-element.34), channel_id=1, source_target_pairs={{0,3},{1,2},{2,1},{3,0},{4,7},{5,6},{6,5},{7,4},{8,11},{9,10},{10,... | collective-permute-start | bytes 393224 | tf_op jit(solution)/shard_map/ppermute | solution.py:317
  37.4 1.3 %collective-permute-start.6 = (f32[128,128]{1,0:T(8,128)S(1)}, f32[128,128]{1,0:T(8,128)S(1)}, u32[]{:S(2)}, u32[]{:S(2)}) collective-permute-start(f32[128,128]{1,0:T(8,128)S(1)} %get-tuple-element.41), channel_id=1, source_target_pairs={{0,1},{1,0},{2,3},{3,2},{4,5},{5,4},{6,7},{7,6},{8,9},{9,8},{10,11... | collective-permute-start | bytes 196616 | tf_op jit(solution)/shard_map/ppermute | solution.py:317
  38.8 4.3 %collective-permute-start.7 = (f32[128,128]{1,0:T(8,128)S(1)}, f32[128,128]{1,0:T(8,128)S(1)}, u32[]{:S(2)}, u32[]{:S(2)}) collective-permute-start(f32[128,128]{1,0:T(8,128)S(1)} %add.12), channel_id=1, source_target_pairs={{0,2},{1,3},{2,0},{3,1},{4,6},{5,7},{6,4},{7,5},{8,10},{9,11},{10,... | collective-permute-start | bytes 196616 | tf_op jit(solution)/shard_map/ppermute | solution.py:317
  43.1 5.0 %collective-permute-start.8 = (f32[128,128]{1,0:T(8,128)S(1)}, f32[128,128]{1,0:T(8,128)S(1)}, u32[]{:S(2)}, u32[]{:S(2)}) collective-permute-start(f32[128,128]{1,0:T(8,128)S(1)} %add.13), channel_id=1, source_target_pairs={{0,4},{1,5},{2,6},{3,7},{4,0},{5,1},{6,2},{7,3},{8,12},{9,13},{10,... | collective-permute-start | bytes 196616 | tf_op jit(solution)/shard_map/ppermute | solution.py:317
  48.1 5.4 %collective-permute-start.9 = (f32[128,128]{1,0:T(8,128)S(1)}, f32[128,128]{1,0:T(8,128)S(1)}, u32[]{:S(2)}, u32[]{:S(2)}) collective-permute-start(f32[128,128]{1,0:T(8,128)S(1)} %add.14), channel_id=1, source_target_pairs={{0,8},{1,9},{2,10},{3,11},{4,12},{5,13},{6,14},{7,15},{8,0},{9,1},... | collective-permute-start | bytes 196616 | tf_op jit(solution)/shard_map/ppermute | solution.py:317
  53.5 1.3 %collective-permute-start.10 = (f32[128,128]{1,0:T(8,128)S(1)}, f32[128,128]{1,0:T(8,128)S(1)}, u32[]{:S(2)}, u32[]{:S(2)}) collective-permute-start(f32[128,128]{1,0:T(8,128)S(1)} %add.15.mine), channel_id=1, source_target_pairs={{0,1},{1,0},{2,3},{3,2},{4,5},{5,4},{6,7},{7,6},{8,9},{9,8},{10,11... | collective-permute-start | bytes 196616 | tf_op jit(solution)/shard_map/ppermute | solution.py:317

commit v7 on v6

--- a/solution.py
+++ b/solution.py
@@ -41,7 +41,7 @@
 
 
 def early_cubes(early, own, slab, dt_in, vt_in, *refs):
-    *first, kept, dt, vt, images, right, arrived, ready = refs
+    *first, kept, dt2, vt2, dd, dt, vt, images, right, arrived, ready = refs
     pixels = slab.shape[1]
     plane, rank = first[0].shape[0], dt.shape[0]
     pitch = early + 1
@@ -55,11 +55,12 @@
         copy.start()
     for copy in factors:
         copy.wait()
-    vt2, dd = paired(slot_order(vt[...], own)), paired(dt[...].T)
+    dt2[...], vt2[...] = (paired(slot_order(x[...], own)) for x in (dt, vt))
+    dd[...] = paired(dt[...].T)
     for at, copy in enumerate(copies):
         copy.wait()
         for c in range(cuts[at], cuts[at + 1], 4):
-            rights = dot(vt2, four_images(images, c), LAST)
+            rights = dot(vt2[...], four_images(images, c), LAST)
             for i in range(2):
                 for j in range(2):
                     right[pl.ds(c + 2 * i + j, rank, stride=pitch), :] = rights[
@@ -72,7 +73,7 @@
             x = [right[pl.ds((b + k) * pitch, early), :] for k in range(2)]
             x = jnp.concatenate(x, axis=1).astype(BF16)
             kept[b // 2] = x
-            to[pl.ds(h * early, early), :] = dot(x, dd).astype(BF16)
+            to[pl.ds(h * early, early), :] = dot(x, dd[...]).astype(BF16)
 
 
 def slot_order(factor, own):
@@ -83,16 +84,15 @@
     return dot(take.astype(BF16), factor).astype(BF16)
 
 
-def late_cubes(own, images, cft, dt, vt, kept, out, right, left, second, sent):
-    cols, pixels, rank = images.shape[0], images.shape[1], dt.shape[0]
+def late_cubes(own, images, cft, dt2, vt2, dd, kept, out, right, left, second, sent):
+    cols, pixels, rank = images.shape[0], images.shape[1], dt2.shape[0] // 2
     early = kept.shape[1]
     late = cols - early
-    dt2, vt2 = (paired(slot_order(x[...], own)) for x in (dt, vt))
     for c in range(0, cols, 4):
         four = four_images(images, c)
-        lefts = dot(dt2, four)
+        lefts = dot(dt2[...], four)
         if c >= early:
-            rights = dot(vt2, four, LAST)
+            rights = dot(vt2[...], four, LAST)
         for i in range(2):
             for j in range(2):
                 at = c + 2 * i + j
@@ -103,7 +103,6 @@
                     right[pl.ds(at - early, rank, stride=late + 1), :] = rights[
                         j * rank : (j + 1) * rank, i * pixels : (i + 1) * pixels
                     ]
-    dd = paired(dt[...].T)
     pairs, pair = own // 2, 2 * SCAN_RANK
 
     def two(ref, b, count):
@@ -121,7 +120,7 @@
             x = two(right, b, late)
             y = two(left, b, cols)
             at = pairs * late + h * pair
-            second[slot, pl.ds(h * late, late), :] = dot(x, dd).astype(BF16)
+            second[slot, pl.ds(h * late, late), :] = dot(x, dd[...]).astype(BF16)
             x = jnp.concatenate([kept[b // 2], x], axis=0)
             second[slot, pl.ds(at, pair), :] = stacked(dot(cft[...], x))
             second[slot, pl.ds(at + pairs * pair, pair), :] = stacked(dot(cft[...], y))
@@ -138,12 +137,14 @@
     anywhere = pl.BlockSpec(memory_space=pl.ANY)
     in_vmem = pl.BlockSpec(memory_space=pltpu.VMEM)
     params = pltpu.CompilerParams(vmem_limit_bytes=56 << 20)
-    *first, kept = pl.pallas_call(
+    *first, kept, dt2, vt2, dd = pl.pallas_call(
         functools.partial(early_cubes, early, own),
         out_shape=[pltpu.VMEM((plane, own // 2 * early, pixels), BF16)] * (n // plane)
-        + [pltpu.VMEM((rank // 2, early, 2 * pixels), BF16)],
+        + [pltpu.VMEM((rank // 2, early, 2 * pixels), BF16)]
+        + [pltpu.VMEM((2 * rank, 2 * pixels), BF16)] * 2
+        + [pltpu.VMEM((2 * pixels, 2 * rank), BF16)],
         in_specs=[anywhere] * 3,
-        out_specs=[in_vmem] * (n // plane + 1),
+        out_specs=[in_vmem] * (n // plane + 4),
         scratch_shapes=[
             pltpu.VMEM(dt.shape, BF16),
             pltpu.VMEM(vt.shape, BF16),
@@ -159,7 +160,7 @@
     second = pl.pallas_call(
         functools.partial(late_cubes, own),
         out_shape=jax.ShapeDtypeStruct((n, height, pixels), BF16),
-        in_specs=[in_vmem] * 5,
+        in_specs=[in_vmem] * 6,
         out_specs=anywhere,
         scratch_shapes=[
             pltpu.VMEM((rank * (late + 1), pixels), F32),
@@ -168,7 +169,7 @@
             pltpu.SemaphoreType.DMA((n,)),
         ],
         compiler_params=pltpu.CompilerParams(vmem_limit_bytes=32 << 20),
-    )(slab, cft, dt, vt, kept)
+    )(slab, cft, dt2, vt2, dd, kept)
     return first, second
 
 

time: 56.2 us -> 56.1 us (level)
  transfers between devices with their start and end apart: 12 -> 12, of which waited for: 9 -> 10; matrix products, arithmetic and copies ran while one was open for 0% -> 0% of each run, Pallas kernels for 7% -> 7%
where the time goes in v7:
time: 56.1 us; the launch traced here: 55.9 us
  waiting for transfers between devices  25.4 us (45%)
  starting transfers between devices  20.8 us (37%)
  Pallas kernels  8.94 us (16%)
  between operations  0.74 us (1%)
    ppermute x11, waiting for transfers between devices, swap(): return lax.ppermute(x, 'row', [(i, i ^ step) for i in range(n)])  22 us
    ppermute x11, starting transfers between devices, swap(): return lax.ppermute(x, 'row', [(i, i ^ step) for i in range(n)])  15.6 us
    all_to_all x1, starting transfers between devices, local(): lax.all_to_all(second, 'row', split_axis=0, concat_axis=0, tiled=True)  5.26 us
    all_to_all x1, waiting for transfers between devices, local(): lax.all_to_all(second, 'row', split_axis=0, concat_axis=0, tiled=True)  3.31 us
    pallas_call x1, Pallas kernels, projections(): pl.pallas_call(functools.partial(late_cubes, own), out_shape=jax.ShapeDty...  3.05 us
    pallas_call x1, Pallas kernels, projections(): pl.pallas_call(functools.partial(early_cubes, early, own), out_shape=[plt...  2.78 us
    pallas_call x4, Pallas kernels, call(): pl.pallas_call(kernel, out_shape=[jax.ShapeDtypeStruct(*out) for out in o...  1.98 us
  transfers between devices with their start and end apart: 12, of which 10 were waited for; matrix products, arithmetic and copies ran while one was open for 0% of the time, Pallas kernels for 7%

profile of v7, /device:TPU:0, one launch (start us, length us, event | category | flops | bytes accessed | tf_op | source)
XLA Modules:
  0.0 55.9 jit_solution(18134849255676856812)
XLA Ops:
  0.7 2.8 %shard_map.84 = (bf16[4,128,128]{2,1,0:T(8,128)(2,1)S(1)}, bf16[4,128,128]{2,1,0:T(8,128)(2,1)S(1)}, bf16[4,128,128]{2,1,0:T(8,128)(2,1)S(1)}, bf16[4,128,128]{2...) custom-call(bf16[128,128,128]{2,1,0:T(8,128)(2,1)} %bitcast.5, ...), custom_call_target="tpu_custom_call" | custom-call | tf_op jit(solution)/shard_map/pallas_call | solution.py:140
  3.4 4.1 %collective-permute-start.1 = (bf16[4,128,128]{2,1,0:T(8,128)(2,1)S(1)}, bf16[4,128,128]{2,1,0:T(8,128)(2,1)S(1)}, u32[]{:S(2)}, u32[]{:S(2)}) collective-permute-start(bf16[4,128,128]{2,1,0:T(8,128)(2,1)S(1)} %get-tuple-element.28), channel_id=1, source_target_pairs={{0,8},{1,9},{2,10},{3,11},{4,12},{5,13},{6,14},{7,15},{8,0},{9,1},... | collective-permute-start | bytes 393224 | tf_op jit(solution)/shard_map/ppermute | solution.py:318
  7.5 1.3 %collective-permute-start.2 = (bf16[4,128,128]{2,1,0:T(8,128)(2,1)S(1)}, bf16[4,128,128]{2,1,0:T(8,128)(2,1)S(1)}, u32[]{:S(2)}, u32[]{:S(2)}) collective-permute-start(bf16[4,128,128]{2,1,0:T(8,128)(2,1)S(1)} %get-tuple-element.29), channel_id=1, source_target_pairs={{0,12},{1,13},{2,14},{3,15},{4,8},{5,9},{6,10},{7,11},{8,4},{9,5},... | collective-permute-start | bytes 393224 | tf_op jit(solution)/shard_map/ppermute | solution.py:318
  8.9 0.2 collective-permute-start
  9.1 3.1 %shard_map.88 = bf16[16,192,128]{2,1,0:T(8,128)(2,1)} custom-call(bf16[128,128,128]{2,1,0:T(8,128)(2,1)S(1)} %bitcast.6, bf16[8,128]{1,0:T(8,128)(2,1)S(1)} %bitcast.7, bf16[128,256]{1,0:T(8,128)(2,1)S(1)} %get-tuple-element.42.dt2, bf16[128,256]{1,0:T(8,128)(2,1)S(1)} %get-tuple-element.43.vt2, bf16[256,128]{1,0:T(8,128)(2,1)S(1)} %get-tuple-element.44.dd, ...), custom_call_target="tpu_custom_call" | custom-call | tf_op jit(solution)/shard_map/pallas_call | solution.py:160
  12.2 5.3 %all-to-all-start = ((bf16[16,192,128]{2,1,0:T(8,128)(2,1)}), bf16[16,192,128]{2,1,0:T(8,128)(2,1)S(1)}, u32[]{:S(2)}, u32[]{:S(2)}) async-start(bf16[16,192,128]{2,1,0:T(8,128)(2,1)} %shard_map.88), calls=%async_computation | async-start | bytes 1572864 | tf_op jit(solution)/shard_map/all_to_all | solution.py:363
  17.6 0.5 collective-permute-done.refs_1_
  18.2 1.6 %collective-permute-start.4 = (bf16[4,128,128]{2,1,0:T(8,128)(2,1)S(1)}, bf16[4,128,128]{2,1,0:T(8,128)(2,1)S(1)}, u32[]{:S(2)}, u32[]{:S(2)}) collective-permute-start(bf16[4,128,128]{2,1,0:T(8,128)(2,1)S(1)} %get-tuple-element.36), channel_id=1, source_target_pairs={{0,2},{1,3},{2,0},{3,1},{4,6},{5,7},{6,4},{7,5},{8,10},{9,11},{10,... | collective-permute-start | bytes 393224 | tf_op jit(solution)/shard_map/ppermute | solution.py:318
  19.8 0.2 collective-permute-start.5
  20.0 10.0 %collective-permute-done.4.refs_2_ = bf16[4,128,128]{2,1,0:T(8,128)(2,1)S(1)} collective-permute-done((bf16[4,128,128]{2,1,0:T(8,128)(2,1)S(1)}, bf16[4,128,128]{2,1,0:T(8,128)(2,1)S(1)}, u32[]{:S(2)}, u32[]{:S(2)}) %collective-permute-start.4) | collective-permute-done | bytes 131104 | tf_op jit(solution)/shard_map/ppermute | solution.py:318
  30.0 2.0 %collective-permute-done.5.refs_3_ = bf16[4,128,128]{2,1,0:T(8,128)(2,1)S(1)} collective-permute-done((bf16[4,128,128]{2,1,0:T(8,128)(2,1)S(1)}, bf16[4,128,128]{2,1,0:T(8,128)(2,1)S(1)}, u32[]{:S(2)}, u32[]{:S(2)}) %collective-permute-start.5) | collective-permute-done | bytes 131104 | tf_op jit(solution)/shard_map/ppermute | solution.py:318
  32.0 0.8 %shard_map.87 = (bf16[128,256]{1,0:T(8,128)(2,1)S(1)}, bf16[8,64,256]{2,1,0:T(8,128)(2,1)S(1)}, f32[2,128,128]{2,1,0:T(8,128)S(1)}, f32[64,64]{1,0:T(8,128)S(1)}) custom-call(bf16[8,16]{1,0:T(8,128)(2,1)S(1)} %bitcast.10, bf16[8,128]{1,0:T(8,128)(2,1)S(1)} %bitcast.8, bf16[4,128,128]{2,1,0:T(8,128)(2,1)S(1)} %get-tuple-element.34.refs_0_, ...), custom_call_target="tpu_custom_call" | custom-call | flops 100000000 | bytes 1048576 | tf_op jit(solution)/shard_map/pallas_call | solution.py:308
  32.9 3.3 %all-to-all-done.second = bf16[16,192,128]{2,1,0:T(8,128)(2,1)S(1)} async-done(((bf16[16,192,128]{2,1,0:T(8,128)(2,1)}), bf16[16,192,128]{2,1,0:T(8,128)(2,1)S(1)}, u32[]{:S(2)}, u32[]{:S(2)}) %all-to-all-start) | async-done | bytes 786464 | tf_op jit(solution)/shard_map/all_to_all | solution.py:363
  36.2 1.1 %shard_map.89 = (f32[128,128]{1,0:T(8,128)S(1)}, f32[128,128]{1,0:T(8,128)S(1)}) custom-call(bf16[8,128]{1,0:T(8,128)(2,1)S(1)} %bitcast.9, bf16[128,256]{1,0:T(8,128)(2,1)S(1)} %get-tuple-element.38.plain, bf16[8,64,256]{2,1,0:T(8,128)(2,1)S(1)} %get-tuple-element.39.early_unfold, f32[2,128,128]{2,1,0:T(8,128)S(1)} %get-tuple-element.40.rowpart, ...), custom_call_target="tpu_custom_call" | custom-call | flops 100000000 | bytes 1048576 | tf_op jit(solution)/shard_map/pallas_call | solution.py:308
  37.3 0.3 collective-permute-start.6
  37.6 1.0 %collective-permute-done.6 = f32[128,128]{1,0:T(8,128)S(1)} collective-permute-done((f32[128,128]{1,0:T(8,128)S(1)}, f32[128,128]{1,0:T(8,128)S(1)}, u32[]{:S(2)}, u32[]{:S(2)}) %collective-permute-start.6) | collective-permute-done | bytes 65568 | tf_op jit(solution)/shard_map/ppermute | solution.py:318
  38.6 1.6 %collective-permute-start.7 = (f32[128,128]{1,0:T(8,128)S(1)}, f32[128,128]{1,0:T(8,128)S(1)}, u32[]{:S(2)}, u32[]{:S(2)}) collective-permute-start(f32[128,128]{1,0:T(8,128)S(1)} %add.12), channel_id=1, source_target_pairs={{0,2},{1,3},{2,0},{3,1},{4,6},{5,7},{6,4},{7,5},{8,10},{9,11},{10,... | collective-permute-start | bytes 196616 | tf_op jit(solution)/shard_map/ppermute | solution.py:318
  40.2 2.7 %collective-permute-done.7 = f32[128,128]{1,0:T(8,128)S(1)} collective-permute-done((f32[128,128]{1,0:T(8,128)S(1)}, f32[128,128]{1,0:T(8,128)S(1)}, u32[]{:S(2)}, u32[]{:S(2)}) %collective-permute-start.7) | collective-permute-done | bytes 65568 | tf_op jit(solution)/shard_map/ppermute | solution.py:318
  43.0 2.7 %collective-permute-start.8 = (f32[128,128]{1,0:T(8,128)S(1)}, f32[128,128]{1,0:T(8,128)S(1)}, u32[]{:S(2)}, u32[]{:S(2)}) collective-permute-start(f32[128,128]{1,0:T(8,128)S(1)} %add.13), channel_id=1, source_target_pairs={{0,4},{1,5},{2,6},{3,7},{4,0},{5,1},{6,2},{7,3},{8,12},{9,13},{10,... | collective-permute-start | bytes 196616 | tf_op jit(solution)/shard_map/ppermute | solution.py:318
  45.7 2.2 %collective-permute-done.8 = f32[128,128]{1,0:T(8,128)S(1)} collective-permute-done((f32[128,128]{1,0:T(8,128)S(1)}, f32[128,128]{1,0:T(8,128)S(1)}, u32[]{:S(2)}, u32[]{:S(2)}) %collective-permute-start.8) | collective-permute-done | bytes 65568 | tf_op jit(solution)/shard_map/ppermute | solution.py:318
  48.0 3.3 %collective-permute-start.9 = (f32[128,128]{1,0:T(8,128)S(1)}, f32[128,128]{1,0:T(8,128)S(1)}, u32[]{:S(2)}, u32[]{:S(2)}) collective-permute-start(f32[128,128]{1,0:T(8,128)S(1)} %add.14), channel_id=1, source_target_pairs={{0,8},{1,9},{2,10},{3,11},{4,12},{5,13},{6,14},{7,15},{8,0},{9,1},... | collective-permute-start | bytes 196616 | tf_op jit(solution)/shard_map/ppermute | solution.py:318
  51.2 2.2 %collective-permute-done.9 = f32[128,128]{1,0:T(8,128)S(1)} collective-permute-done((f32[128,128]{1,0:T(8,128)S(1)}, f32[128,128]{1,0:T(8,128)S(1)}, u32[]{:S(2)}, u32[]{:S(2)}) %collective-permute-start.9) | collective-permute-done | bytes 65568 | tf_op jit(solution)/shard_map/ppermute | solution.py:318
  53.6 1.2 %collective-permute-done.10.other = f32[128,128]{1,0:T(8,128)S(1)} collective-permute-done((f32[128,128]{1,0:T(8,128)S(1)}, f32[128,128]{1,0:T(8,128)S(1)}, u32[]{:S(2)}, u32[]{:S(2)}) %collective-permute-start.10) | collective-permute-done | bytes 65568 | tf_op jit(solution)/shard_map/ppermute | solution.py:318
  54.8 1.1 %shard_map.90 = (f32[16,16]{1,0:T(8,128)}, f32[128,128]{1,0:T(8,128)}, f32[128,128]{1,0:T(8,128)}, f32[128,128]{1,0:T(8,128)}) custom-call(f32[128,128]{1,0:T(8,128)S(1)} %add.15.mine, f32[128,128]{1,0:T(8,128)S(1)} %collective-permute-done.10.other), custom_call_target="tpu_custom_call" | custom-call | tf_op jit(solution)/shard_map/pallas_call | solution.py:386
  (17 shorter events, 0.3 us)
Async XLA Ops:
  0.6 8.5 %copy-start = (bf16[1,128,128,128]{3,2,1,0:T(8,128)(2,1)S(1)}, bf16[1,128,128,128]{3,2,1,0:T(8,128)(2,1)}, u32[]{:S(2)}) copy-start(bf16[1,128,128,128]{3,2,1,0:T(8,128)(2,1)} %param.5) | copy-start | bytes 12582916
  0.6 8.5 %copy-start.1 = (bf16[128,8]{0,1:T(8,128)(2,1)S(1)}, bf16[128,8]{0,1:T(8,128)(2,1)}, u32[]{:S(2)}) copy-start(bf16[128,8]{0,1:T(8,128)(2,1)} %param.7) | copy-start | bytes 6148
  3.4 14.1 %collective-permute-start.1 = (bf16[4,128,128]{2,1,0:T(8,128)(2,1)S(1)}, bf16[4,128,128]{2,1,0:T(8,128)(2,1)S(1)}, u32[]{:S(2)}, u32[]{:S(2)}) collective-permute-start(bf16[4,128,128]{2,1,0:T(8,128)(2,1)S(1)} %get-tuple-element.28), channel_id=1, source_target_pairs={{0,8},{1,9},{2,10},{3,11},{4,12},{5,13},{6,14},{7,15},{8,0},{9,1},... | collective-permute-start | bytes 393224 | tf_op jit(solution)/shard_map/ppermute | solution.py:318
  7.5 10.0 %collective-permute-start.2 = (bf16[4,128,128]{2,1,0:T(8,128)(2,1)S(1)}, bf16[4,128,128]{2,1,0:T(8,128)(2,1)S(1)}, u32[]{:S(2)}, u32[]{:S(2)}) collective-permute-start(bf16[4,128,128]{2,1,0:T(8,128)(2,1)S(1)} %get-tuple-element.29), channel_id=1, source_target_pairs={{0,12},{1,13},{2,14},{3,15},{4,8},{5,9},{6,10},{7,11},{8,4},{9,5},... | collective-permute-start | bytes 393224 | tf_op jit(solution)/shard_map/ppermute | solution.py:318
  8.9 9.1 %collective-permute-start = (bf16[4,128,128]{2,1,0:T(8,128)(2,1)S(1)}, bf16[4,128,128]{2,1,0:T(8,128)(2,1)S(1)}, u32[]{:S(2)}, u32[]{:S(2)}) collective-permute-start(bf16[4,128,128]{2,1,0:T(8,128)(2,1)S(1)} %get-tuple-element.27), channel_id=1, source_target_pairs={{0,4},{1,5},{2,6},{3,7},{4,0},{5,1},{6,2},{7,3},{8,12},{9,13},{10,... | collective-permute-start | bytes 393224 | tf_op jit(solution)/shard_map/ppermute | solution.py:318
  12.2 24.0 %all-to-all-start = ((bf16[16,192,128]{2,1,0:T(8,128)(2,1)}), bf16[16,192,128]{2,1,0:T(8,128)(2,1)S(1)}, u32[]{:S(2)}, u32[]{:S(2)}) async-start(bf16[16,192,128]{2,1,0:T(8,128)(2,1)} %shard_map.88), calls=%async_computation | async-start | bytes 1572864 | tf_op jit(solution)/shard_map/all_to_all | solution.py:363
  17.5 14.6 %copy-start.2 = (bf16[16,8]{0,1:T(8,128)(2,1)S(1)}, bf16[16,8]{0,1:T(8,128)(2,1)}, u32[]{:S(2)}) copy-start(bf16[16,8]{0,1:T(8,128)(2,1)} %param.6) | copy-start | bytes 772
  18.1 1.9 %collective-permute-start.3 = (bf16[4,128,128]{2,1,0:T(8,128)(2,1)S(1)}, bf16[4,128,128]{2,1,0:T(8,128)(2,1)S(1)}, u32[]{:S(2)}, u32[]{:S(2)}) collective-permute-start(bf16[4,128,128]{2,1,0:T(8,128)(2,1)S(1)} %get-tuple-element.35), channel_id=1, source_target_pairs={{0,1},{1,0},{2,3},{3,2},{4,5},{5,4},{6,7},{7,6},{8,9},{9,8},{10,11... | collective-permute-start | bytes 393224 | tf_op jit(solution)/shard_map/ppermute | solution.py:318
  18.2 11.9 %collective-permute-start.4 = (bf16[4,128,128]{2,1,0:T(8,128)(2,1)S(1)}, bf16[4,128,128]{2,1,0:T(8,128)(2,1)S(1)}, u32[]{:S(2)}, u32[]{:S(2)}) collective-permute-start(bf16[4,128,128]{2,1,0:T(8,128)(2,1)S(1)} %get-tuple-element.36), channel_id=1, source_target_pairs={{0,2},{1,3},{2,0},{3,1},{4,6},{5,7},{6,4},{7,5},{8,10},{9,11},{10,... | collective-permute-start | bytes 393224 | tf_op jit(solution)/shard_map/ppermute | solution.py:318
  19.8 12.2 %collective-permute-start.5 = (bf16[4,128,128]{2,1,0:T(8,128)(2,1)S(1)}, bf16[4,128,128]{2,1,0:T(8,128)(2,1)S(1)}, u32[]{:S(2)}, u32[]{:S(2)}) collective-permute-start(bf16[4,128,128]{2,1,0:T(8,128)(2,1)S(1)} %get-tuple-element.37), channel_id=1, source_target_pairs={{0,3},{1,2},{2,1},{3,0},{4,7},{5,6},{6,5},{7,4},{8,11},{9,10},{10,... | collective-permute-start | bytes 393224 | tf_op jit(solution)/shard_map/ppermute | solution.py:318
  37.3 1.3 %collective-permute-start.6 = (f32[128,128]{1,0:T(8,128)S(1)}, f32[128,128]{1,0:T(8,128)S(1)}, u32[]{:S(2)}, u32[]{:S(2)}) collective-permute-start(f32[128,128]{1,0:T(8,128)S(1)} %get-tuple-element.47), channel_id=1, source_target_pairs={{0,1},{1,0},{2,3},{3,2},{4,5},{5,4},{6,7},{7,6},{8,9},{9,8},{10,11... | collective-permute-start | bytes 196616 | tf_op jit(solution)/shard_map/ppermute | solution.py:318
  38.6 4.3 %collective-permute-start.7 = (f32[128,128]{1,0:T(8,128)S(1)}, f32[128,128]{1,0:T(8,128)S(1)}, u32[]{:S(2)}, u32[]{:S(2)}) collective-permute-start(f32[128,128]{1,0:T(8,128)S(1)} %add.12), channel_id=1, source_target_pairs={{0,2},{1,3},{2,0},{3,1},{4,6},{5,7},{6,4},{7,5},{8,10},{9,11},{10,... | collective-permute-start | bytes 196616 | tf_op jit(solution)/shard_map/ppermute | solution.py:318
  43.0 5.0 %collective-permute-start.8 = (f32[128,128]{1,0:T(8,128)S(1)}, f32[128,128]{1,0:T(8,128)S(1)}, u32[]{:S(2)}, u32[]{:S(2)}) collective-permute-start(f32[128,128]{1,0:T(8,128)S(1)} %add.13), channel_id=1, source_target_pairs={{0,4},{1,5},{2,6},{3,7},{4,0},{5,1},{6,2},{7,3},{8,12},{9,13},{10,... | collective-permute-start | bytes 196616 | tf_op jit(solution)/shard_map/ppermute | solution.py:318
  48.0 5.5 %collective-permute-start.9 = (f32[128,128]{1,0:T(8,128)S(1)}, f32[128,128]{1,0:T(8,128)S(1)}, u32[]{:S(2)}, u32[]{:S(2)}) collective-permute-start(f32[128,128]{1,0:T(8,128)S(1)} %add.14), channel_id=1, source_target_pairs={{0,8},{1,9},{2,10},{3,11},{4,12},{5,13},{6,14},{7,15},{8,0},{9,1},... | collective-permute-start | bytes 196616 | tf_op jit(solution)/shard_map/ppermute | solution.py:318
  53.5 1.3 %collective-permute-start.10 = (f32[128,128]{1,0:T(8,128)S(1)}, f32[128,128]{1,0:T(8,128)S(1)}, u32[]{:S(2)}, u32[]{:S(2)}) collective-permute-start(f32[128,128]{1,0:T(8,128)S(1)} %add.15.mine), channel_id=1, source_target_pairs={{0,1},{1,0},{2,3},{3,2},{4,5},{5,4},{6,7},{7,6},{8,9},{9,8},{10,11... | collective-permute-start | bytes 196616 | tf_op jit(solution)/shard_map/ppermute | solution.py:318

commit v8 on v7

--- a/solution.py
+++ b/solution.py
@@ -121,8 +121,8 @@
             y = two(left, b, cols)
             at = pairs * late + h * pair
             second[slot, pl.ds(h * late, late), :] = dot(x, dd[...]).astype(BF16)
-            x = jnp.concatenate([kept[b // 2], x], axis=0)
-            second[slot, pl.ds(at, pair), :] = stacked(dot(cft[...], x))
+            sums = dot(cft[:, :early], kept[b // 2]) + dot(cft[:, early:], x)
+            second[slot, pl.ds(at, pair), :] = stacked(sums)
             second[slot, pl.ds(at + pairs * pair, pair), :] = stacked(dot(cft[...], y))
         copies.append(pltpu.make_async_copy(second.at[slot], out.at[me ^ slot], sent.at[slot]))
         copies[-1].start()

time: 56.1 us -> 56.1 us (level)
  no operation moved by 1% of the time
where the time goes in v8:
time: 56.1 us; the launch traced here: 55.9 us
  waiting for transfers between devices  25.3 us (45%)
  starting transfers between devices  20.8 us (37%)
  Pallas kernels  8.95 us (16%)
  between operations  0.74 us (1%)
    ppermute x11, waiting for transfers between devices, swap(): return lax.ppermute(x, 'row', [(i, i ^ step) for i in range(n)])  22 us
    ppermute x11, starting transfers between devices, swap(): return lax.ppermute(x, 'row', [(i, i ^ step) for i in range(n)])  15.6 us
    all_to_all x1, starting transfers between devices, local(): lax.all_to_all(second, 'row', split_axis=0, concat_axis=0, tiled=True)  5.26 us
    all_to_all x1, waiting for transfers between devices, local(): lax.all_to_all(second, 'row', split_axis=0, concat_axis=0, tiled=True)  3.31 us
    pallas_call x1, Pallas kernels, projections(): pl.pallas_call(functools.partial(late_cubes, own), out_shape=jax.ShapeDty...  3.06 us
    pallas_call x1, Pallas kernels, projections(): pl.pallas_call(functools.partial(early_cubes, early, own), out_shape=[plt...  2.78 us
    pallas_call x4, Pallas kernels, call(): pl.pallas_call(kernel, out_shape=[jax.ShapeDtypeStruct(*out) for out in o...  1.98 us
  transfers between devices with their start and end apart: 12, of which 10 were waited for; matrix products, arithmetic and copies ran while one was open for 0% of the time, Pallas kernels for 7%

profile of v8, /device:TPU:0, one launch (start us, length us, event | category | flops | bytes accessed | tf_op | source)
XLA Modules:
  0.0 55.9 jit_solution(17816711553772733828)
XLA Ops:
  0.7 2.8 %shard_map.84 = (bf16[4,128,128]{2,1,0:T(8,128)(2,1)S(1)}, bf16[4,128,128]{2,1,0:T(8,128)(2,1)S(1)}, bf16[4,128,128]{2,1,0:T(8,128)(2,1)S(1)}, bf16[4,128,128]{2...) custom-call(bf16[128,128,128]{2,1,0:T(8,128)(2,1)} %bitcast.5, ...), custom_call_target="tpu_custom_call" | custom-call | tf_op jit(solution)/shard_map/pallas_call | solution.py:140
  3.4 4.1 %collective-permute-start.1 = (bf16[4,128,128]{2,1,0:T(8,128)(2,1)S(1)}, bf16[4,128,128]{2,1,0:T(8,128)(2,1)S(1)}, u32[]{:S(2)}, u32[]{:S(2)}) collective-permute-start(bf16[4,128,128]{2,1,0:T(8,128)(2,1)S(1)} %get-tuple-element.28), channel_id=1, source_target_pairs={{0,8},{1,9},{2,10},{3,11},{4,12},{5,13},{6,14},{7,15},{8,0},{9,1},... | collective-permute-start | bytes 393224 | tf_op jit(solution)/shard_map/ppermute | solution.py:318
  7.5 1.3 %collective-permute-start.2 = (bf16[4,128,128]{2,1,0:T(8,128)(2,1)S(1)}, bf16[4,128,128]{2,1,0:T(8,128)(2,1)S(1)}, u32[]{:S(2)}, u32[]{:S(2)}) collective-permute-start(bf16[4,128,128]{2,1,0:T(8,128)(2,1)S(1)} %get-tuple-element.29), channel_id=1, source_target_pairs={{0,12},{1,13},{2,14},{3,15},{4,8},{5,9},{6,10},{7,11},{8,4},{9,5},... | collective-permute-start | bytes 393224 | tf_op jit(solution)/shard_map/ppermute | solution.py:318
  8.9 0.2 collective-permute-start
  9.1 3.1 %shard_map.88 = bf16[16,192,128]{2,1,0:T(8,128)(2,1)} custom-call(bf16[128,128,128]{2,1,0:T(8,128)(2,1)S(1)} %bitcast.6, bf16[8,128]{1,0:T(8,128)(2,1)S(1)} %bitcast.7, bf16[128,256]{1,0:T(8,128)(2,1)S(1)} %get-tuple-element.42.dt2, bf16[128,256]{1,0:T(8,128)(2,1)S(1)} %get-tuple-element.43.vt2, bf16[256,128]{1,0:T(8,128)(2,1)S(1)} %get-tuple-element.44.dd, ...), custom_call_target="tpu_custom_call" | custom-call | tf_op jit(solution)/shard_map/pallas_call | solution.py:160
  12.2 5.3 %all-to-all-start = ((bf16[16,192,128]{2,1,0:T(8,128)(2,1)}), bf16[16,192,128]{2,1,0:T(8,128)(2,1)S(1)}, u32[]{:S(2)}, u32[]{:S(2)}) async-start(bf16[16,192,128]{2,1,0:T(8,128)(2,1)} %shard_map.88), calls=%async_computation | async-start | bytes 1572864 | tf_op jit(solution)/shard_map/all_to_all | solution.py:363
  17.6 0.5 collective-permute-done.refs_1_
  18.2 1.6 %collective-permute-start.4 = (bf16[4,128,128]{2,1,0:T(8,128)(2,1)S(1)}, bf16[4,128,128]{2,1,0:T(8,128)(2,1)S(1)}, u32[]{:S(2)}, u32[]{:S(2)}) collective-permute-start(bf16[4,128,128]{2,1,0:T(8,128)(2,1)S(1)} %get-tuple-element.36), channel_id=1, source_target_pairs={{0,2},{1,3},{2,0},{3,1},{4,6},{5,7},{6,4},{7,5},{8,10},{9,11},{10,... | collective-permute-start | bytes 393224 | tf_op jit(solution)/shard_map/ppermute | solution.py:318
  19.8 0.2 collective-permute-start.5
  20.0 10.0 %collective-permute-done.4.refs_2_ = bf16[4,128,128]{2,1,0:T(8,128)(2,1)S(1)} collective-permute-done((bf16[4,128,128]{2,1,0:T(8,128)(2,1)S(1)}, bf16[4,128,128]{2,1,0:T(8,128)(2,1)S(1)}, u32[]{:S(2)}, u32[]{:S(2)}) %collective-permute-start.4) | collective-permute-done | bytes 131104 | tf_op jit(solution)/shard_map/ppermute | solution.py:318
  30.0 2.0 %collective-permute-done.5.refs_3_ = bf16[4,128,128]{2,1,0:T(8,128)(2,1)S(1)} collective-permute-done((bf16[4,128,128]{2,1,0:T(8,128)(2,1)S(1)}, bf16[4,128,128]{2,1,0:T(8,128)(2,1)S(1)}, u32[]{:S(2)}, u32[]{:S(2)}) %collective-permute-start.5) | collective-permute-done | bytes 131104 | tf_op jit(solution)/shard_map/ppermute | solution.py:318
  32.1 0.8 %shard_map.87 = (bf16[128,256]{1,0:T(8,128)(2,1)S(1)}, bf16[8,64,256]{2,1,0:T(8,128)(2,1)S(1)}, f32[2,128,128]{2,1,0:T(8,128)S(1)}, f32[64,64]{1,0:T(8,128)S(1)}) custom-call(bf16[8,16]{1,0:T(8,128)(2,1)S(1)} %bitcast.10, bf16[8,128]{1,0:T(8,128)(2,1)S(1)} %bitcast.8, bf16[4,128,128]{2,1,0:T(8,128)(2,1)S(1)} %get-tuple-element.34.refs_0_, ...), custom_call_target="tpu_custom_call" | custom-call | flops 100000000 | bytes 1048576 | tf_op jit(solution)/shard_map/pallas_call | solution.py:308
  32.9 3.3 %all-to-all-done.second = bf16[16,192,128]{2,1,0:T(8,128)(2,1)S(1)} async-done(((bf16[16,192,128]{2,1,0:T(8,128)(2,1)}), bf16[16,192,128]{2,1,0:T(8,128)(2,1)S(1)}, u32[]{:S(2)}, u32[]{:S(2)}) %all-to-all-start) | async-done | bytes 786464 | tf_op jit(solution)/shard_map/all_to_all | solution.py:363
  36.2 1.1 %shard_map.89 = (f32[128,128]{1,0:T(8,128)S(1)}, f32[128,128]{1,0:T(8,128)S(1)}) custom-call(bf16[8,128]{1,0:T(8,128)(2,1)S(1)} %bitcast.9, bf16[128,256]{1,0:T(8,128)(2,1)S(1)} %get-tuple-element.38.plain, bf16[8,64,256]{2,1,0:T(8,128)(2,1)S(1)} %get-tuple-element.39.early_unfold, f32[2,128,128]{2,1,0:T(8,128)S(1)} %get-tuple-element.40.rowpart, ...), custom_call_target="tpu_custom_call" | custom-call | flops 100000000 | bytes 1048576 | tf_op jit(solution)/shard_map/pallas_call | solution.py:308
  37.3 0.3 collective-permute-start.6
  37.6 1.0 %collective-permute-done.6 = f32[128,128]{1,0:T(8,128)S(1)} collective-permute-done((f32[128,128]{1,0:T(8,128)S(1)}, f32[128,128]{1,0:T(8,128)S(1)}, u32[]{:S(2)}, u32[]{:S(2)}) %collective-permute-start.6) | collective-permute-done | bytes 65568 | tf_op jit(solution)/shard_map/ppermute | solution.py:318
  38.6 1.6 %collective-permute-start.7 = (f32[128,128]{1,0:T(8,128)S(1)}, f32[128,128]{1,0:T(8,128)S(1)}, u32[]{:S(2)}, u32[]{:S(2)}) collective-permute-start(f32[128,128]{1,0:T(8,128)S(1)} %add.12), channel_id=1, source_target_pairs={{0,2},{1,3},{2,0},{3,1},{4,6},{5,7},{6,4},{7,5},{8,10},{9,11},{10,... | collective-permute-start | bytes 196616 | tf_op jit(solution)/shard_map/ppermute | solution.py:318
  40.2 2.7 %collective-permute-done.7 = f32[128,128]{1,0:T(8,128)S(1)} collective-permute-done((f32[128,128]{1,0:T(8,128)S(1)}, f32[128,128]{1,0:T(8,128)S(1)}, u32[]{:S(2)}, u32[]{:S(2)}) %collective-permute-start.7) | collective-permute-done | bytes 65568 | tf_op jit(solution)/shard_map/ppermute | solution.py:318
  43.0 2.7 %collective-permute-start.8 = (f32[128,128]{1,0:T(8,128)S(1)}, f32[128,128]{1,0:T(8,128)S(1)}, u32[]{:S(2)}, u32[]{:S(2)}) collective-permute-start(f32[128,128]{1,0:T(8,128)S(1)} %add.13), channel_id=1, source_target_pairs={{0,4},{1,5},{2,6},{3,7},{4,0},{5,1},{6,2},{7,3},{8,12},{9,13},{10,... | collective-permute-start | bytes 196616 | tf_op jit(solution)/shard_map/ppermute | solution.py:318
  45.7 2.2 %collective-permute-done.8 = f32[128,128]{1,0:T(8,128)S(1)} collective-permute-done((f32[128,128]{1,0:T(8,128)S(1)}, f32[128,128]{1,0:T(8,128)S(1)}, u32[]{:S(2)}, u32[]{:S(2)}) %collective-permute-start.8) | collective-permute-done | bytes 65568 | tf_op jit(solution)/shard_map/ppermute | solution.py:318
  48.0 3.3 %collective-permute-start.9 = (f32[128,128]{1,0:T(8,128)S(1)}, f32[128,128]{1,0:T(8,128)S(1)}, u32[]{:S(2)}, u32[]{:S(2)}) collective-permute-start(f32[128,128]{1,0:T(8,128)S(1)} %add.14), channel_id=1, source_target_pairs={{0,8},{1,9},{2,10},{3,11},{4,12},{5,13},{6,14},{7,15},{8,0},{9,1},... | collective-permute-start | bytes 196616 | tf_op jit(solution)/shard_map/ppermute | solution.py:318
  51.2 2.2 %collective-permute-done.9 = f32[128,128]{1,0:T(8,128)S(1)} collective-permute-done((f32[128,128]{1,0:T(8,128)S(1)}, f32[128,128]{1,0:T(8,128)S(1)}, u32[]{:S(2)}, u32[]{:S(2)}) %collective-permute-start.9) | collective-permute-done | bytes 65568 | tf_op jit(solution)/shard_map/ppermute | solution.py:318
  53.6 1.2 %collective-permute-done.10.other = f32[128,128]{1,0:T(8,128)S(1)} collective-permute-done((f32[128,128]{1,0:T(8,128)S(1)}, f32[128,128]{1,0:T(8,128)S(1)}, u32[]{:S(2)}, u32[]{:S(2)}) %collective-permute-start.10) | collective-permute-done | bytes 65568 | tf_op jit(solution)/shard_map/ppermute | solution.py:318
  54.8 1.1 %shard_map.90 = (f32[16,16]{1,0:T(8,128)}, f32[128,128]{1,0:T(8,128)}, f32[128,128]{1,0:T(8,128)}, f32[128,128]{1,0:T(8,128)}) custom-call(f32[128,128]{1,0:T(8,128)S(1)} %add.15.mine, f32[128,128]{1,0:T(8,128)S(1)} %collective-permute-done.10.other), custom_call_target="tpu_custom_call" | custom-call | tf_op jit(solution)/shard_map/pallas_call | solution.py:386
  (17 shorter events, 0.3 us)
Async XLA Ops:
  0.6 8.5 %copy-start = (bf16[1,128,128,128]{3,2,1,0:T(8,128)(2,1)S(1)}, bf16[1,128,128,128]{3,2,1,0:T(8,128)(2,1)}, u32[]{:S(2)}) copy-start(bf16[1,128,128,128]{3,2,1,0:T(8,128)(2,1)} %param.5) | copy-start | bytes 12582916
  0.6 8.5 %copy-start.1 = (bf16[128,8]{0,1:T(8,128)(2,1)S(1)}, bf16[128,8]{0,1:T(8,128)(2,1)}, u32[]{:S(2)}) copy-start(bf16[128,8]{0,1:T(8,128)(2,1)} %param.7) | copy-start | bytes 6148
  3.4 14.1 %collective-permute-start.1 = (bf16[4,128,128]{2,1,0:T(8,128)(2,1)S(1)}, bf16[4,128,128]{2,1,0:T(8,128)(2,1)S(1)}, u32[]{:S(2)}, u32[]{:S(2)}) collective-permute-start(bf16[4,128,128]{2,1,0:T(8,128)(2,1)S(1)} %get-tuple-element.28), channel_id=1, source_target_pairs={{0,8},{1,9},{2,10},{3,11},{4,12},{5,13},{6,14},{7,15},{8,0},{9,1},... | collective-permute-start | bytes 393224 | tf_op jit(solution)/shard_map/ppermute | solution.py:318
  7.5 10.0 %collective-permute-start.2 = (bf16[4,128,128]{2,1,0:T(8,128)(2,1)S(1)}, bf16[4,128,128]{2,1,0:T(8,128)(2,1)S(1)}, u32[]{:S(2)}, u32[]{:S(2)}) collective-permute-start(bf16[4,128,128]{2,1,0:T(8,128)(2,1)S(1)} %get-tuple-element.29), channel_id=1, source_target_pairs={{0,12},{1,13},{2,14},{3,15},{4,8},{5,9},{6,10},{7,11},{8,4},{9,5},... | collective-permute-start | bytes 393224 | tf_op jit(solution)/shard_map/ppermute | solution.py:318
  8.9 9.1 %collective-permute-start = (bf16[4,128,128]{2,1,0:T(8,128)(2,1)S(1)}, bf16[4,128,128]{2,1,0:T(8,128)(2,1)S(1)}, u32[]{:S(2)}, u32[]{:S(2)}) collective-permute-start(bf16[4,128,128]{2,1,0:T(8,128)(2,1)S(1)} %get-tuple-element.27), channel_id=1, source_target_pairs={{0,4},{1,5},{2,6},{3,7},{4,0},{5,1},{6,2},{7,3},{8,12},{9,13},{10,... | collective-permute-start | bytes 393224 | tf_op jit(solution)/shard_map/ppermute | solution.py:318
  12.2 24.0 %all-to-all-start = ((bf16[16,192,128]{2,1,0:T(8,128)(2,1)}), bf16[16,192,128]{2,1,0:T(8,128)(2,1)S(1)}, u32[]{:S(2)}, u32[]{:S(2)}) async-start(bf16[16,192,128]{2,1,0:T(8,128)(2,1)} %shard_map.88), calls=%async_computation | async-start | bytes 1572864 | tf_op jit(solution)/shard_map/all_to_all | solution.py:363
  17.5 14.6 %copy-start.2 = (bf16[16,8]{0,1:T(8,128)(2,1)S(1)}, bf16[16,8]{0,1:T(8,128)(2,1)}, u32[]{:S(2)}) copy-start(bf16[16,8]{0,1:T(8,128)(2,1)} %param.6) | copy-start | bytes 772
  18.1 1.9 %collective-permute-start.3 = (bf16[4,128,128]{2,1,0:T(8,128)(2,1)S(1)}, bf16[4,128,128]{2,1,0:T(8,128)(2,1)S(1)}, u32[]{:S(2)}, u32[]{:S(2)}) collective-permute-start(bf16[4,128,128]{2,1,0:T(8,128)(2,1)S(1)} %get-tuple-element.35), channel_id=1, source_target_pairs={{0,1},{1,0},{2,3},{3,2},{4,5},{5,4},{6,7},{7,6},{8,9},{9,8},{10,11... | collective-permute-start | bytes 393224 | tf_op jit(solution)/shard_map/ppermute | solution.py:318
  18.2 11.9 %collective-permute-start.4 = (bf16[4,128,128]{2,1,0:T(8,128)(2,1)S(1)}, bf16[4,128,128]{2,1,0:T(8,128)(2,1)S(1)}, u32[]{:S(2)}, u32[]{:S(2)}) collective-permute-start(bf16[4,128,128]{2,1,0:T(8,128)(2,1)S(1)} %get-tuple-element.36), channel_id=1, source_target_pairs={{0,2},{1,3},{2,0},{3,1},{4,6},{5,7},{6,4},{7,5},{8,10},{9,11},{10,... | collective-permute-start | bytes 393224 | tf_op jit(solution)/shard_map/ppermute | solution.py:318
  19.8 12.3 %collective-permute-start.5 = (bf16[4,128,128]{2,1,0:T(8,128)(2,1)S(1)}, bf16[4,128,128]{2,1,0:T(8,128)(2,1)S(1)}, u32[]{:S(2)}, u32[]{:S(2)}) collective-permute-start(bf16[4,128,128]{2,1,0:T(8,128)(2,1)S(1)} %get-tuple-element.37), channel_id=1, source_target_pairs={{0,3},{1,2},{2,1},{3,0},{4,7},{5,6},{6,5},{7,4},{8,11},{9,10},{10,... | collective-permute-start | bytes 393224 | tf_op jit(solution)/shard_map/ppermute | solution.py:318
  37.3 1.3 %collective-permute-start.6 = (f32[128,128]{1,0:T(8,128)S(1)}, f32[128,128]{1,0:T(8,128)S(1)}, u32[]{:S(2)}, u32[]{:S(2)}) collective-permute-start(f32[128,128]{1,0:T(8,128)S(1)} %get-tuple-element.47), channel_id=1, source_target_pairs={{0,1},{1,0},{2,3},{3,2},{4,5},{5,4},{6,7},{7,6},{8,9},{9,8},{10,11... | collective-permute-start | bytes 196616 | tf_op jit(solution)/shard_map/ppermute | solution.py:318
  38.6 4.3 %collective-permute-start.7 = (f32[128,128]{1,0:T(8,128)S(1)}, f32[128,128]{1,0:T(8,128)S(1)}, u32[]{:S(2)}, u32[]{:S(2)}) collective-permute-start(f32[128,128]{1,0:T(8,128)S(1)} %add.12), channel_id=1, source_target_pairs={{0,2},{1,3},{2,0},{3,1},{4,6},{5,7},{6,4},{7,5},{8,10},{9,11},{10,... | collective-permute-start | bytes 196616 | tf_op jit(solution)/shard_map/ppermute | solution.py:318
  43.0 5.0 %collective-permute-start.8 = (f32[128,128]{1,0:T(8,128)S(1)}, f32[128,128]{1,0:T(8,128)S(1)}, u32[]{:S(2)}, u32[]{:S(2)}) collective-permute-start(f32[128,128]{1,0:T(8,128)S(1)} %add.13), channel_id=1, source_target_pairs={{0,4},{1,5},{2,6},{3,7},{4,0},{5,1},{6,2},{7,3},{8,12},{9,13},{10,... | collective-permute-start | bytes 196616 | tf_op jit(solution)/shard_map/ppermute | solution.py:318
  48.0 5.5 %collective-permute-start.9 = (f32[128,128]{1,0:T(8,128)S(1)}, f32[128,128]{1,0:T(8,128)S(1)}, u32[]{:S(2)}, u32[]{:S(2)}) collective-permute-start(f32[128,128]{1,0:T(8,128)S(1)} %add.14), channel_id=1, source_target_pairs={{0,8},{1,9},{2,10},{3,11},{4,12},{5,13},{6,14},{7,15},{8,0},{9,1},... | collective-permute-start | bytes 196616 | tf_op jit(solution)/shard_map/ppermute | solution.py:318
  53.5 1.3 %collective-permute-start.10 = (f32[128,128]{1,0:T(8,128)S(1)}, f32[128,128]{1,0:T(8,128)S(1)}, u32[]{:S(2)}, u32[]{:S(2)}) collective-permute-start(f32[128,128]{1,0:T(8,128)S(1)} %add.15.mine), channel_id=1, source_target_pairs={{0,1},{1,0},{2,3},{3,2},{4,5},{5,4},{6,7},{7,6},{8,9},{9,8},{10,11... | collective-permute-start | bytes 196616 | tf_op jit(solution)/shard_map/ppermute | solution.py:318

commit v9 on v7

--- a/solution.py
+++ b/solution.py
@@ -285,7 +285,7 @@
     cols, rows = col_out.shape[0], row_out.shape[0]
     half, part = cols // 2, cols // 4
     copies = []
-    for k, out in enumerate([col_out, right_out, left_out]):
+    for k, out in reversed(list(enumerate([col_out, right_out, left_out]))):
         top = total[k * half : k * half + part]
         next_top = total[k * half + part : (k + 1) * half]
         low = total[3 * half + k // 2 * part :][:part, k % 2 * half : (k % 2 + 1) * half]

time: 56.1 us -> 56.1 us (level)
  no operation moved by 1% of the time
where the time goes in v9:
time: 56.1 us; the launch traced here: 55.9 us
  waiting for transfers between devices  25.4 us (45%)
  starting transfers between devices  20.8 us (37%)
  Pallas kernels  8.94 us (16%)
  between operations  0.74 us (1%)
    ppermute x11, waiting for transfers between devices, swap(): return lax.ppermute(x, 'row', [(i, i ^ step) for i in range(n)])  22 us
    ppermute x11, starting transfers between devices, swap(): return lax.ppermute(x, 'row', [(i, i ^ step) for i in range(n)])  15.6 us
    all_to_all x1, starting transfers between devices, local(): lax.all_to_all(second, 'row', split_axis=0, concat_axis=0, tiled=True)  5.26 us
    all_to_all x1, waiting for transfers between devices, local(): lax.all_to_all(second, 'row', split_axis=0, concat_axis=0, tiled=True)  3.31 us
    pallas_call x1, Pallas kernels, projections(): pl.pallas_call(functools.partial(late_cubes, own), out_shape=jax.ShapeDty...  3.05 us
    pallas_call x1, Pallas kernels, projections(): pl.pallas_call(functools.partial(early_cubes, early, own), out_shape=[plt...  2.78 us
    pallas_call x4, Pallas kernels, call(): pl.pallas_call(kernel, out_shape=[jax.ShapeDtypeStruct(*out) for out in o...  1.98 us
  transfers between devices with their start and end apart: 12, of which 10 were waited for; matrix products, arithmetic and copies ran while one was open for 0% of the time, Pallas kernels for 7%

profile of v9, /device:TPU:0, one launch (start us, length us, event | category | flops | bytes accessed | tf_op | source)
XLA Modules:
  0.0 55.9 jit_solution(16834300226321223340)
XLA Ops:
  0.7 2.8 %shard_map.84 = (bf16[4,128,128]{2,1,0:T(8,128)(2,1)S(1)}, bf16[4,128,128]{2,1,0:T(8,128)(2,1)S(1)}, bf16[4,128,128]{2,1,0:T(8,128)(2,1)S(1)}, bf16[4,128,128]{2...) custom-call(bf16[128,128,128]{2,1,0:T(8,128)(2,1)} %bitcast.5, ...), custom_call_target="tpu_custom_call" | custom-call | tf_op jit(solution)/shard_map/pallas_call | solution.py:140
  3.4 4.1 %collective-permute-start.1 = (bf16[4,128,128]{2,1,0:T(8,128)(2,1)S(1)}, bf16[4,128,128]{2,1,0:T(8,128)(2,1)S(1)}, u32[]{:S(2)}, u32[]{:S(2)}) collective-permute-start(bf16[4,128,128]{2,1,0:T(8,128)(2,1)S(1)} %get-tuple-element.28), channel_id=1, source_target_pairs={{0,8},{1,9},{2,10},{3,11},{4,12},{5,13},{6,14},{7,15},{8,0},{9,1},... | collective-permute-start | bytes 393224 | tf_op jit(solution)/shard_map/ppermute | solution.py:318
  7.5 1.3 %collective-permute-start.2 = (bf16[4,128,128]{2,1,0:T(8,128)(2,1)S(1)}, bf16[4,128,128]{2,1,0:T(8,128)(2,1)S(1)}, u32[]{:S(2)}, u32[]{:S(2)}) collective-permute-start(bf16[4,128,128]{2,1,0:T(8,128)(2,1)S(1)} %get-tuple-element.29), channel_id=1, source_target_pairs={{0,12},{1,13},{2,14},{3,15},{4,8},{5,9},{6,10},{7,11},{8,4},{9,5},... | collective-permute-start | bytes 393224 | tf_op jit(solution)/shard_map/ppermute | solution.py:318
  8.9 0.2 collective-permute-start
  9.1 3.1 %shard_map.88 = bf16[16,192,128]{2,1,0:T(8,128)(2,1)} custom-call(bf16[128,128,128]{2,1,0:T(8,128)(2,1)S(1)} %bitcast.6, bf16[8,128]{1,0:T(8,128)(2,1)S(1)} %bitcast.7, bf16[128,256]{1,0:T(8,128)(2,1)S(1)} %get-tuple-element.42.dt2, bf16[128,256]{1,0:T(8,128)(2,1)S(1)} %get-tuple-element.43.vt2, bf16[256,128]{1,0:T(8,128)(2,1)S(1)} %get-tuple-element.44.dd, ...), custom_call_target="tpu_custom_call" | custom-call | tf_op jit(solution)/shard_map/pallas_call | solution.py:160
  12.2 5.3 %all-to-all-start = ((bf16[16,192,128]{2,1,0:T(8,128)(2,1)}), bf16[16,192,128]{2,1,0:T(8,128)(2,1)S(1)}, u32[]{:S(2)}, u32[]{:S(2)}) async-start(bf16[16,192,128]{2,1,0:T(8,128)(2,1)} %shard_map.88), calls=%async_computation | async-start | bytes 1572864 | tf_op jit(solution)/shard_map/all_to_all | solution.py:363
  17.6 0.5 collective-permute-done.refs_1_
  18.2 1.6 %collective-permute-start.4 = (bf16[4,128,128]{2,1,0:T(8,128)(2,1)S(1)}, bf16[4,128,128]{2,1,0:T(8,128)(2,1)S(1)}, u32[]{:S(2)}, u32[]{:S(2)}) collective-permute-start(bf16[4,128,128]{2,1,0:T(8,128)(2,1)S(1)} %get-tuple-element.36), channel_id=1, source_target_pairs={{0,2},{1,3},{2,0},{3,1},{4,6},{5,7},{6,4},{7,5},{8,10},{9,11},{10,... | collective-permute-start | bytes 393224 | tf_op jit(solution)/shard_map/ppermute | solution.py:318
  19.8 0.2 collective-permute-start.5
  20.0 10.0 %collective-permute-done.4.refs_2_ = bf16[4,128,128]{2,1,0:T(8,128)(2,1)S(1)} collective-permute-done((bf16[4,128,128]{2,1,0:T(8,128)(2,1)S(1)}, bf16[4,128,128]{2,1,0:T(8,128)(2,1)S(1)}, u32[]{:S(2)}, u32[]{:S(2)}) %collective-permute-start.4) | collective-permute-done | bytes 131104 | tf_op jit(solution)/shard_map/ppermute | solution.py:318
  30.0 2.0 %collective-permute-done.5.refs_3_ = bf16[4,128,128]{2,1,0:T(8,128)(2,1)S(1)} collective-permute-done((bf16[4,128,128]{2,1,0:T(8,128)(2,1)S(1)}, bf16[4,128,128]{2,1,0:T(8,128)(2,1)S(1)}, u32[]{:S(2)}, u32[]{:S(2)}) %collective-permute-start.5) | collective-permute-done | bytes 131104 | tf_op jit(solution)/shard_map/ppermute | solution.py:318
  32.0 0.8 %shard_map.87 = (bf16[128,256]{1,0:T(8,128)(2,1)S(1)}, bf16[8,64,256]{2,1,0:T(8,128)(2,1)S(1)}, f32[2,128,128]{2,1,0:T(8,128)S(1)}, f32[64,64]{1,0:T(8,128)S(1)}) custom-call(bf16[8,16]{1,0:T(8,128)(2,1)S(1)} %bitcast.10, bf16[8,128]{1,0:T(8,128)(2,1)S(1)} %bitcast.8, bf16[4,128,128]{2,1,0:T(8,128)(2,1)S(1)} %get-tuple-element.34.refs_0_, ...), custom_call_target="tpu_custom_call" | custom-call | flops 100000000 | bytes 1048576 | tf_op jit(solution)/shard_map/pallas_call | solution.py:308
  32.9 3.3 %all-to-all-done.second = bf16[16,192,128]{2,1,0:T(8,128)(2,1)S(1)} async-done(((bf16[16,192,128]{2,1,0:T(8,128)(2,1)}), bf16[16,192,128]{2,1,0:T(8,128)(2,1)S(1)}, u32[]{:S(2)}, u32[]{:S(2)}) %all-to-all-start) | async-done | bytes 786464 | tf_op jit(solution)/shard_map/all_to_all | solution.py:363
  36.2 1.1 %shard_map.89 = (f32[128,128]{1,0:T(8,128)S(1)}, f32[128,128]{1,0:T(8,128)S(1)}) custom-call(bf16[8,128]{1,0:T(8,128)(2,1)S(1)} %bitcast.9, bf16[128,256]{1,0:T(8,128)(2,1)S(1)} %get-tuple-element.38.plain, bf16[8,64,256]{2,1,0:T(8,128)(2,1)S(1)} %get-tuple-element.39.early_unfold, f32[2,128,128]{2,1,0:T(8,128)S(1)} %get-tuple-element.40.rowpart, ...), custom_call_target="tpu_custom_call" | custom-call | flops 100000000 | bytes 1048576 | tf_op jit(solution)/shard_map/pallas_call | solution.py:308
  37.3 0.3 collective-permute-start.6
  37.6 1.0 %collective-permute-done.6 = f32[128,128]{1,0:T(8,128)S(1)} collective-permute-done((f32[128,128]{1,0:T(8,128)S(1)}, f32[128,128]{1,0:T(8,128)S(1)}, u32[]{:S(2)}, u32[]{:S(2)}) %collective-permute-start.6) | collective-permute-done | bytes 65568 | tf_op jit(solution)/shard_map/ppermute | solution.py:318
  38.6 1.6 %collective-permute-start.7 = (f32[128,128]{1,0:T(8,128)S(1)}, f32[128,128]{1,0:T(8,128)S(1)}, u32[]{:S(2)}, u32[]{:S(2)}) collective-permute-start(f32[128,128]{1,0:T(8,128)S(1)} %add.12), channel_id=1, source_target_pairs={{0,2},{1,3},{2,0},{3,1},{4,6},{5,7},{6,4},{7,5},{8,10},{9,11},{10,... | collective-permute-start | bytes 196616 | tf_op jit(solution)/shard_map/ppermute | solution.py:318
  40.2 2.7 %collective-permute-done.7 = f32[128,128]{1,0:T(8,128)S(1)} collective-permute-done((f32[128,128]{1,0:T(8,128)S(1)}, f32[128,128]{1,0:T(8,128)S(1)}, u32[]{:S(2)}, u32[]{:S(2)}) %collective-permute-start.7) | collective-permute-done | bytes 65568 | tf_op jit(solution)/shard_map/ppermute | solution.py:318
  43.0 2.7 %collective-permute-start.8 = (f32[128,128]{1,0:T(8,128)S(1)}, f32[128,128]{1,0:T(8,128)S(1)}, u32[]{:S(2)}, u32[]{:S(2)}) collective-permute-start(f32[128,128]{1,0:T(8,128)S(1)} %add.13), channel_id=1, source_target_pairs={{0,4},{1,5},{2,6},{3,7},{4,0},{5,1},{6,2},{7,3},{8,12},{9,13},{10,... | collective-permute-start | bytes 196616 | tf_op jit(solution)/shard_map/ppermute | solution.py:318
  45.7 2.2 %collective-permute-done.8 = f32[128,128]{1,0:T(8,128)S(1)} collective-permute-done((f32[128,128]{1,0:T(8,128)S(1)}, f32[128,128]{1,0:T(8,128)S(1)}, u32[]{:S(2)}, u32[]{:S(2)}) %collective-permute-start.8) | collective-permute-done | bytes 65568 | tf_op jit(solution)/shard_map/ppermute | solution.py:318
  48.0 3.3 %collective-permute-start.9 = (f32[128,128]{1,0:T(8,128)S(1)}, f32[128,128]{1,0:T(8,128)S(1)}, u32[]{:S(2)}, u32[]{:S(2)}) collective-permute-start(f32[128,128]{1,0:T(8,128)S(1)} %add.14), channel_id=1, source_target_pairs={{0,8},{1,9},{2,10},{3,11},{4,12},{5,13},{6,14},{7,15},{8,0},{9,1},... | collective-permute-start | bytes 196616 | tf_op jit(solution)/shard_map/ppermute | solution.py:318
  51.2 2.2 %collective-permute-done.9 = f32[128,128]{1,0:T(8,128)S(1)} collective-permute-done((f32[128,128]{1,0:T(8,128)S(1)}, f32[128,128]{1,0:T(8,128)S(1)}, u32[]{:S(2)}, u32[]{:S(2)}) %collective-permute-start.9) | collective-permute-done | bytes 65568 | tf_op jit(solution)/shard_map/ppermute | solution.py:318
  53.6 1.2 %collective-permute-done.10.other = f32[128,128]{1,0:T(8,128)S(1)} collective-permute-done((f32[128,128]{1,0:T(8,128)S(1)}, f32[128,128]{1,0:T(8,128)S(1)}, u32[]{:S(2)}, u32[]{:S(2)}) %collective-permute-start.10) | collective-permute-done | bytes 65568 | tf_op jit(solution)/shard_map/ppermute | solution.py:318
  54.8 1.1 %shard_map.90 = (f32[16,16]{1,0:T(8,128)}, f32[128,128]{1,0:T(8,128)}, f32[128,128]{1,0:T(8,128)}, f32[128,128]{1,0:T(8,128)}) custom-call(f32[128,128]{1,0:T(8,128)S(1)} %add.15.mine, f32[128,128]{1,0:T(8,128)S(1)} %collective-permute-done.10.other), custom_call_target="tpu_custom_call" | custom-call | tf_op jit(solution)/shard_map/pallas_call | solution.py:386
  (17 shorter events, 0.3 us)
Async XLA Ops:
  0.6 8.5 %copy-start = (bf16[1,128,128,128]{3,2,1,0:T(8,128)(2,1)S(1)}, bf16[1,128,128,128]{3,2,1,0:T(8,128)(2,1)}, u32[]{:S(2)}) copy-start(bf16[1,128,128,128]{3,2,1,0:T(8,128)(2,1)} %param.5) | copy-start | bytes 12582916
  0.6 8.5 %copy-start.1 = (bf16[128,8]{0,1:T(8,128)(2,1)S(1)}, bf16[128,8]{0,1:T(8,128)(2,1)}, u32[]{:S(2)}) copy-start(bf16[128,8]{0,1:T(8,128)(2,1)} %param.7) | copy-start | bytes 6148
  3.4 14.1 %collective-permute-start.1 = (bf16[4,128,128]{2,1,0:T(8,128)(2,1)S(1)}, bf16[4,128,128]{2,1,0:T(8,128)(2,1)S(1)}, u32[]{:S(2)}, u32[]{:S(2)}) collective-permute-start(bf16[4,128,128]{2,1,0:T(8,128)(2,1)S(1)} %get-tuple-element.28), channel_id=1, source_target_pairs={{0,8},{1,9},{2,10},{3,11},{4,12},{5,13},{6,14},{7,15},{8,0},{9,1},... | collective-permute-start | bytes 393224 | tf_op jit(solution)/shard_map/ppermute | solution.py:318
  7.5 10.0 %collective-permute-start.2 = (bf16[4,128,128]{2,1,0:T(8,128)(2,1)S(1)}, bf16[4,128,128]{2,1,0:T(8,128)(2,1)S(1)}, u32[]{:S(2)}, u32[]{:S(2)}) collective-permute-start(bf16[4,128,128]{2,1,0:T(8,128)(2,1)S(1)} %get-tuple-element.29), channel_id=1, source_target_pairs={{0,12},{1,13},{2,14},{3,15},{4,8},{5,9},{6,10},{7,11},{8,4},{9,5},... | collective-permute-start | bytes 393224 | tf_op jit(solution)/shard_map/ppermute | solution.py:318
  8.9 9.1 %collective-permute-start = (bf16[4,128,128]{2,1,0:T(8,128)(2,1)S(1)}, bf16[4,128,128]{2,1,0:T(8,128)(2,1)S(1)}, u32[]{:S(2)}, u32[]{:S(2)}) collective-permute-start(bf16[4,128,128]{2,1,0:T(8,128)(2,1)S(1)} %get-tuple-element.27), channel_id=1, source_target_pairs={{0,4},{1,5},{2,6},{3,7},{4,0},{5,1},{6,2},{7,3},{8,12},{9,13},{10,... | collective-permute-start | bytes 393224 | tf_op jit(solution)/shard_map/ppermute | solution.py:318
  12.2 24.0 %all-to-all-start = ((bf16[16,192,128]{2,1,0:T(8,128)(2,1)}), bf16[16,192,128]{2,1,0:T(8,128)(2,1)S(1)}, u32[]{:S(2)}, u32[]{:S(2)}) async-start(bf16[16,192,128]{2,1,0:T(8,128)(2,1)} %shard_map.88), calls=%async_computation | async-start | bytes 1572864 | tf_op jit(solution)/shard_map/all_to_all | solution.py:363
  17.5 14.6 %copy-start.2 = (bf16[16,8]{0,1:T(8,128)(2,1)S(1)}, bf16[16,8]{0,1:T(8,128)(2,1)}, u32[]{:S(2)}) copy-start(bf16[16,8]{0,1:T(8,128)(2,1)} %param.6) | copy-start | bytes 772
  18.1 1.9 %collective-permute-start.3 = (bf16[4,128,128]{2,1,0:T(8,128)(2,1)S(1)}, bf16[4,128,128]{2,1,0:T(8,128)(2,1)S(1)}, u32[]{:S(2)}, u32[]{:S(2)}) collective-permute-start(bf16[4,128,128]{2,1,0:T(8,128)(2,1)S(1)} %get-tuple-element.35), channel_id=1, source_target_pairs={{0,1},{1,0},{2,3},{3,2},{4,5},{5,4},{6,7},{7,6},{8,9},{9,8},{10,11... | collective-permute-start | bytes 393224 | tf_op jit(solution)/shard_map/ppermute | solution.py:318
  18.2 11.9 %collective-permute-start.4 = (bf16[4,128,128]{2,1,0:T(8,128)(2,1)S(1)}, bf16[4,128,128]{2,1,0:T(8,128)(2,1)S(1)}, u32[]{:S(2)}, u32[]{:S(2)}) collective-permute-start(bf16[4,128,128]{2,1,0:T(8,128)(2,1)S(1)} %get-tuple-element.36), channel_id=1, source_target_pairs={{0,2},{1,3},{2,0},{3,1},{4,6},{5,7},{6,4},{7,5},{8,10},{9,11},{10,... | collective-permute-start | bytes 393224 | tf_op jit(solution)/shard_map/ppermute | solution.py:318
  19.8 12.2 %collective-permute-start.5 = (bf16[4,128,128]{2,1,0:T(8,128)(2,1)S(1)}, bf16[4,128,128]{2,1,0:T(8,128)(2,1)S(1)}, u32[]{:S(2)}, u32[]{:S(2)}) collective-permute-start(bf16[4,128,128]{2,1,0:T(8,128)(2,1)S(1)} %get-tuple-element.37), channel_id=1, source_target_pairs={{0,3},{1,2},{2,1},{3,0},{4,7},{5,6},{6,5},{7,4},{8,11},{9,10},{10,... | collective-permute-start | bytes 393224 | tf_op jit(solution)/shard_map/ppermute | solution.py:318
  37.3 1.3 %collective-permute-start.6 = (f32[128,128]{1,0:T(8,128)S(1)}, f32[128,128]{1,0:T(8,128)S(1)}, u32[]{:S(2)}, u32[]{:S(2)}) collective-permute-start(f32[128,128]{1,0:T(8,128)S(1)} %get-tuple-element.47), channel_id=1, source_target_pairs={{0,1},{1,0},{2,3},{3,2},{4,5},{5,4},{6,7},{7,6},{8,9},{9,8},{10,11... | collective-permute-start | bytes 196616 | tf_op jit(solution)/shard_map/ppermute | solution.py:318
  38.6 4.3 %collective-permute-start.7 = (f32[128,128]{1,0:T(8,128)S(1)}, f32[128,128]{1,0:T(8,128)S(1)}, u32[]{:S(2)}, u32[]{:S(2)}) collective-permute-start(f32[128,128]{1,0:T(8,128)S(1)} %add.12), channel_id=1, source_target_pairs={{0,2},{1,3},{2,0},{3,1},{4,6},{5,7},{6,4},{7,5},{8,10},{9,11},{10,... | collective-permute-start | bytes 196616 | tf_op jit(solution)/shard_map/ppermute | solution.py:318
  43.0 5.0 %collective-permute-start.8 = (f32[128,128]{1,0:T(8,128)S(1)}, f32[128,128]{1,0:T(8,128)S(1)}, u32[]{:S(2)}, u32[]{:S(2)}) collective-permute-start(f32[128,128]{1,0:T(8,128)S(1)} %add.13), channel_id=1, source_target_pairs={{0,4},{1,5},{2,6},{3,7},{4,0},{5,1},{6,2},{7,3},{8,12},{9,13},{10,... | collective-permute-start | bytes 196616 | tf_op jit(solution)/shard_map/ppermute | solution.py:318
  48.0 5.5 %collective-permute-start.9 = (f32[128,128]{1,0:T(8,128)S(1)}, f32[128,128]{1,0:T(8,128)S(1)}, u32[]{:S(2)}, u32[]{:S(2)}) collective-permute-start(f32[128,128]{1,0:T(8,128)S(1)} %add.14), channel_id=1, source_target_pairs={{0,8},{1,9},{2,10},{3,11},{4,12},{5,13},{6,14},{7,15},{8,0},{9,1},... | collective-permute-start | bytes 196616 | tf_op jit(solution)/shard_map/ppermute | solution.py:318
  53.5 1.3 %collective-permute-start.10 = (f32[128,128]{1,0:T(8,128)S(1)}, f32[128,128]{1,0:T(8,128)S(1)}, u32[]{:S(2)}, u32[]{:S(2)}) collective-permute-start(f32[128,128]{1,0:T(8,128)S(1)} %add.15.mine), channel_id=1, source_target_pairs={{0,1},{1,0},{2,3},{3,2},{4,5},{5,4},{6,7},{7,6},{8,9},{9,8},{10,11... | collective-permute-start | bytes 196616 | tf_op jit(solution)/shard_map/ppermute | solution.py:318
